TPU v7x, 512 devices: a whole 4x8x8 slice. The times are simulated.
512 devices in a mesh: ep: 64 (over y, z_hi, x), tp: 8 (over z_lo, core).
Axes of the slice: x: 4, y: 8, z: 8 (z_hi: 2, z_lo: 4; z = z_hi * 4 + z_lo), core: 2. Of those that a mesh axis runs over, the one named last changes fastest.
Arguments:
- tokens: bfloat16 [65536, 1024], P(('ep', 'tp')), may hold values from -6 to 6
- gates: float32 [65536, 8], P(('ep', 'tp')), may hold values from 0.1 to 0.5
- routes: int32 [65536, 8], P(('ep', 'tp')), may hold values from 0 to 63, all different within a row; in each aligned block of 128 rows (0 to 127, 128 to 255, ...) at most 16 rows name the same one
- cotangent: bfloat16 [65536, 1024], P(('ep', 'tp')), may hold values from -6 to 6
- old_home: int32 [64], replicated, may hold values from 0 to 63, each once
- swap_flags: int32 [32], replicated, may hold values 0 or 1
- weights: bfloat16 [64, 3, 384, 1024], P('ep', None, 'tp'), may hold values from -0.3125 to 0.3125
- first_moment: float32 [64, 3, 384, 1024], P('ep', None, 'tp'), may hold values from -18 to 18
- second_moment: float32 [64, 3, 384, 1024], P('ep', None, 'tp'), may hold values from 1 to 1000
Outputs:
- layer_output_rows: bfloat16 [65536, 1024], P(('ep', 'tp'))
- token_gradient_rows: bfloat16 [65536, 1024], P(('ep', 'tp'))
- new_weights: bfloat16 [64, 3, 384, 1024], P('ep', None, 'tp')
- new_first: float32 [64, 3, 384, 1024], P('ep', None, 'tp')
- new_second: float32 [64, 3, 384, 1024], P('ep', None, 'tp')
Inputs may be any that keep to these rules, and one draw needn't show every extreme that they name: `routes`: in the 128 rows of one device every expert is named exactly 16 times; each row names 8 different experts. `old_home`: each expert appears once.
All inputs are finite; a program needn't handle non-finite values.
Results may differ from a plain program's by a relative error of at most 0.025.
Values may be sent and summed in bfloat16 or wider, within the bound.
No kernel may reach another device: no remote copies, remote signals or barrier semaphores. Data moves between devices by JAX's collectives and lax.ppermute only.
A program may use at most 64 MiB of HBM per device.

v0:
```python
import jax
import jax.numpy as jnp
from jax import lax
from jax.sharding import PartitionSpec as P

BETA_ONE = 0.9
BETA_TWO = 0.95
LEARN_RATE = 0.001
EPSILON = 1e-08
STEP_COUNT = 20.0


def partner(array, axis, apart):
    return lax.ppermute(array, axis, [(i, i ^ 1 << apart) for i in range(lax.axis_size(axis))])


def trade_weights(weights, is_swapped, top_bit):
    other = partner(weights, "ep", top_bit)
    return jnp.where(is_swapped, other, weights)


def trade_moments(first_moment, second_moment, is_swapped, top_bit):
    other_first, other_second = (
        partner(first_moment.astype(jnp.bfloat16), "ep", top_bit).astype(first_moment.dtype),
        partner(second_moment.astype(jnp.bfloat16), "ep", top_bit).astype(second_moment.dtype),
    )
    return (
        jnp.where(is_swapped, other_first, first_moment),
        jnp.where(is_swapped, other_second, second_moment),
    )


def expert_forward(x_rows, gathered):
    hidden_width = gathered.shape[1]
    model_width = gathered.shape[2]
    inner = gathered[:2].reshape(2 * hidden_width, model_width)
    projected = jnp.einsum("rd,gd->rg", x_rows, inner, preferred_element_type=jnp.float32)
    gate_pre = projected[:, :hidden_width]
    up_pre = projected[:, hidden_width:]
    sigmoid_gate = jax.nn.sigmoid(gate_pre)
    hidden = (gate_pre * sigmoid_gate * up_pre).astype(jnp.bfloat16)
    expert_out = jnp.dot(hidden, gathered[2], preferred_element_type=jnp.float32).astype(
        jnp.bfloat16
    )
    return (hidden, gate_pre, up_pre, sigmoid_gate, expert_out)


def expert_backward(upstream_rows, gathered, gate_pre, up_pre, sigmoid_gate):
    hidden_width = gathered.shape[1]
    model_width = gathered.shape[2]
    inner = gathered[:2].reshape(2 * hidden_width, model_width)
    hidden_grad = jnp.einsum(
        "rd,fd->rf", upstream_rows, gathered[2], preferred_element_type=jnp.float32
    )
    gate_grad = hidden_grad * up_pre * sigmoid_gate * (1.0 + gate_pre * (1.0 - sigmoid_gate))
    up_grad = hidden_grad * gate_pre * sigmoid_gate
    projected_grad = jnp.concatenate([gate_grad, up_grad], axis=1).astype(jnp.bfloat16)
    row_grad = jnp.dot(projected_grad, inner, preferred_element_type=jnp.float32).astype(
        jnp.bfloat16
    )
    return (projected_grad, row_grad)


def adam_update(weights, first_moment, second_moment, gradient):
    first_new = BETA_ONE * first_moment + (1.0 - BETA_ONE) * gradient
    second_new = BETA_TWO * second_moment + (1.0 - BETA_TWO) * gradient * gradient
    adam_step = (
        LEARN_RATE
        * (first_new / (1.0 - BETA_ONE**STEP_COUNT))
        / (jnp.sqrt(second_new / (1.0 - BETA_TWO**STEP_COUNT)) + EPSILON)
    )
    weight_new = (weights.astype(jnp.float32) - adam_step).astype(jnp.bfloat16)
    return (weight_new, first_new, second_new)


def shards(
    tokens, gates, routes, cotangent, old_home, swap_flags, weights, first_moment, second_moment
):
    slot_count = lax.axis_size("ep")
    half_axis = slot_count // 2
    top_bit = slot_count.bit_length() - 2
    device_own_index = lax.axis_index("ep")
    tok_rows = tokens.shape[0]
    model_width = tokens.shape[1]
    top_count = routes.shape[1]
    capacity = tok_rows * top_count // slot_count
    slot_numbers = jnp.arange(slot_count, dtype=jnp.int32)
    flag_rows = jnp.concatenate([swap_flags, swap_flags])
    is_swapped = jnp.sum(jnp.where(slot_numbers == device_own_index, flag_rows, 0)) == 1
    moved_home = jnp.roll(old_home, -half_axis)
    current_home = jnp.where(flag_rows == 1, moved_home, old_home)
    weights = trade_weights(weights, is_swapped, top_bit)
    first_moment, second_moment = trade_moments(first_moment, second_moment, is_swapped, top_bit)
    expert_slot = jnp.sum(
        jnp.where(current_home[None, :] == slot_numbers[:, None], slot_numbers[None, :], 0), axis=1
    )
    target = jnp.sum(
        jnp.where(routes[:, :, None] == slot_numbers[None, None, :], expert_slot[None, None, :], 0),
        axis=2,
    )
    flat = routes.reshape(-1)
    indicator_matrix = (flat[:, None] == slot_numbers[None, :]).astype(jnp.int32)
    before = jnp.cumsum(indicator_matrix, axis=0) - indicator_matrix
    route_rank = jnp.sum(before * indicator_matrix, axis=1).reshape(tok_rows, top_count)
    route_place = target * capacity + route_rank
    buffer_size = slot_count * capacity
    place_flat = route_place.reshape(-1)
    token_ids = jnp.broadcast_to(
        jnp.arange(tok_rows, dtype=jnp.int32)[:, None], (tok_rows, top_count)
    ).reshape(-1)
    slot_token = jnp.zeros((buffer_size,), jnp.int32).at[place_flat].set(token_ids)
    slot_gate = jnp.zeros((buffer_size,), jnp.float32).at[place_flat].set(gates.reshape(-1))
    slot_live = jnp.zeros((buffer_size,), jnp.float32).at[place_flat].set(1.0)
    send_rows = jnp.where(slot_live[:, None] > 0, tokens[slot_token], jnp.zeros((), jnp.bfloat16))
    send_rows = send_rows.reshape(slot_count, capacity, model_width)
    send_grads = (slot_gate[:, None] * cotangent[slot_token].astype(jnp.float32)).astype(
        jnp.bfloat16
    )
    send_grads = send_grads.reshape(slot_count, capacity, model_width)
    gathered = lax.all_gather(weights[0], "tp", axis=1, tiled=True)
    arrived = lax.all_to_all(send_rows, "ep", split_axis=0, concat_axis=0, tiled=True)
    x_rows = arrived.reshape(-1, model_width)
    hidden, gate_pre, up_pre, sigmoid_gate, expert_out = expert_forward(x_rows, gathered)
    back_out = lax.all_to_all(
        expert_out.reshape(slot_count, capacity, model_width),
        "ep",
        split_axis=0,
        concat_axis=0,
        tiled=True,
    )
    arrived_grads = lax.all_to_all(send_grads, "ep", split_axis=0, concat_axis=0, tiled=True)
    upstream_rows = arrived_grads.reshape(-1, model_width)
    projected_grad, row_grad = expert_backward(
        upstream_rows, gathered, gate_pre, up_pre, sigmoid_gate
    )
    back_grad = lax.all_to_all(
        row_grad.reshape(slot_count, capacity, model_width),
        "ep",
        split_axis=0,
        concat_axis=0,
        tiled=True,
    )
    picked_out = back_out.reshape(-1, model_width)[route_place]
    layer_output_rows = jnp.sum(gates[:, :, None] * picked_out.astype(jnp.float32), axis=1).astype(
        jnp.bfloat16
    )
    picked_grad = back_grad.reshape(-1, model_width)[route_place]
    token_gradient_rows = jnp.sum(picked_grad.astype(jnp.float32), axis=1).astype(jnp.bfloat16)
    hidden_width = hidden.shape[1]
    inner_terms = jnp.einsum(
        "rg,rd->gd", projected_grad, x_rows, preferred_element_type=jnp.float32
    )
    inner_terms = inner_terms.reshape(2, hidden_width, model_width)
    down_terms = jnp.einsum("rf,rd->fd", hidden, upstream_rows, preferred_element_type=jnp.float32)[
        None
    ]
    inner_sum, down_sum = (
        lax.psum_scatter(
            inner_terms.astype(jnp.bfloat16), "tp", scatter_dimension=1, tiled=True
        ).astype(jnp.float32),
        lax.psum_scatter(
            down_terms.astype(jnp.bfloat16), "tp", scatter_dimension=1, tiled=True
        ).astype(jnp.float32),
    )
    gradient = jnp.concatenate([inner_sum, down_sum], axis=0)[None]
    new_weights, new_first, new_second = adam_update(weights, first_moment, second_moment, gradient)
    return (layer_output_rows, token_gradient_rows, new_weights, new_first, new_second)


def solution(mesh):
    in_specs = (
        P(("ep", "tp"), None),
        P(("ep", "tp"), None),
        P(("ep", "tp"), None),
        P(("ep", "tp"), None),
        P(),
        P(),
        P("ep", None, "tp", None),
        P("ep", None, "tp", None),
        P("ep", None, "tp", None),
    )
    out_specs = (
        P(("ep", "tp"), None),
        P(("ep", "tp"), None),
        P("ep", None, "tp", None),
        P("ep", None, "tp", None),
        P("ep", None, "tp", None),
    )
    return jax.shard_map(shards, mesh=mesh, in_specs=in_specs, out_specs=out_specs, check_vma=False)
```

profile of v0, /device:TPU:40, one launch (start us, length us, event | category | flops | bytes accessed | tf_op | source)
XLA Modules:
  0.0 418.2 jit_solution(3394245605315286445)
XLA Ops:
  7.2 0.8 copy.25
  8.0 0.1 eq.78
  8.1 0.1 eq.74
  8.3 18.0 %reduce-window.6 = s32[64,8,128]{2,1,0:T(8,128)S(1)} reduce-window(s32[64,8,128]{2,1,0:T(8,128)S(1)} %fusion.9, s32[]{:T(128)} %constant.19.clone.1), window={size=1x1x128 pad=0_0x0_0x127_0}, to_apply=%region_2.3 | reduce-window | flops 8323072 | bytes 524292 | tf_op jit(solution)/shard_map/reduce-window
  26.3 0.1 slice.46
  26.4 0.1 copy.27
  26.6 0.1 copy.28
  26.7 0.1 broadcast_add_fusion
  26.8 0.1 fusion.20
  26.9 0.7 fusion.17
  27.6 0.1 select_reduce_fusion.1
  27.7 0.1 select_reduce_fusion
  27.8 0.1 copy.24
  28.0 0.1 mul.133
  28.1 0.1 reshape.288
  28.2 0.1 fusion.8
  28.2 4.3 %scatter_custom_fusion.1 = s32[1024]{0:T(1024)S(1)} fusion(s32[1024]{0:T(1024)S(1)} %bitcast.80, s32[1024]{0:T(1024)S(1)} %reshape.288, s32[]{:T(128)} %constant.19.clone.1), kind=kCustom, calls=%fused_computation.50 | custom fusion | bytes 4100 | tf_op jit(solution)/shard_map/scatter | solution.py:111
  32.6 4.3 %scatter_custom_fusion = f32[1024]{0:T(1024)S(1)} fusion(s32[1024]{0:T(1024)S(1)} %bitcast.81, f32[1024]{0:T(1024)S(1)} %broadcast.123, f32[]{:T(128)} %constant.17.clone.1), kind=kCustom, calls=%fused_computation.56 | custom fusion | bytes 4100 | tf_op jit(solution)/shard_map/scatter | solution.py:113
  36.9 0.1 broadcast_in_dim.77
  37.0 4.1 gather_fusion
  41.1 1.6 broadcast_select_fusion
  42.7 19.0 %all-to-all-start = ((bf16[64,16,1024]{2,1,0:T(8,128)(2,1)}), bf16[64,16,1024]{2,1,0:T(8,128)(2,1)}, u32[]{:S(2)}, u32[]{:S(2)}) async-start(bf16[64,16,1024]{2,1,0:T(8,128)(2,1)} %broadcast_select_fusion), calls=%async_computation | async-start | bytes 4194304 | tf_op jit(solution)/shard_map/all_to_all | solution.py:121
  61.7 0.0 all-gather.3.cloned.1.call-start
  61.8 3.2 collective-permute-start
  65.6 54.7 %collective-permute-done = bf16[1,3,48,1024]{3,2,1,0:T(8,128)(2,1)S(1)} collective-permute-done((bf16[1,3,48,1024]{3,2,1,0:T(8,128)(2,1)S(1)}, bf16[1,3,48,1024]{3,2,1,0:T(8,128)(2,1)S(1)}, u32[]{:S(2)}, u32[]{:S(2)}) %collective-permute-start) | collective-permute-done | bytes 294944 | tf_op jit(solution)/shard_map/ppermute | solution.py:14
  120.4 0.7 broadcast_select_fusion.1
  121.2 4.1 gather_fusion.2
  125.2 0.1 copy.23
  125.3 0.1 reshape.296
  125.4 4.3 %scatter_custom_fusion.2 = f32[1024]{0:T(1024)S(1)} fusion(s32[1024]{0:T(1024)S(1)} %bitcast.82, f32[1024]{0:T(1024)S(1)} %reshape.296, f32[]{:T(128)} %constant.17.clone.1), kind=kCustom, calls=%fused_computation.53 | custom fusion | bytes 4100 | tf_op jit(solution)/shard_map/scatter | solution.py:112
  129.8 0.1 mul.139
  129.8 1.8 fusion
  131.6 15.3 %all-to-all-start.2 = ((bf16[64,16,1024]{2,1,0:T(8,128)(2,1)}), bf16[64,16,1024]{2,1,0:T(8,128)(2,1)S(1)}, u32[]{:S(2)}, u32[]{:S(2)}) async-start(bf16[64,16,1024]{2,1,0:T(8,128)(2,1)} %fusion), calls=%async_computation.2 | async-start | bytes 4194304 | tf_op jit(solution)/shard_map/all_to_all | solution.py:131
  147.0 62.4 %all-gather.3.cloned.1.call-done = bf16[1,3,384,1024]{3,2,1,0:T(8,128)(2,1)} async-done(((bf16[1,3,48,1024]{3,2,1,0:T(8,128)(2,1)}), bf16[1,3,384,1024]{3,2,1,0:T(8,128)(2,1)}) %all-gather.3.cloned.1.call-update) | async-done | bytes 2359312 | tf_op jit(solution)/shard_map/all_gather | solution.py:120
  209.4 1.5 slice.48
  210.9 1.2 copy-done.5
  212.1 5.1 %fusion.21 = f32[1024,768]{0,1:T(8,128)} fusion(bf16[1024,1024]{1,0:T(8,128)(2,1)} %bitcast.5, bf16[768,1024]{1,0:T(8,128)(2,1)S(1)} %bitcast.73), kind=kOutput, calls=%fused_computation.63 | convolution fusion | flops 1610612736 | bytes 6815744 | tf_op jit(solution)/shard_map/rd,gd->rg/dot_general | solution.py:37
  217.2 5.3 %multiply_convert_fusion.1 = (bf16[1024,384]{0,1:T(8,128)(2,1)S(1)}, bf16[1024,384]{0,1:T(8,128)(2,1)S(1)}, bf16[1024,384]{0,1:T(8,128)(2,1)}) fusion(f32[1024,768]{0,1:T(8,128)} %fusion.21, bf16[1024,1024]{1,0:T(8,128)(2,1)S(1)} %bitcast.69, bf16[1,3,384,1024]{3,2,1,0:T(8,128)(2,1)} %all-gather.3.cloned.1.call-done), kind=kOutput, calls=%fused_computation.18 | convolution fusion | flops 811597824 | bytes 8388608 | tf_op jit(solution)/shard_map/rd,fd->rf/dot_general | solution.py:52
  222.5 3.2 convolution_convert_fusion.1
  225.8 14.0 %all-to-all-start.3 = ((bf16[64,16,1024]{2,1,0:T(8,128)(2,1)}), bf16[64,16,1024]{2,1,0:T(8,128)(2,1)S(1)}, u32[]{:S(2)}, u32[]{:S(2)}) async-start(bf16[64,16,1024]{2,1,0:T(8,128)(2,1)} %bitcast.71), calls=%async_computation.3 | async-start | bytes 4194304 | tf_op jit(solution)/shard_map/all_to_all | solution.py:136
  239.8 0.0 reduce-scatter.5.cloned.1.call-start
  239.9 3.7 fusion.2
  243.6 0.0 reduce-scatter.5.cloned.1.call-update
  243.6 2.5 pad_maximum_fusion
  246.1 3.8 convolution_convert_fusion
  249.9 40.1 %all-to-all-done.3 = bf16[64,16,1024]{2,1,0:T(8,128)(2,1)S(1)} async-done(((bf16[64,16,1024]{2,1,0:T(8,128)(2,1)}), bf16[64,16,1024]{2,1,0:T(8,128)(2,1)S(1)}, u32[]{:S(2)}, u32[]{:S(2)}) %all-to-all-start.3) | async-done | bytes 2097184 | tf_op jit(solution)/shard_map/all_to_all | solution.py:136
  290.0 13.1 %all-to-all-start.1 = ((bf16[64,16,1024]{2,1,0:T(8,128)(2,1)}), bf16[64,16,1024]{2,1,0:T(8,128)(2,1)}, u32[]{:S(2)}, u32[]{:S(2)}) async-start(bf16[64,16,1024]{2,1,0:T(8,128)(2,1)} %bitcast.68), calls=%async_computation.1 | async-start | bytes 4194304 | tf_op jit(solution)/shard_map/all_to_all | solution.py:124
  303.2 0.0 reduce-scatter.3.cloned.1.call-start
  303.2 5.2 %convolution_convert_fusion.2 = bf16[2,384,1024]{2,1,0:T(8,128)(2,1)} fusion(bf16[2,384,1024]{2,1,0:T(8,128)(2,1)} %bitcast.72, bf16[1024,1024,1]{1,0,2:T(8,128)(2,1)} %bitcast.19), kind=kOutput, calls=%fused_computation.15 | convolution fusion | flops 1611399168 | bytes 5242880 | tf_op jit(solution)/shard_map/rg,rd->gd/dot_general | solution.py:150
  308.4 0.8 convert_element_type.76
  309.2 3.2 collective-permute-start.1
  312.4 1.8 convert_element_type.81
  314.2 6.7 %collective-permute-start.2 = (bf16[1,3,48,1024]{3,2,1,0:T(8,128)(2,1)}, bf16[1,3,48,1024]{3,2,1,0:T(8,128)(2,1)}, u32[]{:S(2)}, u32[]{:S(2)}) collective-permute-start(bf16[1,3,48,1024]{3,2,1,0:T(8,128)(2,1)} %convert_element_type.81), channel_id=1, source_target_pairs={{0,256},{8,264},{16,272},{24,280},{32,288},{40,296},{48,304},{56,3... | collective-permute-start | bytes 884744 | tf_op jit(solution)/shard_map/ppermute | solution.py:14
  320.9 0.1 reshape.238
  321.1 0.1 copy.30
  321.2 0.1 reshape.254
  321.3 44.9 %collective-permute-done.1 = bf16[1,3,48,1024]{3,2,1,0:T(8,128)(2,1)} collective-permute-done((bf16[1,3,48,1024]{3,2,1,0:T(8,128)(2,1)}, bf16[1,3,48,1024]{3,2,1,0:T(8,128)(2,1)}, u32[]{:S(2)}, u32[]{:S(2)}) %collective-permute-start.1) | collective-permute-done | bytes 294944 | tf_op jit(solution)/shard_map/ppermute | solution.py:14
  366.2 3.2 collective-permute-done.2
  369.4 21.5 %reduce-scatter.3.cloned.1.call-done = bf16[2,48,1024]{2,1,0:T(8,128)(2,1)} async-done(((bf16[2,384,1024]{2,1,0:T(8,128)(2,1)}), bf16[2,48,1024]{2,1,0:T(8,128)(2,1)}) %reduce-scatter.3.cloned.1.call-update) | async-done | bytes 196624 | tf_op jit(solution)/shard_map/reduce_scatter | solution.py:158
  390.9 2.8 subtract_convert_fusion
  393.7 5.4 %gather_fusion.3 = bf16[1024,1024]{1,0:T(8,128)(2,1)} fusion(bf16[1024,1024]{1,0:T(8,128)(2,1)S(1)} %bitcast.65, s32[1024]{0:T(1024)S(1)} %broadcast_clamp_fusion), kind=kCustom, calls=%fused_computation.3 | custom fusion | bytes 4198400 | tf_op jit(solution)/shard_map/gather | solution.py:147
  399.1 3.7 bitcast_reduce_fusion
  402.8 6.8 %gather_fusion.1 = bf16[1024,1024]{1,0:T(8,128)(2,1)S(1)} fusion(bf16[1024,1024]{1,0:T(8,128)(2,1)} %bitcast.9, s32[1024]{0:T(1024)S(1)} %broadcast_clamp_fusion), kind=kCustom, calls=%fused_computation.1 | custom fusion | bytes 4198400 | tf_op jit(solution)/shard_map/gather | solution.py:143
  409.7 2.0 fusion.1
  (45 shorter events, 0.3 us)
Async XLA Ops:
  7.2 29.8 %copy-start = (bf16[128,1024]{1,0:T(8,128)(2,1)S(1)}, bf16[128,1024]{1,0:T(8,128)(2,1)}, u32[]{:S(2)}) copy-start(bf16[128,1024]{1,0:T(8,128)(2,1)} %param.9) | copy-start | bytes 786436
  7.2 20.5 %copy-start.9 = (s32[128,8]{0,1:T(8,128)S(1)}, s32[128,8]{0,1:T(8,128)}, u32[]{:S(2)}) copy-start(s32[128,8]{0,1:T(8,128)} %param.11) | copy-start | bytes 12292
  7.2 19.6 %copy-start.10 = (s32[64]{0:T(128)S(1)}, s32[64]{0:T(128)}, u32[]{:S(2)}) copy-start(s32[64]{0:T(128)} %param.13) | copy-start | bytes 772
  7.2 19.7 %copy-start.12 = (s32[32]{0:T(128)S(1)}, s32[32]{0:T(128)}, u32[]{:S(2)}) copy-start(s32[32]{0:T(128)} %param.14) | copy-start | bytes 388
  42.7 19.1 %copy-start.8 = (bf16[1,3,48,1024]{3,2,1,0:T(8,128)(2,1)S(1)}, bf16[1,3,48,1024]{3,2,1,0:T(8,128)(2,1)}, u32[]{:S(2)}) copy-start(bf16[1,3,48,1024]{3,2,1,0:T(8,128)(2,1)} %param.15) | copy-start | bytes 884740
  42.7 78.5 %copy-start.1 = (bf16[128,1024]{1,0:T(8,128)(2,1)S(1)}, bf16[128,1024]{1,0:T(8,128)(2,1)}, u32[]{:S(2)}) copy-start(bf16[128,1024]{1,0:T(8,128)(2,1)} %param.12) | copy-start | bytes 786436
  42.7 89.0 %all-to-all-start = ((bf16[64,16,1024]{2,1,0:T(8,128)(2,1)}), bf16[64,16,1024]{2,1,0:T(8,128)(2,1)}, u32[]{:S(2)}, u32[]{:S(2)}) async-start(bf16[64,16,1024]{2,1,0:T(8,128)(2,1)} %broadcast_select_fusion), calls=%async_computation | async-start | bytes 4194304 | tf_op jit(solution)/shard_map/all_to_all | solution.py:121
  61.7 147.7 %all-gather.3.cloned.1.call-start = ((), (), s32[]{:S(2)}) async-start(), calls=%async_computation.8 | async-start | bytes 2654208 | tf_op jit(solution)/shard_map/all_gather | solution.py:120
  61.8 58.6 %collective-permute-start = (bf16[1,3,48,1024]{3,2,1,0:T(8,128)(2,1)S(1)}, bf16[1,3,48,1024]{3,2,1,0:T(8,128)(2,1)S(1)}, u32[]{:S(2)}, u32[]{:S(2)}) collective-permute-start(bf16[1,3,48,1024]{3,2,1,0:T(8,128)(2,1)S(1)} %copy-done.8), channel_id=1, source_target_pairs={{0,256},{8,264},{16,272},{24,280},{32,288},{40,296},{48,304},{56,3... | collective-permute-start | bytes 884744 | tf_op jit(solution)/shard_map/ppermute | solution.py:14
  121.1 4.1 copy-start.11
  131.6 85.6 %all-to-all-start.2 = ((bf16[64,16,1024]{2,1,0:T(8,128)(2,1)}), bf16[64,16,1024]{2,1,0:T(8,128)(2,1)S(1)}, u32[]{:S(2)}, u32[]{:S(2)}) async-start(bf16[64,16,1024]{2,1,0:T(8,128)(2,1)} %fusion), calls=%async_computation.2 | async-start | bytes 4194304 | tf_op jit(solution)/shard_map/all_to_all | solution.py:131
  210.9 1.3 copy-start.5
  217.2 5.3 %copy-start.4 = (bf16[64,16,1024]{2,1,0:T(8,128)(2,1)}, bf16[64,16,1024]{2,1,0:T(8,128)(2,1)S(1)}, u32[]{:S(2)}) copy-start(bf16[64,16,1024]{2,1,0:T(8,128)(2,1)S(1)} %all-to-all-done.2) | copy-start | bytes 6291460
  217.2 5.3 %copy-start.6 = (bf16[1,2,384,1024]{3,2,1,0:T(8,128)(2,1)S(1)}, bf16[1,2,384,1024]{3,2,1,0:T(8,128)(2,1)}, u32[]{:S(2)}) copy-start(bf16[1,2,384,1024]{3,2,1,0:T(8,128)(2,1)} %copy-done.5) | copy-start | bytes 4718596
  222.5 3.3 copy-start.7
  225.8 64.2 %all-to-all-start.3 = ((bf16[64,16,1024]{2,1,0:T(8,128)(2,1)}), bf16[64,16,1024]{2,1,0:T(8,128)(2,1)S(1)}, u32[]{:S(2)}, u32[]{:S(2)}) async-start(bf16[64,16,1024]{2,1,0:T(8,128)(2,1)} %bitcast.71), calls=%async_computation.3 | async-start | bytes 4194304 | tf_op jit(solution)/shard_map/all_to_all | solution.py:136
  239.8 129.6 %reduce-scatter.5.cloned.1.call-start = ((), (), s32[]{:S(2)}) async-start(), calls=%async_computation.7 | async-start | bytes 884736 | tf_op jit(solution)/shard_map/reduce_scatter | solution.py:161
  243.6 2.5 copy-start.13
  290.0 112.8 %all-to-all-start.1 = ((bf16[64,16,1024]{2,1,0:T(8,128)(2,1)}), bf16[64,16,1024]{2,1,0:T(8,128)(2,1)}, u32[]{:S(2)}, u32[]{:S(2)}) async-start(bf16[64,16,1024]{2,1,0:T(8,128)(2,1)} %bitcast.68), calls=%async_computation.1 | async-start | bytes 4194304 | tf_op jit(solution)/shard_map/all_to_all | solution.py:124
  303.2 87.7 %reduce-scatter.3.cloned.1.call-start = ((), (), s32[]{:S(2)}) async-start(), calls=%async_computation.6 | async-start | bytes 1769472 | tf_op jit(solution)/shard_map/reduce_scatter | solution.py:158
  303.2 5.2 %copy-start.3 = (f32[1,3,48,1024]{3,2,1,0:T(8,128)S(1)}, f32[1,3,48,1024]{3,2,1,0:T(8,128)}, u32[]{:S(2)}) copy-start(f32[1,3,48,1024]{3,2,1,0:T(8,128)} %param.16) | copy-start | bytes 1769476
  308.4 82.5 %copy-start.2 = (bf16[1,3,48,1024]{3,2,1,0:T(8,128)(2,1)S(1)}, bf16[1,3,48,1024]{3,2,1,0:T(8,128)(2,1)}, u32[]{:S(2)}) copy-start(bf16[1,3,48,1024]{3,2,1,0:T(8,128)(2,1)} %broadcast_select_fusion.1) | copy-start | bytes 884740
  309.2 57.1 %collective-permute-start.1 = (bf16[1,3,48,1024]{3,2,1,0:T(8,128)(2,1)}, bf16[1,3,48,1024]{3,2,1,0:T(8,128)(2,1)}, u32[]{:S(2)}, u32[]{:S(2)}) collective-permute-start(bf16[1,3,48,1024]{3,2,1,0:T(8,128)(2,1)} %convert_element_type.76), channel_id=1, source_target_pairs={{0,256},{8,264},{16,272},{24,280},{32,288},{40,296},{48,304},{56,3... | collective-permute-start | bytes 884744 | tf_op jit(solution)/shard_map/ppermute | solution.py:14
  314.2 55.2 %collective-permute-start.2 = (bf16[1,3,48,1024]{3,2,1,0:T(8,128)(2,1)}, bf16[1,3,48,1024]{3,2,1,0:T(8,128)(2,1)}, u32[]{:S(2)}, u32[]{:S(2)}) collective-permute-start(bf16[1,3,48,1024]{3,2,1,0:T(8,128)(2,1)} %convert_element_type.81), channel_id=1, source_target_pairs={{0,256},{8,264},{16,272},{24,280},{32,288},{40,296},{48,304},{56,3... | collective-permute-start | bytes 884744 | tf_op jit(solution)/shard_map/ppermute | solution.py:14
Sparse Core Ops, SparseCore 0:
  121.3 88.0 all-gather.2
  243.7 76.8 reduce-scatter.4
  323.7 67.1 reduce-scatter.2
where the time goes:
time: 419 us; the launch traced here: 418 us
  waiting for transfers between devices  227 us (54%)
  starting transfers between devices  74.8 us (18%)
  local copies, waits for them, and re-layouts  38.5 us (9%)
  other arithmetic  36.9 us (9%)
  matrix products  26.3 us (6%)
  between operations  14.8 us (4%)
    ppermute x3, waiting for transfers between devices, partner(): lax.ppermute(array, axis, [(i, i ^ 1 << apart) for i in range(lax.axis_si...  103 us
    all_gather x1, waiting for transfers between devices, shards(): gathered = lax.all_gather(weights[0], 'tp', axis=1, tiled=True)  62.4 us
    all_to_all x1, waiting for transfers between devices, shards(): lax.all_to_all(row_grad.reshape(slot_count, capacity, model_width), 'ep',...  40.1 us
    reduce_scatter x1, waiting for transfers between devices, shards(): lax.psum_scatter(inner_terms.astype(jnp.bfloat16), 'tp', scatter_dimensio...  21.5 us
    all_to_all x1, starting transfers between devices, shards(): lax.all_to_all(send_rows, 'ep', split_axis=0, concat_axis=0, tiled=True)  19 us
    another operation x3, other arithmetic  18.2 us
    all_to_all x1, starting transfers between devices, shards(): lax.all_to_all(send_grads, 'ep', split_axis=0, concat_axis=0, tiled=True)  15.3 us
    all_to_all x1, starting transfers between devices, shards(): lax.all_to_all(row_grad.reshape(slot_count, capacity, model_width), 'ep',...  14 us
  transfers between devices with their start and end apart: 10, of which 6 were waited for; matrix products, arithmetic and copies ran while one was open for 11% of the time, Pallas kernels for 0%

commit v1 on v0

v1 whole, which is shorter than its diff:
```python
import jax
import jax.numpy as jnp
from jax import lax
from jax.experimental import pallas as pl
from jax.experimental.pallas import tpu as pltpu
from jax.sharding import PartitionSpec as P

BETA_ONE = 0.9
BETA_TWO = 0.95
LEARN_RATE = 0.001
EPSILON = 1e-08
STEP_COUNT = 20.0

VMEM_LIMIT = 40 * 1024 * 1024


def partner(array, axis, apart):
    return lax.ppermute(array, axis, [(i, i ^ 1 << apart) for i in range(lax.axis_size(axis))])


def dot_first(a, b):
    return lax.dot_general(a, b, (((0,), (0,)), ((), ())), preferred_element_type=jnp.float32)


def dispatch_kernel(routes_ref, gates_ref, home_ref, tokens_ref, cotangent_ref,
                    send_x_ref, send_g_ref, place_ref, weigh_ref):
    tok_rows, top_count = routes_ref.shape
    slot_count = home_ref.shape[1]
    buffer_rows = send_x_ref.shape[0]
    capacity = buffer_rows // slot_count
    home = home_ref[...]
    named = jnp.zeros((tok_rows, slot_count), jnp.float32)
    gate = jnp.zeros((tok_rows, slot_count), jnp.float32)
    for k in range(top_count):
        hit = routes_ref[:, k : k + 1] == home
        named = named + jnp.where(hit, 1.0, 0.0)
        gate = gate + jnp.where(hit, gates_ref[:, k : k + 1], 0.0)
    row = lax.broadcasted_iota(jnp.int32, (tok_rows, tok_rows), 0)
    col = lax.broadcasted_iota(jnp.int32, (tok_rows, tok_rows), 1)
    earlier = jnp.where(col < row, 1.0, 0.0).astype(jnp.bfloat16)
    rank = jnp.dot(earlier, named.astype(jnp.bfloat16), preferred_element_type=jnp.float32)
    rank = jnp.where(named > 0, rank, -1.0)
    slot = lax.broadcasted_iota(jnp.int32, (slot_count, buffer_rows), 0)
    place = lax.broadcasted_iota(jnp.int32, (slot_count, buffer_rows), 1)
    spread = jnp.where(place // capacity == slot, 1.0, 0.0).astype(jnp.bfloat16)

    def widen(values):
        return jnp.dot(values.astype(jnp.bfloat16), spread, preferred_element_type=jnp.float32)

    gate_high = gate.astype(jnp.bfloat16).astype(jnp.float32)
    gate_low = gate - gate_high
    place = lax.broadcasted_iota(jnp.int32, (tok_rows, buffer_rows), 1)
    hit = widen(rank) == (place % capacity).astype(jnp.float32)
    one = jnp.where(hit, 1.0, 0.0).astype(jnp.bfloat16)
    high = jnp.where(hit, widen(gate_high), 0.0).astype(jnp.bfloat16)
    low = jnp.where(hit, widen(gate_low), 0.0).astype(jnp.bfloat16)
    place_ref[...] = one
    weigh_ref[:, :buffer_rows] = high
    weigh_ref[:, buffer_rows:] = low
    send_x_ref[...] = dot_first(one, tokens_ref[...]).astype(jnp.bfloat16)
    cotangent = cotangent_ref[...]
    send_g_ref[...] = (dot_first(high, cotangent) + dot_first(low, cotangent)).astype(jnp.bfloat16)


def dispatch(routes, gates, home, tokens, cotangent):
    tok_rows, model_width = tokens.shape
    buffer_rows = tok_rows * routes.shape[1]
    return pl.pallas_call(
        dispatch_kernel,
        out_shape=(
            jax.ShapeDtypeStruct((buffer_rows, model_width), jnp.bfloat16),
            jax.ShapeDtypeStruct((buffer_rows, model_width), jnp.bfloat16),
            jax.ShapeDtypeStruct((tok_rows, buffer_rows), jnp.bfloat16),
            jax.ShapeDtypeStruct((tok_rows, 2 * buffer_rows), jnp.bfloat16),
        ),
        compiler_params=pltpu.CompilerParams(vmem_limit_bytes=VMEM_LIMIT),
    )(routes, gates, home, tokens, cotangent)


def expert_forward(x_rows, gathered):
    hidden_width = gathered.shape[1]
    model_width = gathered.shape[2]
    inner = gathered[:2].reshape(2 * hidden_width, model_width)
    projected = jnp.einsum("rd,gd->rg", x_rows, inner, preferred_element_type=jnp.float32)
    gate_pre = projected[:, :hidden_width]
    up_pre = projected[:, hidden_width:]
    sigmoid_gate = jax.nn.sigmoid(gate_pre)
    hidden = (gate_pre * sigmoid_gate * up_pre).astype(jnp.bfloat16)
    expert_out = jnp.dot(hidden, gathered[2], preferred_element_type=jnp.float32).astype(
        jnp.bfloat16
    )
    return (hidden, gate_pre, up_pre, sigmoid_gate, expert_out)


def expert_backward(upstream_rows, gathered, gate_pre, up_pre, sigmoid_gate):
    hidden_width = gathered.shape[1]
    model_width = gathered.shape[2]
    inner = gathered[:2].reshape(2 * hidden_width, model_width)
    hidden_grad = jnp.einsum(
        "rd,fd->rf", upstream_rows, gathered[2], preferred_element_type=jnp.float32
    )
    gate_grad = hidden_grad * up_pre * sigmoid_gate * (1.0 + gate_pre * (1.0 - sigmoid_gate))
    up_grad = hidden_grad * gate_pre * sigmoid_gate
    projected_grad = jnp.concatenate([gate_grad, up_grad], axis=1).astype(jnp.bfloat16)
    row_grad = jnp.dot(projected_grad, inner, preferred_element_type=jnp.float32).astype(
        jnp.bfloat16
    )
    return (projected_grad, row_grad)


def adam_update(weights, first_moment, second_moment, gradient):
    first_new = BETA_ONE * first_moment + (1.0 - BETA_ONE) * gradient
    second_new = BETA_TWO * second_moment + (1.0 - BETA_TWO) * gradient * gradient
    adam_step = (
        LEARN_RATE
        * (first_new / (1.0 - BETA_ONE**STEP_COUNT))
        / (jnp.sqrt(second_new / (1.0 - BETA_TWO**STEP_COUNT)) + EPSILON)
    )
    weight_new = (weights.astype(jnp.float32) - adam_step).astype(jnp.bfloat16)
    return (weight_new, first_new, second_new)


def shards(
    tokens, gates, routes, cotangent, old_home, swap_flags, weights, first_moment, second_moment
):
    slot_count = lax.axis_size("ep")
    top_bit = slot_count.bit_length() - 2
    own = lax.axis_index("ep")
    model_width = tokens.shape[1]
    flag_rows = jnp.concatenate([swap_flags, swap_flags])
    is_swapped = jnp.sum(jnp.where(jnp.arange(slot_count) == own, flag_rows, 0)) == 1

    def exchange(rows):
        rows = rows.reshape(slot_count, -1, model_width)
        rows = lax.all_to_all(rows, "ep", split_axis=0, concat_axis=0, tiled=True)
        return rows.reshape(-1, model_width)

    weights = jnp.where(is_swapped, partner(weights, "ep", top_bit), weights)
    gathered = lax.all_gather(weights[0], "tp", axis=1, tiled=True)
    new_home = jnp.where(flag_rows == 1, jnp.roll(old_home, -(slot_count // 2)), old_home)
    send_x, send_g, place, weigh = dispatch(
        routes, gates, new_home.reshape(1, -1), tokens, cotangent
    )
    x_rows = exchange(send_x)
    upstream_rows = exchange(send_g)
    hidden, gate_pre, up_pre, sigmoid_gate, expert_out = expert_forward(x_rows, gathered)
    back_out = exchange(expert_out)
    projected_grad, row_grad = expert_backward(
        upstream_rows, gathered, gate_pre, up_pre, sigmoid_gate
    )
    back_grad = exchange(row_grad)

    hidden_width = hidden.shape[1]
    down_terms = dot_first(hidden, upstream_rows).astype(jnp.bfloat16)[None]
    inner_terms = dot_first(projected_grad, x_rows).astype(jnp.bfloat16)
    inner_terms = inner_terms.reshape(2, hidden_width, model_width)
    down_sum = lax.psum_scatter(down_terms, "tp", scatter_dimension=1, tiled=True)
    inner_sum = lax.psum_scatter(inner_terms, "tp", scatter_dimension=1, tiled=True)
    gradient = jnp.concatenate([inner_sum, down_sum], axis=0)[None]

    other_first = partner(first_moment.astype(jnp.bfloat16), "ep", top_bit)
    other_second = partner(second_moment.astype(jnp.bfloat16), "ep", top_bit)
    first_moment = jnp.where(is_swapped, other_first.astype(jnp.float32), first_moment)
    second_moment = jnp.where(is_swapped, other_second.astype(jnp.float32), second_moment)
    gradient = gradient.astype(jnp.float32)
    new_weights, new_first, new_second = adam_update(weights, first_moment, second_moment, gradient)

    buffer_rows = place.shape[1]
    layer_output_rows = (
        jnp.dot(weigh[:, :buffer_rows], back_out, preferred_element_type=jnp.float32)
        + jnp.dot(weigh[:, buffer_rows:], back_out, preferred_element_type=jnp.float32)
    ).astype(jnp.bfloat16)
    token_gradient_rows = jnp.dot(place, back_grad, preferred_element_type=jnp.float32).astype(
        jnp.bfloat16
    )
    return (layer_output_rows, token_gradient_rows, new_weights, new_first, new_second)


def solution(mesh):
    in_specs = (
        P(("ep", "tp"), None),
        P(("ep", "tp"), None),
        P(("ep", "tp"), None),
        P(("ep", "tp"), None),
        P(),
        P(),
        P("ep", None, "tp", None),
        P("ep", None, "tp", None),
        P("ep", None, "tp", None),
    )
    out_specs = (
        P(("ep", "tp"), None),
        P(("ep", "tp"), None),
        P("ep", None, "tp", None),
        P("ep", None, "tp", None),
        P("ep", None, "tp", None),
    )
    return jax.shard_map(shards, mesh=mesh, in_specs=in_specs, out_specs=out_specs, check_vma=False)
```

time: 419 us -> 379 us (0.905)
  the two profiles are of different devices: /device:TPU:40 before, /device:TPU:10 now
where the time goes in v1:
time: 379 us; the launch traced here: 378 us
  waiting for transfers between devices  241 us (64%)
  starting transfers between devices  73.1 us (19%)
  matrix products  31.1 us (8%)
  between operations  14.5 us (4%)
  other arithmetic  7.34 us (2%)
  local copies, waits for them, and re-layouts  7.01 us (2%)
    ppermute x3, waiting for transfers between devices, partner(): lax.ppermute(array, axis, [(i, i ^ 1 << apart) for i in range(lax.axis_si...  109 us
    all_gather x1, waiting for transfers between devices, shards(): gathered = lax.all_gather(weights[0], 'tp', axis=1, tiled=True)  73.1 us
    all_to_all x4, starting transfers between devices, exchange(): rows = lax.all_to_all(rows, 'ep', split_axis=0, concat_axis=0, tiled=True)  56.5 us
    all_to_all x4, waiting for transfers between devices, exchange(): rows = lax.all_to_all(rows, 'ep', split_axis=0, concat_axis=0, tiled=True)  43.1 us
    ppermute x3, starting transfers between devices, partner(): lax.ppermute(array, axis, [(i, i ^ 1 << apart) for i in range(lax.axis_si...  16.3 us
    reduce_scatter x1, waiting for transfers between devices, shards(): lax.psum_scatter(inner_terms, 'tp', scatter_dimension=1, tiled=True)  16.2 us
    dot_general x2, matrix products, dot_first(): lax.dot_general(a, b, (((0,), (0,)), ((), ())), preferred_element_type=jn...  8.8 us
  transfers between devices with their start and end apart: 10, of which 6 were waited for; matrix products, arithmetic and copies ran while one was open for 7% of the time, Pallas kernels for 0%

profile of v1, /device:TPU:10, one launch (start us, length us, event | category | flops | bytes accessed | tf_op | source)
XLA Modules:
  0.0 378.1 jit_solution(14870875457992810020)
XLA Ops:
  7.2 0.8 fusion.14
  8.0 0.8 copy.14.routes_ref
  8.8 0.8 copy.15.gates_ref
  9.5 1.4 fusion.9
  11.0 0.0 copy-start
  11.0 0.9 copy-done
  11.9 0.0 copy-start.1
  11.9 0.9 copy-done.1
  12.9 3.7 shard_map.128
  16.6 0.0 copy-start.5
  16.6 19.1 %all-to-all-start = ((bf16[64,16,1024]{2,1,0:T(8,128)(2,1)}), bf16[64,16,1024]{2,1,0:T(8,128)(2,1)S(1)}, u32[]{:S(2)}, u32[]{:S(2)}) async-start(bf16[64,16,1024]{2,1,0:T(8,128)(2,1)} %bitcast.1), calls=%async_computation | async-start | bytes 4194304 | tf_op jit(solution)/shard_map/all_to_all | solution.py:135
  35.7 0.0 all-gather.3.cloned.1.call-start
  35.8 0.0 copy-done.5
  35.8 6.5 %collective-permute-start = (bf16[1,3,48,1024]{3,2,1,0:T(8,128)(2,1)S(1)}, bf16[1,3,48,1024]{3,2,1,0:T(8,128)(2,1)S(1)}, u32[]{:S(2)}, u32[]{:S(2)}) collective-permute-start(bf16[1,3,48,1024]{3,2,1,0:T(8,128)(2,1)S(1)} %copy-done.5), channel_id=1, source_target_pairs={{0,256},{8,264},{16,272},{24,280},{32,288},{40,296},{48,304},{56,3... | collective-permute-start | bytes 884744 | tf_op jit(solution)/shard_map/ppermute | solution.py:18
  43.0 54.9 %collective-permute-done = bf16[1,3,48,1024]{3,2,1,0:T(8,128)(2,1)S(1)} collective-permute-done((bf16[1,3,48,1024]{3,2,1,0:T(8,128)(2,1)S(1)}, bf16[1,3,48,1024]{3,2,1,0:T(8,128)(2,1)S(1)}, u32[]{:S(2)}, u32[]{:S(2)}) %collective-permute-start) | collective-permute-done | bytes 294944 | tf_op jit(solution)/shard_map/ppermute | solution.py:18
  97.9 0.7 broadcast_select_fusion
  98.6 0.0 all-gather.3.cloned.1.call-update
  98.7 0.0 all-to-all-done
  98.7 0.0 copy-start.3
  98.7 12.2 %all-to-all-start.2 = ((bf16[64,16,1024]{2,1,0:T(8,128)(2,1)}), bf16[64,16,1024]{2,1,0:T(8,128)(2,1)}, u32[]{:S(2)}, u32[]{:S(2)}) async-start(bf16[64,16,1024]{2,1,0:T(8,128)(2,1)} %bitcast.7), calls=%async_computation.2 | async-start | bytes 4194304 | tf_op jit(solution)/shard_map/all_to_all | solution.py:135
  110.9 73.1 %all-gather.3.cloned.1.call-done = bf16[1,3,384,1024]{3,2,1,0:T(8,128)(2,1)} async-done(((bf16[1,3,48,1024]{3,2,1,0:T(8,128)(2,1)}), bf16[1,3,384,1024]{3,2,1,0:T(8,128)(2,1)}) %all-gather.3.cloned.1.call-update) | async-done | bytes 2359312 | tf_op jit(solution)/shard_map/all_gather | solution.py:139
  184.0 1.5 slice.38
  185.5 0.0 copy-start.4
  185.5 0.0 copy-done.3
  185.5 1.2 copy-done.4
  186.7 3.5 fusion.15
  190.2 0.0 all-to-all-done.2
  190.2 5.4 %multiply_convert_fusion.1 = (bf16[1024,384]{0,1:T(8,128)(2,1)}, bf16[1024,384]{0,1:T(8,128)(2,1)}, bf16[1024,384]{0,1:T(8,128)(2,1)S(1)}) fusion(f32[1024,768]{0,1:T(8,128)} %fusion.15, bf16[1024,1024]{1,0:T(8,128)(2,1)} %bitcast.8, bf16[1,3,384,1024]{3,2,1,0:T(8,128)(2,1)} %all-gather.3.cloned.1.call-done), kind=kOutput, calls=%fused_computation.5 | convolution fusion | flops 811597824 | bytes 8388608 | tf_op jit(solution)/shard_map/rd,fd->rf/dot_general | solution.py:99
  195.6 0.0 copy-start.6
  195.6 4.0 %convolution_convert_fusion = bf16[1024,1024]{1,0:T(8,128)(2,1)} fusion(bf16[1024,384]{0,1:T(8,128)(2,1)S(1)} %get-tuple-element.18, bf16[1,3,384,1024]{3,2,1,0:T(8,128)(2,1)} %all-gather.3.cloned.1.call-done), kind=kOutput, calls=%fused_computation | convolution fusion | flops 806354944 | bytes 3670016 | tf_op jit(solution)/shard_map/dot_general | solution.py:89
  199.6 0.0 copy-done.6
  199.6 13.0 %all-to-all-start.1 = ((bf16[64,16,1024]{2,1,0:T(8,128)(2,1)}), bf16[64,16,1024]{2,1,0:T(8,128)(2,1)S(1)}, u32[]{:S(2)}, u32[]{:S(2)}) async-start(bf16[64,16,1024]{2,1,0:T(8,128)(2,1)} %bitcast.39), calls=%async_computation.1 | async-start | bytes 4194304 | tf_op jit(solution)/shard_map/all_to_all | solution.py:135
  212.7 0.2 reduce-scatter.5.cloned.1.call-start
  212.9 3.7 fusion
  216.6 0.0 reduce-scatter.5.cloned.1.call-update
  216.6 5.1 %convolution_convert_fusion.1 = bf16[1024,1024]{1,0:T(8,128)(2,1)} fusion(bf16[768,1024]{1,0:T(8,128)(2,1)} %bitcast.41, bf16[1024,384]{0,1:T(8,128)(2,1)} %get-tuple-element.17, bf16[1024,384]{0,1:T(8,128)(2,1)} %get-tuple-element.16), kind=kOutput, calls=%fused_computation.1 | convolution fusion | flops 1614807040 | bytes 5242880 | tf_op jit(solution)/shard_map/dot_general | solution.py:105
  221.7 43.1 %all-to-all-done.1 = bf16[64,16,1024]{2,1,0:T(8,128)(2,1)S(1)} async-done(((bf16[64,16,1024]{2,1,0:T(8,128)(2,1)}), bf16[64,16,1024]{2,1,0:T(8,128)(2,1)S(1)}, u32[]{:S(2)}, u32[]{:S(2)}) %all-to-all-start.1) | async-done | bytes 2097184 | tf_op jit(solution)/shard_map/all_to_all | solution.py:135
  264.7 12.2 %all-to-all-start.3 = ((bf16[64,16,1024]{2,1,0:T(8,128)(2,1)}), bf16[64,16,1024]{2,1,0:T(8,128)(2,1)}, u32[]{:S(2)}, u32[]{:S(2)}) async-start(bf16[64,16,1024]{2,1,0:T(8,128)(2,1)} %bitcast.38), calls=%async_computation.3 | async-start | bytes 4194304 | tf_op jit(solution)/shard_map/all_to_all | solution.py:135
  276.9 0.0 reduce-scatter.3.cloned.1.call-start
  277.0 5.1 %convolution_convert_fusion.2 = bf16[768,1024]{1,0:T(8,128)(2,1)} fusion(bf16[1024,1024]{1,0:T(8,128)(2,1)} %bitcast.37, bf16[1024,384]{0,1:T(8,128)(2,1)} %get-tuple-element.17, bf16[1024,384]{0,1:T(8,128)(2,1)} %get-tuple-element.16), kind=kOutput, calls=%fused_computation.2 | convolution fusion | flops 1614544896 | bytes 5242880 | tf_op jit(solution)/shard_map/dot_general | solution.py:22
  282.1 0.0 copy-start.2
  282.1 0.0 reduce-scatter.3.cloned.1.call-update
  282.1 1.1 convert_element_type.61
  283.2 6.5 %collective-permute-start.1 = (bf16[1,3,48,1024]{3,2,1,0:T(8,128)(2,1)S(1)}, bf16[1,3,48,1024]{3,2,1,0:T(8,128)(2,1)S(1)}, u32[]{:S(2)}, u32[]{:S(2)}) collective-permute-start(bf16[1,3,48,1024]{3,2,1,0:T(8,128)(2,1)S(1)} %convert_element_type.61), channel_id=1, source_target_pairs={{0,256},{8,264},{16,272},{24,280},{32,288},{40,296},{48,304},{56,3... | collective-permute-start | bytes 884744 | tf_op jit(solution)/shard_map/ppermute | solution.py:18
  289.8 1.1 convert_element_type.66
  290.9 3.2 collective-permute-start.2
  294.1 50.1 %collective-permute-done.1 = bf16[1,3,48,1024]{3,2,1,0:T(8,128)(2,1)S(1)} collective-permute-done((bf16[1,3,48,1024]{3,2,1,0:T(8,128)(2,1)S(1)}, bf16[1,3,48,1024]{3,2,1,0:T(8,128)(2,1)S(1)}, u32[]{:S(2)}, u32[]{:S(2)}) %collective-permute-start.1) | collective-permute-done | bytes 294944 | tf_op jit(solution)/shard_map/ppermute | solution.py:18
  344.2 4.0 %collective-permute-done.2 = bf16[1,3,48,1024]{3,2,1,0:T(8,128)(2,1)} collective-permute-done((bf16[1,3,48,1024]{3,2,1,0:T(8,128)(2,1)S(1)}, bf16[1,3,48,1024]{3,2,1,0:T(8,128)(2,1)}, u32[]{:S(2)}, u32[]{:S(2)}) %collective-permute-start.2) | collective-permute-done | bytes 294944 | tf_op jit(solution)/shard_map/ppermute | solution.py:18
  348.2 0.0 reduce-scatter.5.cloned.1.call-done
  348.2 16.2 %reduce-scatter.3.cloned.1.call-done = bf16[2,48,1024]{2,1,0:T(8,128)(2,1)} async-done(((bf16[2,384,1024]{2,1,0:T(8,128)(2,1)}), bf16[2,48,1024]{2,1,0:T(8,128)(2,1)}) %reduce-scatter.3.cloned.1.call-update) | async-done | bytes 196624 | tf_op jit(solution)/shard_map/reduce_scatter | solution.py:158
  364.3 0.0 copy-done.2
  364.3 2.9 subtract_convert_fusion
  367.2 0.4 fusion.6
  367.7 1.2 fusion.1
  368.8 0.0 all-to-all-done.3
  368.8 2.7 convolution_convert_fusion.4
Async XLA Ops:
  11.0 0.9 copy-start
  11.9 0.9 copy-start.1
  16.6 19.2 %copy-start.5 = (bf16[1,3,48,1024]{3,2,1,0:T(8,128)(2,1)S(1)}, bf16[1,3,48,1024]{3,2,1,0:T(8,128)(2,1)}, u32[]{:S(2)}) copy-start(bf16[1,3,48,1024]{3,2,1,0:T(8,128)(2,1)} %param.15) | copy-start | bytes 884740
  16.6 82.1 %all-to-all-start = ((bf16[64,16,1024]{2,1,0:T(8,128)(2,1)}), bf16[64,16,1024]{2,1,0:T(8,128)(2,1)S(1)}, u32[]{:S(2)}, u32[]{:S(2)}) async-start(bf16[64,16,1024]{2,1,0:T(8,128)(2,1)} %bitcast.1), calls=%async_computation | async-start | bytes 4194304 | tf_op jit(solution)/shard_map/all_to_all | solution.py:135
  35.7 148.2 %all-gather.3.cloned.1.call-start = ((), (), s32[]{:S(2)}) async-start(), calls=%async_computation.8 | async-start | bytes 2654208 | tf_op jit(solution)/shard_map/all_gather | solution.py:139
  35.8 62.1 %collective-permute-start = (bf16[1,3,48,1024]{3,2,1,0:T(8,128)(2,1)S(1)}, bf16[1,3,48,1024]{3,2,1,0:T(8,128)(2,1)S(1)}, u32[]{:S(2)}, u32[]{:S(2)}) collective-permute-start(bf16[1,3,48,1024]{3,2,1,0:T(8,128)(2,1)S(1)} %copy-done.5), channel_id=1, source_target_pairs={{0,256},{8,264},{16,272},{24,280},{32,288},{40,296},{48,304},{56,3... | collective-permute-start | bytes 884744 | tf_op jit(solution)/shard_map/ppermute | solution.py:18
  98.7 86.8 %copy-start.3 = (bf16[64,16,1024]{2,1,0:T(8,128)(2,1)}, bf16[64,16,1024]{2,1,0:T(8,128)(2,1)S(1)}, u32[]{:S(2)}) copy-start(bf16[64,16,1024]{2,1,0:T(8,128)(2,1)S(1)} %all-to-all-done) | copy-start | bytes 6291460
  98.7 91.5 %all-to-all-start.2 = ((bf16[64,16,1024]{2,1,0:T(8,128)(2,1)}), bf16[64,16,1024]{2,1,0:T(8,128)(2,1)}, u32[]{:S(2)}, u32[]{:S(2)}) async-start(bf16[64,16,1024]{2,1,0:T(8,128)(2,1)} %bitcast.7), calls=%async_computation.2 | async-start | bytes 4194304 | tf_op jit(solution)/shard_map/all_to_all | solution.py:135
  185.5 1.2 copy-start.4
  195.6 4.0 %copy-start.6 = (bf16[1024,384]{0,1:T(8,128)(2,1)}, bf16[1024,384]{0,1:T(8,128)(2,1)S(1)}, u32[]{:S(2)}) copy-start(bf16[1024,384]{0,1:T(8,128)(2,1)S(1)} %get-tuple-element.18) | copy-start | bytes 2359300
  199.6 65.1 %all-to-all-start.1 = ((bf16[64,16,1024]{2,1,0:T(8,128)(2,1)}), bf16[64,16,1024]{2,1,0:T(8,128)(2,1)S(1)}, u32[]{:S(2)}, u32[]{:S(2)}) async-start(bf16[64,16,1024]{2,1,0:T(8,128)(2,1)} %bitcast.39), calls=%async_computation.1 | async-start | bytes 4194304 | tf_op jit(solution)/shard_map/all_to_all | solution.py:135
  212.7 135.5 %reduce-scatter.5.cloned.1.call-start = ((), (), s32[]{:S(2)}) async-start(), calls=%async_computation.7 | async-start | bytes 884736 | tf_op jit(solution)/shard_map/reduce_scatter | solution.py:157
  264.7 104.1 %all-to-all-start.3 = ((bf16[64,16,1024]{2,1,0:T(8,128)(2,1)}), bf16[64,16,1024]{2,1,0:T(8,128)(2,1)}, u32[]{:S(2)}, u32[]{:S(2)}) async-start(bf16[64,16,1024]{2,1,0:T(8,128)(2,1)} %bitcast.38), calls=%async_computation.3 | async-start | bytes 4194304 | tf_op jit(solution)/shard_map/all_to_all | solution.py:135
  276.9 87.4 %reduce-scatter.3.cloned.1.call-start = ((), (), s32[]{:S(2)}) async-start(), calls=%async_computation.6 | async-start | bytes 1769472 | tf_op jit(solution)/shard_map/reduce_scatter | solution.py:158
  282.1 82.3 %copy-start.2 = (bf16[1,3,48,1024]{3,2,1,0:T(8,128)(2,1)S(1)}, bf16[1,3,48,1024]{3,2,1,0:T(8,128)(2,1)}, u32[]{:S(2)}) copy-start(bf16[1,3,48,1024]{3,2,1,0:T(8,128)(2,1)} %broadcast_select_fusion) | copy-start | bytes 884740
  283.2 60.9 %collective-permute-start.1 = (bf16[1,3,48,1024]{3,2,1,0:T(8,128)(2,1)S(1)}, bf16[1,3,48,1024]{3,2,1,0:T(8,128)(2,1)S(1)}, u32[]{:S(2)}, u32[]{:S(2)}) collective-permute-start(bf16[1,3,48,1024]{3,2,1,0:T(8,128)(2,1)S(1)} %convert_element_type.61), channel_id=1, source_target_pairs={{0,256},{8,264},{16,272},{24,280},{32,288},{40,296},{48,304},{56,3... | collective-permute-start | bytes 884744 | tf_op jit(solution)/shard_map/ppermute | solution.py:18
  290.9 57.2 %collective-permute-start.2 = (bf16[1,3,48,1024]{3,2,1,0:T(8,128)(2,1)S(1)}, bf16[1,3,48,1024]{3,2,1,0:T(8,128)(2,1)}, u32[]{:S(2)}, u32[]{:S(2)}) collective-permute-start(bf16[1,3,48,1024]{3,2,1,0:T(8,128)(2,1)S(1)} %convert_element_type.66), channel_id=1, source_target_pairs={{0,256},{8,264},{16,272},{24,280},{32,288},{40,296},{48,304},{56,3... | collective-permute-start | bytes 884744 | tf_op jit(solution)/shard_map/ppermute | solution.py:18
Sparse Core Ops, SparseCore 0:
  98.8 85.1 all-gather.2
  216.7 78.7 reduce-scatter.4
  298.6 65.6 reduce-scatter.2

commit v2 on v1

v2 whole, which is shorter than its diff:
```python
import jax
import jax.numpy as jnp
from jax import lax
from jax.experimental import pallas as pl
from jax.experimental.pallas import tpu as pltpu
from jax.sharding import PartitionSpec as P

BETA_ONE = 0.9
BETA_TWO = 0.95
LEARN_RATE = 0.001
EPSILON = 1e-08
STEP_COUNT = 20.0

X_SIZE = 4
VMEM_LIMIT = 60 * 1024 * 1024
PARAMS = pltpu.CompilerParams(vmem_limit_bytes=VMEM_LIMIT)


def partner(array, apart):
    return lax.ppermute(array, "ep", [(i, i ^ apart) for i in range(lax.axis_size("ep"))])


def dot(a, b):
    return jnp.dot(a, b, preferred_element_type=jnp.float32)


def dot_last(a, b):
    return lax.dot_general(a, b, (((1,), (1,)), ((), ())), preferred_element_type=jnp.float32)


def dot_first(a, b):
    return lax.dot_general(a, b, (((0,), (0,)), ((), ())), preferred_element_type=jnp.float32)


def iota(shape, axis):
    return lax.broadcasted_iota(jnp.int32, shape, axis)


def route_kernel(pack_ref, home_ref, flags_ref, tokens_ref, cotangent_ref, send_ref, mats_ref):
    top_count = pack_ref.shape[0] // 2
    tok_rows = pack_ref.shape[1]
    slot_count = home_ref.shape[1]
    pairs = slot_count // 2
    half = slot_count // 2
    rows = send_ref.shape[0]
    capacity = rows // half // 2
    z_half = lax.axis_index("ep") // X_SIZE % 2
    place = iota((half, 1), 0)
    slot = (place // X_SIZE * 2 + z_half) * X_SIZE + place % X_SIZE
    flag = jnp.sum(
        jnp.where(iota((half, pairs), 1) == slot % pairs, flags_ref[...].astype(jnp.float32), 0.0),
        axis=1,
        keepdims=True,
    )
    source = jnp.where(flag > 0, (slot + pairs) % slot_count, slot)
    expert = jnp.sum(
        jnp.where(iota((half, slot_count), 1) == source, home_ref[...].astype(jnp.float32), 0.0),
        axis=1,
        keepdims=True,
    )
    named = jnp.zeros((half, tok_rows), jnp.float32)
    gate = jnp.zeros((half, tok_rows), jnp.float32)
    for k in range(top_count):
        hit = pack_ref[k : k + 1, :] == expert
        named = named + jnp.where(hit, 1.0, 0.0)
        gate = gate + jnp.where(hit, pack_ref[top_count + k : top_count + k + 1, :], 0.0)
    earlier = iota((tok_rows, tok_rows), 0) < iota((tok_rows, tok_rows), 1)
    earlier = jnp.where(earlier, 1.0, 0.0).astype(jnp.bfloat16)
    rank = jnp.where(named > 0, dot(named.astype(jnp.bfloat16), earlier), -1.0)
    spread = iota((rows, half), 0) // (2 * capacity) == iota((rows, half), 1)
    spread = jnp.where(spread, 1.0, 0.0).astype(jnp.bfloat16)
    gate_high = gate.astype(jnp.bfloat16)
    gate_low = (gate - gate_high.astype(jnp.float32)).astype(jnp.bfloat16)
    row = iota((rows, 1), 0)
    hit = dot(spread, rank.astype(jnp.bfloat16)) == (row % capacity).astype(jnp.float32)
    first = row // capacity % 2 == 0
    high = dot(spread, gate_high)
    low = dot(spread, gate_low)

    def pick(values, kind):
        return jnp.where(hit & kind, values, 0.0).astype(jnp.bfloat16)

    second = jnp.logical_not(first)
    mats_ref[0] = pick(high, first)
    mats_ref[1] = pick(low, first)
    mats_ref[2] = pick(1.0, second)
    cotangent = cotangent_ref[...]
    send_ref[...] = (
        dot(pick(1.0, first), tokens_ref[...])
        + dot(pick(high, second), cotangent)
        + dot(pick(low, second), cotangent)
    ).astype(jnp.bfloat16)


def route(pack, home, flags, tokens, cotangent):
    tok_rows, model_width = tokens.shape
    rows = tok_rows * (pack.shape[0] // 2)
    return pl.pallas_call(
        route_kernel,
        out_shape=(
            jax.ShapeDtypeStruct((rows, model_width), jnp.bfloat16),
            jax.ShapeDtypeStruct((3, rows, tok_rows), jnp.bfloat16),
        ),
        compiler_params=PARAMS,
        name="route",
    )(pack, home, flags, tokens, cotangent)


def expert_kernel(arrived_ref, weights_ref, back_ref, act_ref):
    sources, double, width = arrived_ref.shape
    capacity = double // 2
    hidden_width = weights_ref.shape[1]
    x_rows = arrived_ref[:, :capacity, :].reshape(sources * capacity, width)
    upstream = arrived_ref[:, capacity:, :].reshape(sources * capacity, width)
    w_gate, w_up, w_down = weights_ref[0], weights_ref[1], weights_ref[2]
    gate_pre = dot_last(x_rows, w_gate)
    up_pre = dot_last(x_rows, w_up)
    sigmoid = jax.nn.sigmoid(gate_pre)
    hidden = (gate_pre * sigmoid * up_pre).astype(jnp.bfloat16)
    out = dot(hidden, w_down).astype(jnp.bfloat16)
    back_ref[:, :capacity, :] = out.reshape(sources, capacity, width)
    hidden_grad = dot_last(upstream, w_down)
    gate_grad = hidden_grad * up_pre * sigmoid * (1.0 + gate_pre * (1.0 - sigmoid))
    gate_grad = gate_grad.astype(jnp.bfloat16)
    up_grad = (hidden_grad * gate_pre * sigmoid).astype(jnp.bfloat16)
    row_grad = (dot(gate_grad, w_gate) + dot(up_grad, w_up)).astype(jnp.bfloat16)
    back_ref[:, capacity:, :] = row_grad.reshape(sources, capacity, width)
    act_ref[:, :hidden_width] = gate_grad
    act_ref[:, hidden_width : 2 * hidden_width] = up_grad
    act_ref[:, 2 * hidden_width :] = hidden


def expert(arrived, weights, steps):
    sources, double, width = arrived.shape
    hidden_width = weights.shape[1]
    block = sources // steps
    rows = block * double // 2
    return pl.pallas_call(
        expert_kernel,
        grid=(steps,),
        in_specs=[
            pl.BlockSpec((block, double, width), lambda i: (i, 0, 0)),
            pl.BlockSpec((3, hidden_width, width), lambda i: (0, 0, 0)),
        ],
        out_specs=(
            pl.BlockSpec((block, double, width), lambda i: (i, 0, 0)),
            pl.BlockSpec((rows, 3 * hidden_width), lambda i: (i, 0)),
        ),
        out_shape=(
            jax.ShapeDtypeStruct(arrived.shape, jnp.bfloat16),
            jax.ShapeDtypeStruct((rows * steps, 3 * hidden_width), jnp.bfloat16),
        ),
        compiler_params=PARAMS,
        name="expert",
    )(arrived, weights)


def terms_kernel(one_ref, one_act_ref, two_ref, two_act_ref, terms_ref):
    sources, double, width = one_ref.shape
    capacity = double // 2
    inner = terms_ref.shape[0] // 3 * 2

    def kind(ref, low):
        return ref[:, low : low + capacity, :].reshape(sources * capacity, width)

    terms_ref[:inner] = (
        dot_first(one_act_ref[:, :inner], kind(one_ref, 0))
        + dot_first(two_act_ref[:, :inner], kind(two_ref, 0))
    ).astype(jnp.bfloat16)
    terms_ref[inner:] = (
        dot_first(one_act_ref[:, inner:], kind(one_ref, capacity))
        + dot_first(two_act_ref[:, inner:], kind(two_ref, capacity))
    ).astype(jnp.bfloat16)


def gradient_terms(one, one_act, two, two_act):
    return pl.pallas_call(
        terms_kernel,
        out_shape=jax.ShapeDtypeStruct((one_act.shape[1], one.shape[2]), jnp.bfloat16),
        compiler_params=PARAMS,
        name="terms",
    )(one, one_act, two, two_act)


def share_kernel(back_ref, mats_ref, share_ref):
    back = back_ref[...]
    tok_rows = mats_ref.shape[2]
    out = dot_first(mats_ref[0], back) + dot_first(mats_ref[1], back)
    share_ref[:tok_rows] = out.astype(jnp.bfloat16)
    share_ref[tok_rows:] = dot_first(mats_ref[2], back).astype(jnp.bfloat16)


def share(back, mats):
    return pl.pallas_call(
        share_kernel,
        out_shape=jax.ShapeDtypeStruct((2 * mats.shape[2], back.shape[1]), jnp.bfloat16),
        compiler_params=PARAMS,
        name="share",
    )(back, mats)


def combine_kernel(back_ref, mats_ref, share_ref, out_ref, grad_ref):
    back = back_ref[...]
    tok_rows = mats_ref.shape[2]
    out = dot_first(mats_ref[0], back) + dot_first(mats_ref[1], back)
    out_ref[...] = (out + share_ref[:tok_rows].astype(jnp.float32)).astype(jnp.bfloat16)
    grad = dot_first(mats_ref[2], back)
    grad_ref[...] = (grad + share_ref[tok_rows:].astype(jnp.float32)).astype(jnp.bfloat16)


def combine(back, mats, other_share):
    shape = jax.ShapeDtypeStruct((mats.shape[2], back.shape[1]), jnp.bfloat16)
    return pl.pallas_call(
        combine_kernel,
        out_shape=(shape, shape),
        compiler_params=PARAMS,
        name="combine",
    )(back, mats, other_share)


def adam_update(weights, first_moment, second_moment, gradient):
    first_new = BETA_ONE * first_moment + (1.0 - BETA_ONE) * gradient
    second_new = BETA_TWO * second_moment + (1.0 - BETA_TWO) * gradient * gradient
    adam_step = (
        LEARN_RATE
        * (first_new / (1.0 - BETA_ONE**STEP_COUNT))
        / (jnp.sqrt(second_new / (1.0 - BETA_TWO**STEP_COUNT)) + EPSILON)
    )
    weight_new = (weights.astype(jnp.float32) - adam_step).astype(jnp.bfloat16)
    return (weight_new, first_new, second_new)


def shards(
    tokens, gates, routes, cotangent, old_home, swap_flags, weights, first_moment, second_moment
):
    slot_count = lax.axis_size("ep")
    half = slot_count // 2
    own = lax.axis_index("ep")
    model_width = tokens.shape[1]
    hidden_width = weights.shape[2] * lax.axis_size("tp")
    is_swapped = jnp.sum(jnp.where(jnp.arange(half) == own % half, swap_flags, 0)) == 1
    groups = [
        [i for i in range(slot_count) if i // X_SIZE % 2 == z_half] for z_half in range(2)
    ]

    def exchange(rows):
        rows = rows.reshape(half, -1, model_width)
        return lax.all_to_all(
            rows, "ep", split_axis=0, concat_axis=0, tiled=True, axis_index_groups=groups
        )

    home = old_home.reshape(1, -1)
    flags = swap_flags.reshape(1, -1)
    pack = jnp.concatenate([routes.T.astype(jnp.float32), gates.T], axis=0)
    own_send, own_mats = route(pack, home, flags, tokens, cotangent)
    own_arrived = exchange(own_send)
    both = jnp.concatenate([tokens, cotangent], axis=0)
    pack, both, _ = lax.optimization_barrier((pack, both, own_send))
    other_pack, both = partner(pack, X_SIZE), partner(both, X_SIZE)
    tok_rows = tokens.shape[0]
    other_send, other_mats = route(other_pack, home, flags, both[:tok_rows], both[tok_rows:])
    first_sent, second_sent = first_moment.astype(jnp.bfloat16), second_moment.astype(jnp.bfloat16)
    other_send, own_arrived, first_sent = lax.optimization_barrier(
        (other_send, own_arrived, first_sent)
    )
    other_first = partner(first_sent, half)
    other_arrived = exchange(other_send)

    weights = jnp.where(is_swapped, partner(weights, half), weights)
    gathered = lax.all_gather(weights[0], "tp", axis=1, tiled=True)
    own_back, own_act = expert(own_arrived, gathered, 2)
    other_arrived, own_back, own_act, other_first, second_sent = lax.optimization_barrier(
        (other_arrived, own_back, own_act, other_first, second_sent)
    )
    other_second = partner(second_sent, half)
    other_back, other_act = expert(other_arrived, gathered, 2)
    other_returned = exchange(other_back)
    own_back, other_returned, other_second = lax.optimization_barrier(
        (own_back, other_returned, other_second)
    )
    own_returned = exchange(own_back).reshape(-1, model_width)
    other_returned = other_returned.reshape(-1, model_width)

    terms = gradient_terms(own_arrived, own_act, other_arrived, other_act)
    terms = terms.reshape(3, hidden_width, model_width)
    gradient = lax.psum_scatter(terms, "tp", scatter_dimension=1, tiled=True)
    gradient = gradient[None].astype(jnp.float32)
    first_moment = jnp.where(is_swapped, other_first.astype(jnp.float32), first_moment)
    second_moment = jnp.where(is_swapped, other_second.astype(jnp.float32), second_moment)
    new_weights, new_first, new_second = adam_update(weights, first_moment, second_moment, gradient)

    other_share = partner(share(other_returned, other_mats), X_SIZE)
    layer_output_rows, token_gradient_rows = combine(own_returned, own_mats, other_share)
    return (layer_output_rows, token_gradient_rows, new_weights, new_first, new_second)


def solution(mesh):
    in_specs = (
        P(("ep", "tp"), None),
        P(("ep", "tp"), None),
        P(("ep", "tp"), None),
        P(("ep", "tp"), None),
        P(),
        P(),
        P("ep", None, "tp", None),
        P("ep", None, "tp", None),
        P("ep", None, "tp", None),
    )
    out_specs = (
        P(("ep", "tp"), None),
        P(("ep", "tp"), None),
        P("ep", None, "tp", None),
        P("ep", None, "tp", None),
        P("ep", None, "tp", None),
    )
    return jax.shard_map(shards, mesh=mesh, in_specs=in_specs, out_specs=out_specs, check_vma=False)
```

time: 379 us -> 307 us (0.81)
  the two profiles are of different devices: /device:TPU:10 before, /device:TPU:386 now
where the time goes in v2:
time: 307 us; the launch traced here: 306 us
  waiting for transfers between devices  176 us (57%)
  starting transfers between devices  64.8 us (21%)
  Pallas kernels  38.3 us (12%)
  between operations  14.9 us (5%)
  other arithmetic  8.2 us (3%)
  local copies, waits for them, and re-layouts  4.23 us (1%)
    ppermute x6, waiting for transfers between devices, partner(): lax.ppermute(array, 'ep', [(i, i ^ apart) for i in range(lax.axis_size('e...  147 us
    ppermute x6, starting transfers between devices, partner(): lax.ppermute(array, 'ep', [(i, i ^ apart) for i in range(lax.axis_size('e...  33.5 us
    all_to_all x4, starting transfers between devices, exchange(): lax.all_to_all(rows, 'ep', split_axis=0, concat_axis=0, tiled=True, axis_...  31.3 us
    all_to_all x4, waiting for transfers between devices, exchange(): lax.all_to_all(rows, 'ep', split_axis=0, concat_axis=0, tiled=True, axis_...  16.7 us
    pallas_call x2, Pallas kernels, expert(): pl.pallas_call(expert_kernel, grid=(steps,), in_specs=[pl.BlockSpec((bloc...  14.2 us
    all_gather x1, waiting for transfers between devices, shards(): gathered = lax.all_gather(weights[0], 'tp', axis=1, tiled=True)  11.4 us
    pallas_call x2, Pallas kernels, route(): pl.pallas_call(route_kernel, out_shape=(jax.ShapeDtypeStruct((rows, model...  9.86 us
    pallas_call x1, Pallas kernels, gradient_terms(): pl.pallas_call(terms_kernel, out_shape=jax.ShapeDtypeStruct((one_act.shap...  6.93 us
  transfers between devices with their start and end apart: 12, of which 6 were waited for; matrix products, arithmetic and copies ran while one was open for 2% of the time, Pallas kernels for 7%

profile of v2, /device:TPU:386, one launch (start us, length us, event | category | flops | bytes accessed | tf_op | source)
XLA Modules:
  0.0 306.1 jit_solution(202586241280690362)
XLA Ops:
  7.2 0.7 convert_bitcast_fusion
  7.9 1.3 pad_maximum_fusion.1.pack_ref
  9.1 4.9 %route.2 = (bf16[1024,1024]{1,0:T(8,128)(2,1)}, bf16[3,1024,128]{2,1,0:T(8,128)(2,1)}) custom-call(f32[16,128]{1,0:T(8,128)} %pad_maximum_fusion.1.pack_ref, s32[1,64]{1,0:T(1,128)} %bitcast.28, s32[1,32]{1,0:T(1,128)} %bitcast.30, bf16[128,1024]{1,0:T(8,128)(2,1)} %tokens_ref.1, bf16[128,1024]{1,0:T(8,128)(2,1)} %cotangent_ref.1), custom_call_target="tpu_custom_call" | custom-call | tf_op jit(solution)/shard_map/route/pallas_call | solution.py:98
  14.1 0.0 copy-start.10
  14.1 0.0 copy-start.5
  14.1 0.0 copy-start.11
  14.1 0.0 copy-start.3
  14.1 0.0 copy-start.13
  14.1 10.4 %all-to-all-start = ((bf16[32,32,1024]{2,1,0:T(8,128)(2,1)}), bf16[32,32,1024]{2,1,0:T(8,128)(2,1)S(1)}, u32[]{:S(2)}, u32[]{:S(2)}) async-start(bf16[32,32,1024]{2,1,0:T(8,128)(2,1)} %bitcast.25), calls=%async_computation | async-start | bytes 4194304 | tf_op jit(solution)/shard_map/all_to_all | solution.py:248
  24.5 0.0 all-gather.3.cloned.1.call-start
  24.6 0.0 copy-done.10
  24.6 7.3 %collective-permute-start.2 = (bf16[1,3,48,1024]{3,2,1,0:T(8,128)(2,1)S(1)}, bf16[1,3,48,1024]{3,2,1,0:T(8,128)(2,1)}, u32[]{:S(2)}, u32[]{:S(2)}) collective-permute-start(bf16[1,3,48,1024]{3,2,1,0:T(8,128)(2,1)S(1)} %copy-done.10), channel_id=1, source_target_pairs={{0,256},{8,264},{16,272},{24,280},{32,288},{40,296},{48,304},{56,3... | collective-permute-start | bytes 884744 | tf_op jit(solution)/shard_map/ppermute | solution.py:20
  31.9 0.0 copy-done.5
  31.9 0.0 copy-done.6
  31.9 0.8 pad_maximum_fusion
  32.7 1.9 collective-permute-start.1
  34.7 0.0 copy-done.11
  34.7 7.8 %collective-permute-start = (f32[16,128]{1,0:T(8,128)S(1)}, f32[16,128]{1,0:T(8,128)S(1)}, u32[]{:S(2)}, u32[]{:S(2)}) collective-permute-start(f32[16,128]{1,0:T(8,128)S(1)} %copy-done.11), channel_id=1, source_target_pairs={{0,32},{8,40},{16,48},{24,56},{32,0},{40,8},{48,16},{56,24},{64,96... | collective-permute-start | bytes 24584 | tf_op jit(solution)/shard_map/ppermute | solution.py:20
  42.5 0.0 copy-done.3
  42.5 0.8 convert_element_type.30
  43.3 0.0 copy-done.13
  43.3 0.6 fusion.4
  44.6 43.3 %collective-permute-done.2 = bf16[1,3,48,1024]{3,2,1,0:T(8,128)(2,1)} collective-permute-done((bf16[1,3,48,1024]{3,2,1,0:T(8,128)(2,1)S(1)}, bf16[1,3,48,1024]{3,2,1,0:T(8,128)(2,1)}, u32[]{:S(2)}, u32[]{:S(2)}) %collective-permute-start.2) | collective-permute-done | bytes 294944 | tf_op jit(solution)/shard_map/ppermute | solution.py:20
  87.8 0.7 broadcast_select_fusion
  88.6 0.0 all-gather.3.cloned.1.call-update
  88.6 0.0 collective-permute-done.1
  88.6 0.8 fusion.7
  89.4 0.0 collective-permute-done.pack_ref
  89.4 0.6 copy-done.12
  90.0 4.9 %route.3 = (bf16[1024,1024]{1,0:T(8,128)(2,1)}, bf16[3,1024,128]{2,1,0:T(8,128)(2,1)}) custom-call(f32[16,128]{1,0:T(8,128)} %copy-done.12, s32[1,64]{1,0:T(1,128)} %bitcast.29, s32[1,32]{1,0:T(1,128)} %bitcast.31, bf16[128,1024]{1,0:T(8,128)(2,1)} %get-tuple-element.55.tokens_ref, bf16[128,1024]{1,0:T(8,128)(2,1)} %get-tuple-element.54.cotangent_ref), custom_call_target="tpu_custom_call" | custom-call | tf_op jit(solution)/shard_map/route/pallas_call | solution.py:98
  95.0 0.0 all-to-all-done.arrived_ref.one_ref
  95.0 0.0 copy-start.4
  95.0 1.4 copy-done
  96.3 5.8 %all-to-all-start.1 = ((bf16[32,32,1024]{2,1,0:T(8,128)(2,1)}), bf16[32,32,1024]{2,1,0:T(8,128)(2,1)}, u32[]{:S(2)}, u32[]{:S(2)}) async-start(bf16[32,32,1024]{2,1,0:T(8,128)(2,1)} %bitcast.26), calls=%async_computation.1 | async-start | bytes 4194304 | tf_op jit(solution)/shard_map/all_to_all | solution.py:248
  102.1 7.3 %collective-permute-start.3 = (bf16[1,3,48,1024]{3,2,1,0:T(8,128)(2,1)}, bf16[1,3,48,1024]{3,2,1,0:T(8,128)(2,1)S(1)}, u32[]{:S(2)}, u32[]{:S(2)}) collective-permute-start(bf16[1,3,48,1024]{3,2,1,0:T(8,128)(2,1)} %convert_element_type.30), channel_id=1, source_target_pairs={{0,256},{8,264},{16,272},{24,280},{32,288},{40,296},{48,304},{56,3... | collective-permute-start | bytes 884744 | tf_op jit(solution)/shard_map/ppermute | solution.py:20
  109.4 0.0 copy-done.4
  109.4 0.8 convert_element_type.31
  110.2 11.4 %all-gather.3.cloned.1.call-done = bf16[1,3,384,1024]{3,2,1,0:T(8,128)(2,1)} async-done(((bf16[1,3,48,1024]{3,2,1,0:T(8,128)(2,1)}), bf16[1,3,384,1024]{3,2,1,0:T(8,128)(2,1)}) %all-gather.3.cloned.1.call-update) | async-done | bytes 2359312 | tf_op jit(solution)/shard_map/all_gather | solution.py:270
  121.6 7.0 %expert.2 = (bf16[32,32,1024]{2,1,0:T(8,128)(2,1)}, bf16[512,1152]{1,0:T(8,128)(2,1)}) custom-call(bf16[32,32,1024]{2,1,0:T(8,128)(2,1)} %copy-done, bf16[3,384,1024]{2,1,0:T(8,128)(2,1)} %bitcast.21), custom_call_target="tpu_custom_call" | custom-call | tf_op jit(solution)/shard_map/expert/pallas_call | solution.py:138
  128.7 32.1 %collective-permute-done.3 = bf16[1,3,48,1024]{3,2,1,0:T(8,128)(2,1)S(1)} collective-permute-done((bf16[1,3,48,1024]{3,2,1,0:T(8,128)(2,1)}, bf16[1,3,48,1024]{3,2,1,0:T(8,128)(2,1)S(1)}, u32[]{:S(2)}, u32[]{:S(2)}) %collective-permute-start.3) | collective-permute-done | bytes 294944 | tf_op jit(solution)/shard_map/ppermute | solution.py:20
  160.8 0.0 all-to-all-done.1.arrived_ref.two_ref
  160.8 7.1 %expert.3 = (bf16[32,32,1024]{2,1,0:T(8,128)(2,1)}, bf16[512,1152]{1,0:T(8,128)(2,1)}) custom-call(bf16[32,32,1024]{2,1,0:T(8,128)(2,1)} %all-to-all-done.1.arrived_ref.two_ref, bf16[3,384,1024]{2,1,0:T(8,128)(2,1)} %bitcast.22), custom_call_target="tpu_custom_call" | custom-call | tf_op jit(solution)/shard_map/expert/pallas_call | solution.py:138
  167.9 0.0 copy-done.8
  167.9 9.5 %all-to-all-start.2 = ((bf16[32,32,1024]{2,1,0:T(8,128)(2,1)}), bf16[32,32,1024]{2,1,0:T(8,128)(2,1)S(1)}, u32[]{:S(2)}, u32[]{:S(2)}) async-start(bf16[32,32,1024]{2,1,0:T(8,128)(2,1)} %get-tuple-element.39), calls=%async_computation.2 | async-start | bytes 4194304 | tf_op jit(solution)/shard_map/all_to_all | solution.py:248
  177.5 0.0 reduce-scatter.2.cloned.1.call-start
  177.5 6.9 %terms.1 = bf16[1152,1024]{1,0:T(8,128)(2,1)} custom-call(bf16[32,32,1024]{2,1,0:T(8,128)(2,1)} %copy-done, bf16[512,1152]{1,0:T(8,128)(2,1)} %get-tuple-element.48.one_act_ref, bf16[32,32,1024]{2,1,0:T(8,128)(2,1)} %all-to-all-done.1.arrived_ref.two_ref, bf16[512,1152]{1,0:T(8,128)(2,1)} %get-tuple-element.49.two_act_ref), custom_call_target="tpu_custom_call" | custom-call | tf_op jit(solution)/shard_map/terms/pallas_call | solution.py:177
  184.4 0.0 reduce-scatter.2.cloned.1.call-update
  184.5 7.3 %collective-permute-start.4 = (bf16[1,3,48,1024]{3,2,1,0:T(8,128)(2,1)}, bf16[1,3,48,1024]{3,2,1,0:T(8,128)(2,1)}, u32[]{:S(2)}, u32[]{:S(2)}) collective-permute-start(bf16[1,3,48,1024]{3,2,1,0:T(8,128)(2,1)} %convert_element_type.31), channel_id=1, source_target_pairs={{0,256},{8,264},{16,272},{24,280},{32,288},{40,296},{48,304},{56,3... | collective-permute-start | bytes 884744 | tf_op jit(solution)/shard_map/ppermute | solution.py:20
  191.8 47.8 %collective-permute-done.4 = bf16[1,3,48,1024]{3,2,1,0:T(8,128)(2,1)} collective-permute-done((bf16[1,3,48,1024]{3,2,1,0:T(8,128)(2,1)}, bf16[1,3,48,1024]{3,2,1,0:T(8,128)(2,1)}, u32[]{:S(2)}, u32[]{:S(2)}) %collective-permute-start.4) | collective-permute-done | bytes 294944 | tf_op jit(solution)/shard_map/ppermute | solution.py:20
  239.5 0.0 all-to-all-done.2
  239.6 1.4 copy-done.1
  240.9 5.5 %all-to-all-start.3 = ((bf16[32,32,1024]{2,1,0:T(8,128)(2,1)}), bf16[32,32,1024]{2,1,0:T(8,128)(2,1)}, u32[]{:S(2)}, u32[]{:S(2)}) async-start(bf16[32,32,1024]{2,1,0:T(8,128)(2,1)} %get-tuple-element.41), calls=%async_computation.3 | async-start | bytes 4194304 | tf_op jit(solution)/shard_map/all_to_all | solution.py:248
  246.5 0.0 copy-start.2
  246.5 0.0 copy-start.9
  246.5 3.7 %share.1 = bf16[256,1024]{1,0:T(8,128)(2,1)} custom-call(bf16[1024,1024]{1,0:T(8,128)(2,1)} %bitcast.24, bf16[3,1024,128]{2,1,0:T(8,128)(2,1)} %get-tuple-element.44.mats_ref), custom_call_target="tpu_custom_call" | custom-call | tf_op jit(solution)/shard_map/share/pallas_call | solution.py:194
  250.2 1.9 collective-permute-start.5
  252.1 0.0 reduce-scatter.2.cloned.1.call-done
  252.1 0.0 copy-done.2
  252.1 0.0 copy-done.9
  252.1 2.5 subtract_convert_fusion
  254.6 24.3 %collective-permute-done.5.share_ref = bf16[256,1024]{1,0:T(8,128)(2,1)S(1)} collective-permute-done((bf16[256,1024]{1,0:T(8,128)(2,1)}, bf16[256,1024]{1,0:T(8,128)(2,1)S(1)}, u32[]{:S(2)}, u32[]{:S(2)}) %collective-permute-start.5) | collective-permute-done | bytes 524320 | tf_op jit(solution)/shard_map/ppermute | solution.py:20
  278.9 16.7 %all-to-all-done.3 = bf16[32,32,1024]{2,1,0:T(8,128)(2,1)} async-done(((bf16[32,32,1024]{2,1,0:T(8,128)(2,1)}), bf16[32,32,1024]{2,1,0:T(8,128)(2,1)}, u32[]{:S(2)}, u32[]{:S(2)}) %all-to-all-start.3) | async-done | bytes 2097184 | tf_op jit(solution)/shard_map/all_to_all | solution.py:248
  295.6 0.0 copy-done.7
  295.6 3.6 %combine.1 = (bf16[128,1024]{1,0:T(8,128)(2,1)}, bf16[128,1024]{1,0:T(8,128)(2,1)}) custom-call(bf16[1024,1024]{1,0:T(8,128)(2,1)} %bitcast.7.back_ref, bf16[3,1024,128]{2,1,0:T(8,128)(2,1)} %get-tuple-element.42.mats_ref, bf16[256,1024]{1,0:T(8,128)(2,1)} %copy-done.7), custom_call_target="tpu_custom_call" | custom-call | tf_op jit(solution)/shard_map/combine/pallas_call | solution.py:213
  (6 shorter events, 0.0 us)
Async XLA Ops:
  14.1 10.5 %copy-start.10 = (bf16[1,3,48,1024]{3,2,1,0:T(8,128)(2,1)S(1)}, bf16[1,3,48,1024]{3,2,1,0:T(8,128)(2,1)}, u32[]{:S(2)}) copy-start(bf16[1,3,48,1024]{3,2,1,0:T(8,128)(2,1)} %param.15) | copy-start | bytes 884740
  14.1 17.8 %copy-start.5 = (bf16[128,1024]{1,0:T(8,128)(2,1)S(1)}, bf16[128,1024]{1,0:T(8,128)(2,1)}, u32[]{:S(2)}) copy-start(bf16[128,1024]{1,0:T(8,128)(2,1)} %tokens_ref.1) | copy-start | bytes 786436
  14.1 17.8 %copy-start.6 = (bf16[128,1024]{1,0:T(8,128)(2,1)S(1)}, bf16[128,1024]{1,0:T(8,128)(2,1)}, u32[]{:S(2)}) copy-start(bf16[128,1024]{1,0:T(8,128)(2,1)} %cotangent_ref.1) | copy-start | bytes 786436
  14.1 20.6 %copy-start.11 = (f32[16,128]{1,0:T(8,128)S(1)}, f32[16,128]{1,0:T(8,128)}, u32[]{:S(2)}) copy-start(f32[16,128]{1,0:T(8,128)} %pad_maximum_fusion.1.pack_ref) | copy-start | bytes 24580
  14.1 28.4 %copy-start.3 = (f32[1,3,48,1024]{3,2,1,0:T(8,128)S(1)}, f32[1,3,48,1024]{3,2,1,0:T(8,128)}, u32[]{:S(2)}) copy-start(f32[1,3,48,1024]{3,2,1,0:T(8,128)} %param.16) | copy-start | bytes 1769476
  14.1 29.2 %copy-start.13 = (s32[32]{0:T(128)S(1)}, s32[32]{0:T(128)}, u32[]{:S(2)}) copy-start(s32[32]{0:T(128)} %param.14) | copy-start | bytes 388
  14.1 80.8 %all-to-all-start = ((bf16[32,32,1024]{2,1,0:T(8,128)(2,1)}), bf16[32,32,1024]{2,1,0:T(8,128)(2,1)S(1)}, u32[]{:S(2)}, u32[]{:S(2)}) async-start(bf16[32,32,1024]{2,1,0:T(8,128)(2,1)} %bitcast.25), calls=%async_computation | async-start | bytes 4194304 | tf_op jit(solution)/shard_map/all_to_all | solution.py:248
  24.5 97.1 %all-gather.3.cloned.1.call-start = ((), (), s32[]{:S(2)}) async-start(), calls=%async_computation.6 | async-start | bytes 2654208 | tf_op jit(solution)/shard_map/all_gather | solution.py:270
  24.6 63.2 %collective-permute-start.2 = (bf16[1,3,48,1024]{3,2,1,0:T(8,128)(2,1)S(1)}, bf16[1,3,48,1024]{3,2,1,0:T(8,128)(2,1)}, u32[]{:S(2)}, u32[]{:S(2)}) collective-permute-start(bf16[1,3,48,1024]{3,2,1,0:T(8,128)(2,1)S(1)} %copy-done.10), channel_id=1, source_target_pairs={{0,256},{8,264},{16,272},{24,280},{32,288},{40,296},{48,304},{56,3... | collective-permute-start | bytes 884744 | tf_op jit(solution)/shard_map/ppermute | solution.py:20
  32.7 55.9 %collective-permute-start.1 = (bf16[256,1024]{1,0:T(8,128)(2,1)}, bf16[256,1024]{1,0:T(8,128)(2,1)S(1)}, u32[]{:S(2)}, u32[]{:S(2)}) collective-permute-start(bf16[256,1024]{1,0:T(8,128)(2,1)} %pad_maximum_fusion), channel_id=1, source_target_pairs={{0,32},{8,40},{16,48},{24,56},{32,0},{40,8},{48,16},{56,24},{64,96... | collective-permute-start | bytes 1572872 | tf_op jit(solution)/shard_map/ppermute | solution.py:20
  34.7 54.8 %collective-permute-start = (f32[16,128]{1,0:T(8,128)S(1)}, f32[16,128]{1,0:T(8,128)S(1)}, u32[]{:S(2)}, u32[]{:S(2)}) collective-permute-start(f32[16,128]{1,0:T(8,128)S(1)} %copy-done.11), channel_id=1, source_target_pairs={{0,32},{8,40},{16,48},{24,56},{32,0},{40,8},{48,16},{56,24},{64,96... | collective-permute-start | bytes 24584 | tf_op jit(solution)/shard_map/ppermute | solution.py:20
  89.4 0.6 copy-start.12
  95.0 1.4 copy-start
  95.0 14.5 %copy-start.4 = (f32[1,3,48,1024]{3,2,1,0:T(8,128)S(1)}, f32[1,3,48,1024]{3,2,1,0:T(8,128)}, u32[]{:S(2)}) copy-start(f32[1,3,48,1024]{3,2,1,0:T(8,128)} %param.17) | copy-start | bytes 1769476
  96.3 64.4 %all-to-all-start.1 = ((bf16[32,32,1024]{2,1,0:T(8,128)(2,1)}), bf16[32,32,1024]{2,1,0:T(8,128)(2,1)}, u32[]{:S(2)}, u32[]{:S(2)}) async-start(bf16[32,32,1024]{2,1,0:T(8,128)(2,1)} %bitcast.26), calls=%async_computation.1 | async-start | bytes 4194304 | tf_op jit(solution)/shard_map/all_to_all | solution.py:248
  102.1 58.6 %collective-permute-start.3 = (bf16[1,3,48,1024]{3,2,1,0:T(8,128)(2,1)}, bf16[1,3,48,1024]{3,2,1,0:T(8,128)(2,1)S(1)}, u32[]{:S(2)}, u32[]{:S(2)}) collective-permute-start(bf16[1,3,48,1024]{3,2,1,0:T(8,128)(2,1)} %convert_element_type.30), channel_id=1, source_target_pairs={{0,256},{8,264},{16,272},{24,280},{32,288},{40,296},{48,304},{56,3... | collective-permute-start | bytes 884744 | tf_op jit(solution)/shard_map/ppermute | solution.py:20
  160.8 7.1 %copy-start.8 = (bf16[1,3,48,1024]{3,2,1,0:T(8,128)(2,1)}, bf16[1,3,48,1024]{3,2,1,0:T(8,128)(2,1)S(1)}, u32[]{:S(2)}) copy-start(bf16[1,3,48,1024]{3,2,1,0:T(8,128)(2,1)S(1)} %collective-permute-done.3) | copy-start | bytes 884740
  167.9 71.6 %all-to-all-start.2 = ((bf16[32,32,1024]{2,1,0:T(8,128)(2,1)}), bf16[32,32,1024]{2,1,0:T(8,128)(2,1)S(1)}, u32[]{:S(2)}, u32[]{:S(2)}) async-start(bf16[32,32,1024]{2,1,0:T(8,128)(2,1)} %get-tuple-element.39), calls=%async_computation.2 | async-start | bytes 4194304 | tf_op jit(solution)/shard_map/all_to_all | solution.py:248
  177.5 74.6 %reduce-scatter.2.cloned.1.call-start = ((), (), s32[]{:S(2)}) async-start(), calls=%async_computation.5 | async-start | bytes 2654208 | tf_op jit(solution)/shard_map/reduce_scatter | solution.py:286
  184.5 55.1 %collective-permute-start.4 = (bf16[1,3,48,1024]{3,2,1,0:T(8,128)(2,1)}, bf16[1,3,48,1024]{3,2,1,0:T(8,128)(2,1)}, u32[]{:S(2)}, u32[]{:S(2)}) collective-permute-start(bf16[1,3,48,1024]{3,2,1,0:T(8,128)(2,1)} %convert_element_type.31), channel_id=1, source_target_pairs={{0,256},{8,264},{16,272},{24,280},{32,288},{40,296},{48,304},{56,3... | collective-permute-start | bytes 884744 | tf_op jit(solution)/shard_map/ppermute | solution.py:20
  239.5 1.4 copy-start.1
  240.9 54.7 %all-to-all-start.3 = ((bf16[32,32,1024]{2,1,0:T(8,128)(2,1)}), bf16[32,32,1024]{2,1,0:T(8,128)(2,1)}, u32[]{:S(2)}, u32[]{:S(2)}) async-start(bf16[32,32,1024]{2,1,0:T(8,128)(2,1)} %get-tuple-element.41), calls=%async_computation.3 | async-start | bytes 4194304 | tf_op jit(solution)/shard_map/all_to_all | solution.py:248
  246.5 5.6 %copy-start.2 = (bf16[1,3,48,1024]{3,2,1,0:T(8,128)(2,1)S(1)}, bf16[1,3,48,1024]{3,2,1,0:T(8,128)(2,1)}, u32[]{:S(2)}) copy-start(bf16[1,3,48,1024]{3,2,1,0:T(8,128)(2,1)} %broadcast_select_fusion) | copy-start | bytes 884740
  246.5 5.6 %copy-start.9 = (bf16[1,3,48,1024]{3,2,1,0:T(8,128)(2,1)S(1)}, bf16[1,3,48,1024]{3,2,1,0:T(8,128)(2,1)}, u32[]{:S(2)}) copy-start(bf16[1,3,48,1024]{3,2,1,0:T(8,128)(2,1)} %copy-done.8) | copy-start | bytes 884740
  250.2 28.8 %collective-permute-start.5 = (bf16[256,1024]{1,0:T(8,128)(2,1)}, bf16[256,1024]{1,0:T(8,128)(2,1)S(1)}, u32[]{:S(2)}, u32[]{:S(2)}) collective-permute-start(bf16[256,1024]{1,0:T(8,128)(2,1)} %share.1), channel_id=1, source_target_pairs={{0,32},{8,40},{16,48},{24,56},{32,0},{40,8},{48,16},{56,24},{64,96... | collective-permute-start | bytes 1572872 | tf_op jit(solution)/shard_map/ppermute | solution.py:20
  278.9 16.7 %copy-start.7 = (bf16[256,1024]{1,0:T(8,128)(2,1)}, bf16[256,1024]{1,0:T(8,128)(2,1)S(1)}, u32[]{:S(2)}) copy-start(bf16[256,1024]{1,0:T(8,128)(2,1)S(1)} %collective-permute-done.5.share_ref) | copy-start | bytes 1572868
Sparse Core Ops, SparseCore 0:
  88.7 32.8 all-gather.2
  184.6 38.9 reduce-scatter.1

commit v3 on v2

--- a/solution.py
+++ b/solution.py
@@ -13,7 +13,12 @@
 
 X_SIZE = 4
 VMEM_LIMIT = 60 * 1024 * 1024
+COST = {"route_own": 30, "route_other": 30, "expert_own": 100, "expert_other": 10, "terms": 30, "share": 10, "combine": 10}
 PARAMS = pltpu.CompilerParams(vmem_limit_bytes=VMEM_LIMIT)
+
+
+def cost(name):
+    return pl.CostEstimate(flops=COST[name] * 10**9, bytes_accessed=0, transcendentals=0)
 
 
 def partner(array, apart):
@@ -92,7 +97,7 @@
     ).astype(jnp.bfloat16)
 
 
-def route(pack, home, flags, tokens, cotangent):
+def route(pack, home, flags, tokens, cotangent, name):
     tok_rows, model_width = tokens.shape
     rows = tok_rows * (pack.shape[0] // 2)
     return pl.pallas_call(
@@ -102,7 +107,8 @@
             jax.ShapeDtypeStruct((3, rows, tok_rows), jnp.bfloat16),
         ),
         compiler_params=PARAMS,
-        name="route",
+        cost_estimate=cost(name),
+        name=name,
     )(pack, home, flags, tokens, cotangent)
 
 
@@ -130,7 +136,7 @@
     act_ref[:, 2 * hidden_width :] = hidden
 
 
-def expert(arrived, weights, steps):
+def expert(arrived, weights, steps, name):
     sources, double, width = arrived.shape
     hidden_width = weights.shape[1]
     block = sources // steps
@@ -151,7 +157,8 @@
             jax.ShapeDtypeStruct((rows * steps, 3 * hidden_width), jnp.bfloat16),
         ),
         compiler_params=PARAMS,
-        name="expert",
+        cost_estimate=cost(name),
+        name=name,
     )(arrived, weights)
 
 
@@ -178,6 +185,7 @@
         terms_kernel,
         out_shape=jax.ShapeDtypeStruct((one_act.shape[1], one.shape[2]), jnp.bfloat16),
         compiler_params=PARAMS,
+        cost_estimate=cost("terms"),
         name="terms",
     )(one, one_act, two, two_act)
 
@@ -195,6 +203,7 @@
         share_kernel,
         out_shape=jax.ShapeDtypeStruct((2 * mats.shape[2], back.shape[1]), jnp.bfloat16),
         compiler_params=PARAMS,
+        cost_estimate=cost("share"),
         name="share",
     )(back, mats)
 
@@ -214,6 +223,7 @@
         combine_kernel,
         out_shape=(shape, shape),
         compiler_params=PARAMS,
+        cost_estimate=cost("combine"),
         name="combine",
     )(back, mats, other_share)
 
@@ -252,13 +262,15 @@
     home = old_home.reshape(1, -1)
     flags = swap_flags.reshape(1, -1)
     pack = jnp.concatenate([routes.T.astype(jnp.float32), gates.T], axis=0)
-    own_send, own_mats = route(pack, home, flags, tokens, cotangent)
+    own_send, own_mats = route(pack, home, flags, tokens, cotangent, "route_own")
     own_arrived = exchange(own_send)
+    weights = jnp.where(is_swapped, partner(weights, half), weights)
+    gathered = lax.all_gather(weights[0], "tp", axis=1, tiled=True)
     both = jnp.concatenate([tokens, cotangent], axis=0)
-    pack, both, _ = lax.optimization_barrier((pack, both, own_send))
+    pack, both, _, _ = lax.optimization_barrier((pack, both, own_send, weights))
     other_pack, both = partner(pack, X_SIZE), partner(both, X_SIZE)
     tok_rows = tokens.shape[0]
-    other_send, other_mats = route(other_pack, home, flags, both[:tok_rows], both[tok_rows:])
+    other_send, other_mats = route(other_pack, home, flags, both[:tok_rows], both[tok_rows:], "route_other")
     first_sent, second_sent = first_moment.astype(jnp.bfloat16), second_moment.astype(jnp.bfloat16)
     other_send, own_arrived, first_sent = lax.optimization_barrier(
         (other_send, own_arrived, first_sent)
@@ -266,18 +278,16 @@
     other_first = partner(first_sent, half)
     other_arrived = exchange(other_send)
 
-    weights = jnp.where(is_swapped, partner(weights, half), weights)
-    gathered = lax.all_gather(weights[0], "tp", axis=1, tiled=True)
-    own_back, own_act = expert(own_arrived, gathered, 2)
-    other_arrived, own_back, own_act, other_first, second_sent = lax.optimization_barrier(
-        (other_arrived, own_back, own_act, other_first, second_sent)
+    own_arrived, other_first = lax.optimization_barrier((own_arrived, other_first))
+    own_back, own_act = expert(own_arrived, gathered, 2, "expert_own")
+    other_arrived, own_back, own_act, second_sent = lax.optimization_barrier(
+        (other_arrived, own_back, own_act, second_sent)
     )
     other_second = partner(second_sent, half)
-    other_back, other_act = expert(other_arrived, gathered, 2)
+    other_back, other_act = expert(other_arrived, gathered, 2, "expert_other")
     other_returned = exchange(other_back)
-    own_back, other_returned, other_second = lax.optimization_barrier(
-        (own_back, other_returned, other_second)
-    )
+    other_act, other_second = lax.optimization_barrier((other_act, other_second))
+    own_back, other_returned = lax.optimization_barrier((own_back, other_returned))
     own_returned = exchange(own_back).reshape(-1, model_width)
     other_returned = other_returned.reshape(-1, model_width)
 

time: 307 us -> 282 us (0.919)
  the two profiles are of different devices: /device:TPU:386 before, /device:TPU:128 now
where the time goes in v3:
time: 282 us; the launch traced here: 281 us
  waiting for transfers between devices  154 us (55%)
  starting transfers between devices  62.7 us (22%)
  Pallas kernels  38.5 us (14%)
  between operations  15 us (5%)
  other arithmetic  7.53 us (3%)
  local copies, waits for them, and re-layouts  2.88 us (1%)
    all_to_all x4, waiting for transfers between devices, exchange(): lax.all_to_all(rows, 'ep', split_axis=0, concat_axis=0, tiled=True, axis_...  97.3 us
    ppermute x6, waiting for transfers between devices, partner(): lax.ppermute(array, 'ep', [(i, i ^ apart) for i in range(lax.axis_size('e...  57.1 us
    ppermute x6, starting transfers between devices, partner(): lax.ppermute(array, 'ep', [(i, i ^ apart) for i in range(lax.axis_size('e...  39.1 us
    all_to_all x4, starting transfers between devices, exchange(): lax.all_to_all(rows, 'ep', split_axis=0, concat_axis=0, tiled=True, axis_...  23.5 us
    pallas_call x2, Pallas kernels, expert(): pl.pallas_call(expert_kernel, grid=(steps,), in_specs=[pl.BlockSpec((bloc...  14.2 us
    pallas_call x2, Pallas kernels, route(): pl.pallas_call(route_kernel, out_shape=(jax.ShapeDtypeStruct((rows, model...  9.95 us
    pallas_call x1, Pallas kernels, gradient_terms(): pl.pallas_call(terms_kernel, out_shape=jax.ShapeDtypeStruct((one_act.shap...  6.93 us
  transfers between devices with their start and end apart: 12, of which 7 were waited for; matrix products, arithmetic and copies ran while one was open for 3% of the time, Pallas kernels for 12%

profile of v3, /device:TPU:128, one launch (start us, length us, event | category | flops | bytes accessed | tf_op | source)
XLA Modules:
  0.0 280.9 jit_solution(2868939121983118964)
XLA Ops:
  7.2 7.7 %collective-permute-start = (bf16[1,3,48,1024]{3,2,1,0:T(8,128)(2,1)}, bf16[1,3,48,1024]{3,2,1,0:T(8,128)(2,1)S(1)}, u32[]{:S(2)}, u32[]{:S(2)}) collective-permute-start(bf16[1,3,48,1024]{3,2,1,0:T(8,128)(2,1)} %param.15), channel_id=1, source_target_pairs={{0,256},{8,264},{16,272},{24,280},{32,288},{40,296},{48,304},{56,3... | collective-permute-start | bytes 884744 | tf_op jit(solution)/shard_map/ppermute | solution.py:25
  14.9 0.7 convert_bitcast_fusion
  15.6 1.3 pad_maximum_fusion.1.pack_ref
  16.9 4.9 %route_own.1 = (bf16[1024,1024]{1,0:T(8,128)(2,1)}, bf16[3,1024,128]{2,1,0:T(8,128)(2,1)}) custom-call(f32[16,128]{1,0:T(8,128)} %pad_maximum_fusion.1.pack_ref, s32[1,64]{1,0:T(1,128)} %bitcast.28, s32[1,32]{1,0:T(1,128)} %bitcast.30, bf16[128,1024]{1,0:T(8,128)(2,1)} %tokens_ref.1, bf16[128,1024]{1,0:T(8,128)(2,1)} %cotangent_ref.1), custom_call_target="tpu_custom_call" | custom-call | flops 30000001024 | tf_op jit(solution)/shard_map/route_own/pallas_call | solution.py:103
  21.8 0.0 copy-start.9
  21.8 0.0 copy-start.11
  21.8 5.2 %all-to-all-start = ((bf16[32,32,1024]{2,1,0:T(8,128)(2,1)}), bf16[32,32,1024]{2,1,0:T(8,128)(2,1)S(1)}, u32[]{:S(2)}, u32[]{:S(2)}) async-start(bf16[32,32,1024]{2,1,0:T(8,128)(2,1)} %bitcast.22), calls=%async_computation | async-start | bytes 4194304 | tf_op jit(solution)/shard_map/all_to_all | solution.py:258
  27.0 0.0 copy-start.1
  27.0 0.0 copy-start.12
  27.0 0.0 all-gather.3.cloned.1.call-start
  27.1 0.0 copy-done.15
  27.1 0.6 fusion.4
  28.4 0.0 collective-permute-done
  28.4 0.0 copy-done.9
  28.4 0.7 broadcast_select_fusion
  29.2 0.0 all-gather.3.cloned.1.call-update
  29.2 0.0 copy-done.11
  29.2 1.0 pad_maximum_fusion
  30.2 9.1 %collective-permute-start.2 = (bf16[256,1024]{1,0:T(8,128)(2,1)S(1)}, bf16[256,1024]{1,0:T(8,128)(2,1)S(1)}, u32[]{:S(2)}, u32[]{:S(2)}) collective-permute-start(bf16[256,1024]{1,0:T(8,128)(2,1)S(1)} %pad_maximum_fusion), channel_id=1, source_target_pairs={{0,32},{8,40},{16,48},{24,56},{32,0},{40,8},{48,16},{56,24},{64,96... | collective-permute-start | bytes 1572872 | tf_op jit(solution)/shard_map/ppermute | solution.py:25
  39.3 0.0 copy-done.1
  39.4 0.0 copy-done.12
  39.4 1.9 collective-permute-start.1
  41.3 30.1 %collective-permute-done.2 = bf16[256,1024]{1,0:T(8,128)(2,1)S(1)} collective-permute-done((bf16[256,1024]{1,0:T(8,128)(2,1)S(1)}, bf16[256,1024]{1,0:T(8,128)(2,1)S(1)}, u32[]{:S(2)}, u32[]{:S(2)}) %collective-permute-start.2) | collective-permute-done | bytes 524320 | tf_op jit(solution)/shard_map/ppermute | solution.py:25
  71.4 0.8 fusion.7
  72.2 0.0 collective-permute-done.1.pack_ref
  72.2 0.6 copy-done.14
  72.8 5.0 %route_other.1 = (bf16[1024,1024]{1,0:T(8,128)(2,1)}, bf16[3,1024,128]{2,1,0:T(8,128)(2,1)}) custom-call(f32[16,128]{1,0:T(8,128)} %copy-done.14, s32[1,64]{1,0:T(1,128)} %bitcast.29, s32[1,32]{1,0:T(1,128)} %bitcast.31, bf16[128,1024]{1,0:T(8,128)(2,1)} %get-tuple-element.59.tokens_ref, bf16[128,1024]{1,0:T(8,128)(2,1)} %get-tuple-element.58.cotangent_ref), custom_call_target="tpu_custom_call" | custom-call | flops 30000001024 | tf_op jit(solution)/shard_map/route_other/pallas_call | solution.py:103
  77.8 0.0 all-to-all-done.arrived_ref.one_ref
  77.8 7.6 %collective-permute-start.3 = (bf16[1,3,48,1024]{3,2,1,0:T(8,128)(2,1)S(1)}, bf16[1,3,48,1024]{3,2,1,0:T(8,128)(2,1)S(1)}, u32[]{:S(2)}, u32[]{:S(2)}) collective-permute-start(bf16[1,3,48,1024]{3,2,1,0:T(8,128)(2,1)S(1)} %convert_element_type.30), channel_id=1, source_target_pairs={{0,256},{8,264},{16,272},{24,280},{32,288},{40,296},{48,304},{56,3... | collective-permute-start | bytes 884744 | tf_op jit(solution)/shard_map/ppermute | solution.py:25
  85.4 0.0 copy-done.3
  85.4 0.8 convert_element_type.31
  86.2 0.0 copy-done.5
  86.2 6.4 %all-to-all-start.1 = ((bf16[32,32,1024]{2,1,0:T(8,128)(2,1)}), bf16[32,32,1024]{2,1,0:T(8,128)(2,1)}, u32[]{:S(2)}, u32[]{:S(2)}) async-start(bf16[32,32,1024]{2,1,0:T(8,128)(2,1)} %bitcast.24), calls=%async_computation.1 | async-start | bytes 4194304 | tf_op jit(solution)/shard_map/all_to_all | solution.py:258
  92.6 6.9 %collective-permute-done.3 = bf16[1,3,48,1024]{3,2,1,0:T(8,128)(2,1)S(1)} collective-permute-done((bf16[1,3,48,1024]{3,2,1,0:T(8,128)(2,1)S(1)}, bf16[1,3,48,1024]{3,2,1,0:T(8,128)(2,1)S(1)}, u32[]{:S(2)}, u32[]{:S(2)}) %collective-permute-start.3) | collective-permute-done | bytes 294944 | tf_op jit(solution)/shard_map/ppermute | solution.py:25
  99.5 7.2 %expert_own.1 = (bf16[32,32,1024]{2,1,0:T(8,128)(2,1)}, bf16[512,1152]{1,0:T(8,128)(2,1)}) custom-call(bf16[32,32,1024]{2,1,0:T(8,128)(2,1)} %copy-done.5, bf16[3,384,1024]{2,1,0:T(8,128)(2,1)} %bitcast.26), custom_call_target="tpu_custom_call" | custom-call | flops 99999997952 | tf_op jit(solution)/shard_map/expert_own/pallas_call | solution.py:144
  106.6 0.0 copy-done.7
  106.6 40.3 %all-to-all-done.1.arrived_ref.two_ref = bf16[32,32,1024]{2,1,0:T(8,128)(2,1)} async-done(((bf16[32,32,1024]{2,1,0:T(8,128)(2,1)}), bf16[32,32,1024]{2,1,0:T(8,128)(2,1)}, u32[]{:S(2)}, u32[]{:S(2)}) %all-to-all-start.1) | async-done | bytes 2097184 | tf_op jit(solution)/shard_map/all_to_all | solution.py:258
  147.0 0.0 copy-done.10
  147.0 4.3 %collective-permute-start.5 = (bf16[1,3,48,1024]{3,2,1,0:T(8,128)(2,1)S(1)}, bf16[1,3,48,1024]{3,2,1,0:T(8,128)(2,1)S(1)}, u32[]{:S(2)}, u32[]{:S(2)}) collective-permute-start(bf16[1,3,48,1024]{3,2,1,0:T(8,128)(2,1)S(1)} %copy-done.10), channel_id=1, source_target_pairs={{0,256},{8,264},{16,272},{24,280},{32,288},{40,296},{48,304},{56,3... | collective-permute-start | bytes 884744 | tf_op jit(solution)/shard_map/ppermute | solution.py:25
  151.2 7.1 %expert_other.1 = (bf16[32,32,1024]{2,1,0:T(8,128)(2,1)}, bf16[512,1152]{1,0:T(8,128)(2,1)}) custom-call(bf16[32,32,1024]{2,1,0:T(8,128)(2,1)} %all-to-all-done.1.arrived_ref.two_ref, bf16[3,384,1024]{2,1,0:T(8,128)(2,1)} %bitcast.27), custom_call_target="tpu_custom_call" | custom-call | flops 10000000000 | tf_op jit(solution)/shard_map/expert_other/pallas_call | solution.py:144
  158.3 5.7 %all-to-all-start.2 = ((bf16[32,32,1024]{2,1,0:T(8,128)(2,1)}), bf16[32,32,1024]{2,1,0:T(8,128)(2,1)S(1)}, u32[]{:S(2)}, u32[]{:S(2)}) async-start(bf16[32,32,1024]{2,1,0:T(8,128)(2,1)} %get-tuple-element.42), calls=%async_computation.2 | async-start | bytes 4194304 | tf_op jit(solution)/shard_map/all_to_all | solution.py:258
  163.9 0.0 reduce-scatter.2.cloned.1.call-start
  164.0 3.4 %collective-permute-done.5 = bf16[1,3,48,1024]{3,2,1,0:T(8,128)(2,1)S(1)} collective-permute-done((bf16[1,3,48,1024]{3,2,1,0:T(8,128)(2,1)S(1)}, bf16[1,3,48,1024]{3,2,1,0:T(8,128)(2,1)S(1)}, u32[]{:S(2)}, u32[]{:S(2)}) %collective-permute-start.5) | collective-permute-done | bytes 294944 | tf_op jit(solution)/shard_map/ppermute | solution.py:25
  167.3 6.9 %terms.1 = bf16[1152,1024]{1,0:T(8,128)(2,1)} custom-call(bf16[32,32,1024]{2,1,0:T(8,128)(2,1)} %copy-done.5, bf16[512,1152]{1,0:T(8,128)(2,1)} %get-tuple-element.50.one_act_ref, bf16[32,32,1024]{2,1,0:T(8,128)(2,1)} %all-to-all-done.1.arrived_ref.two_ref, bf16[512,1152]{1,0:T(8,128)(2,1)} %get-tuple-element.53.two_act_ref), custom_call_target="tpu_custom_call" | custom-call | flops 30000001024 | tf_op jit(solution)/shard_map/terms/pallas_call | solution.py:184
  174.3 0.0 reduce-scatter.2.cloned.1.call-update
  174.3 39.5 %all-to-all-done.2 = bf16[32,32,1024]{2,1,0:T(8,128)(2,1)S(1)} async-done(((bf16[32,32,1024]{2,1,0:T(8,128)(2,1)}), bf16[32,32,1024]{2,1,0:T(8,128)(2,1)S(1)}, u32[]{:S(2)}, u32[]{:S(2)}) %all-to-all-start.2) | async-done | bytes 2097184 | tf_op jit(solution)/shard_map/all_to_all | solution.py:258
  213.8 1.4 copy-done.6
  215.2 6.3 %all-to-all-start.3 = ((bf16[32,32,1024]{2,1,0:T(8,128)(2,1)}), bf16[32,32,1024]{2,1,0:T(8,128)(2,1)}, u32[]{:S(2)}, u32[]{:S(2)}) async-start(bf16[32,32,1024]{2,1,0:T(8,128)(2,1)} %get-tuple-element.43), calls=%async_computation.3 | async-start | bytes 4194304 | tf_op jit(solution)/shard_map/all_to_all | solution.py:258
  221.5 0.0 copy-start
  221.5 0.0 copy-start.2
  221.5 0.0 copy-start.4
  221.5 0.0 copy-start.8
  221.5 3.7 %share.1 = bf16[256,1024]{1,0:T(8,128)(2,1)} custom-call(bf16[1024,1024]{1,0:T(8,128)(2,1)} %bitcast.23, bf16[3,1024,128]{2,1,0:T(8,128)(2,1)} %get-tuple-element.46.mats_ref), custom_call_target="tpu_custom_call" | custom-call | flops 10000000000 | tf_op jit(solution)/shard_map/share/pallas_call | solution.py:202
  225.2 8.5 %collective-permute-start.4 = (bf16[256,1024]{1,0:T(8,128)(2,1)}, bf16[256,1024]{1,0:T(8,128)(2,1)S(1)}, u32[]{:S(2)}, u32[]{:S(2)}) collective-permute-start(bf16[256,1024]{1,0:T(8,128)(2,1)} %share.1), channel_id=1, source_target_pairs={{0,32},{8,40},{16,48},{24,56},{32,0},{40,8},{48,16},{56,24},{64,96... | collective-permute-start | bytes 1572872 | tf_op jit(solution)/shard_map/ppermute | solution.py:25
  233.7 0.0 reduce-scatter.2.cloned.1.call-done
  233.7 0.0 copy-done
  233.8 0.0 copy-done.2
  233.8 0.0 copy-done.4
  233.8 0.0 copy-done.8
  233.8 2.4 subtract_convert_fusion
  236.2 16.8 %collective-permute-done.4.share_ref = bf16[256,1024]{1,0:T(8,128)(2,1)S(1)} collective-permute-done((bf16[256,1024]{1,0:T(8,128)(2,1)}, bf16[256,1024]{1,0:T(8,128)(2,1)S(1)}, u32[]{:S(2)}, u32[]{:S(2)}) %collective-permute-start.4) | collective-permute-done | bytes 524320 | tf_op jit(solution)/shard_map/ppermute | solution.py:25
  253.0 17.4 %all-to-all-done.3 = bf16[32,32,1024]{2,1,0:T(8,128)(2,1)} async-done(((bf16[32,32,1024]{2,1,0:T(8,128)(2,1)}), bf16[32,32,1024]{2,1,0:T(8,128)(2,1)}, u32[]{:S(2)}, u32[]{:S(2)}) %all-to-all-start.3) | async-done | bytes 2097184 | tf_op jit(solution)/shard_map/all_to_all | solution.py:258
  270.4 0.0 copy-done.13
  270.4 3.6 %combine.1 = (bf16[128,1024]{1,0:T(8,128)(2,1)}, bf16[128,1024]{1,0:T(8,128)(2,1)}) custom-call(bf16[1024,1024]{1,0:T(8,128)(2,1)} %bitcast.7.back_ref, bf16[3,1024,128]{2,1,0:T(8,128)(2,1)} %get-tuple-element.44.mats_ref, bf16[256,1024]{1,0:T(8,128)(2,1)} %copy-done.13), custom_call_target="tpu_custom_call" | custom-call | flops 10000000000 | tf_op jit(solution)/shard_map/combine/pallas_call | solution.py:222
  (10 shorter events, 0.0 us)
Async XLA Ops:
  7.2 21.2 %collective-permute-start = (bf16[1,3,48,1024]{3,2,1,0:T(8,128)(2,1)}, bf16[1,3,48,1024]{3,2,1,0:T(8,128)(2,1)S(1)}, u32[]{:S(2)}, u32[]{:S(2)}) collective-permute-start(bf16[1,3,48,1024]{3,2,1,0:T(8,128)(2,1)} %param.15), channel_id=1, source_target_pairs={{0,256},{8,264},{16,272},{24,280},{32,288},{40,296},{48,304},{56,3... | collective-permute-start | bytes 884744 | tf_op jit(solution)/shard_map/ppermute | solution.py:25
  21.8 5.3 %copy-start.15 = (s32[32]{0:T(128)S(1)}, s32[32]{0:T(128)}, u32[]{:S(2)}) copy-start(s32[32]{0:T(128)} %param.14) | copy-start | bytes 388
  21.8 6.6 %copy-start.9 = (bf16[1,3,48,1024]{3,2,1,0:T(8,128)(2,1)S(1)}, bf16[1,3,48,1024]{3,2,1,0:T(8,128)(2,1)}, u32[]{:S(2)}) copy-start(bf16[1,3,48,1024]{3,2,1,0:T(8,128)(2,1)} %param.15) | copy-start | bytes 884740
  21.8 7.4 %copy-start.11 = (bf16[128,1024]{1,0:T(8,128)(2,1)S(1)}, bf16[128,1024]{1,0:T(8,128)(2,1)}, u32[]{:S(2)}) copy-start(bf16[128,1024]{1,0:T(8,128)(2,1)} %tokens_ref.1) | copy-start | bytes 786436
  21.8 56.0 %all-to-all-start = ((bf16[32,32,1024]{2,1,0:T(8,128)(2,1)}), bf16[32,32,1024]{2,1,0:T(8,128)(2,1)S(1)}, u32[]{:S(2)}, u32[]{:S(2)}) async-start(bf16[32,32,1024]{2,1,0:T(8,128)(2,1)} %bitcast.22), calls=%async_computation | async-start | bytes 4194304 | tf_op jit(solution)/shard_map/all_to_all | solution.py:258
  27.0 12.3 %copy-start.1 = (f32[1,3,48,1024]{3,2,1,0:T(8,128)S(1)}, f32[1,3,48,1024]{3,2,1,0:T(8,128)}, u32[]{:S(2)}) copy-start(f32[1,3,48,1024]{3,2,1,0:T(8,128)} %param.16) | copy-start | bytes 1769476
  27.0 12.3 %copy-start.12 = (f32[16,128]{1,0:T(8,128)S(1)}, f32[16,128]{1,0:T(8,128)}, u32[]{:S(2)}) copy-start(f32[16,128]{1,0:T(8,128)} %pad_maximum_fusion.1.pack_ref) | copy-start | bytes 24580
  27.0 72.4 %all-gather.3.cloned.1.call-start = ((), (), s32[]{:S(2)}) async-start(), calls=%async_computation.6 | async-start | bytes 2654208 | tf_op jit(solution)/shard_map/all_gather | solution.py:268
  30.2 41.2 %collective-permute-start.2 = (bf16[256,1024]{1,0:T(8,128)(2,1)S(1)}, bf16[256,1024]{1,0:T(8,128)(2,1)S(1)}, u32[]{:S(2)}, u32[]{:S(2)}) collective-permute-start(bf16[256,1024]{1,0:T(8,128)(2,1)S(1)} %pad_maximum_fusion), channel_id=1, source_target_pairs={{0,32},{8,40},{16,48},{24,56},{32,0},{40,8},{48,16},{56,24},{64,96... | collective-permute-start | bytes 1572872 | tf_op jit(solution)/shard_map/ppermute | solution.py:25
  39.4 32.8 %collective-permute-start.1 = (f32[16,128]{1,0:T(8,128)S(1)}, f32[16,128]{1,0:T(8,128)S(1)}, u32[]{:S(2)}, u32[]{:S(2)}) collective-permute-start(f32[16,128]{1,0:T(8,128)S(1)} %copy-done.12), channel_id=1, source_target_pairs={{0,32},{8,40},{16,48},{24,56},{32,0},{40,8},{48,16},{56,24},{64,96... | collective-permute-start | bytes 24584 | tf_op jit(solution)/shard_map/ppermute | solution.py:25
  72.2 0.6 copy-start.14
  72.8 12.6 %copy-start.3 = (f32[1,3,48,1024]{3,2,1,0:T(8,128)S(1)}, f32[1,3,48,1024]{3,2,1,0:T(8,128)}, u32[]{:S(2)}) copy-start(f32[1,3,48,1024]{3,2,1,0:T(8,128)} %param.17) | copy-start | bytes 1769476
  77.8 8.4 %copy-start.5 = (bf16[32,32,1024]{2,1,0:T(8,128)(2,1)}, bf16[32,32,1024]{2,1,0:T(8,128)(2,1)S(1)}, u32[]{:S(2)}) copy-start(bf16[32,32,1024]{2,1,0:T(8,128)(2,1)S(1)} %all-to-all-done.arrived_ref.one_ref) | copy-start | bytes 6291460
  77.8 21.6 %collective-permute-start.3 = (bf16[1,3,48,1024]{3,2,1,0:T(8,128)(2,1)S(1)}, bf16[1,3,48,1024]{3,2,1,0:T(8,128)(2,1)S(1)}, u32[]{:S(2)}, u32[]{:S(2)}) collective-permute-start(bf16[1,3,48,1024]{3,2,1,0:T(8,128)(2,1)S(1)} %convert_element_type.30), channel_id=1, source_target_pairs={{0,256},{8,264},{16,272},{24,280},{32,288},{40,296},{48,304},{56,3... | collective-permute-start | bytes 884744 | tf_op jit(solution)/shard_map/ppermute | solution.py:25
  86.2 60.8 %all-to-all-start.1 = ((bf16[32,32,1024]{2,1,0:T(8,128)(2,1)}), bf16[32,32,1024]{2,1,0:T(8,128)(2,1)}, u32[]{:S(2)}, u32[]{:S(2)}) async-start(bf16[32,32,1024]{2,1,0:T(8,128)(2,1)} %bitcast.24), calls=%async_computation.1 | async-start | bytes 4194304 | tf_op jit(solution)/shard_map/all_to_all | solution.py:258
  99.5 7.2 %copy-start.7 = (bf16[1,3,48,1024]{3,2,1,0:T(8,128)(2,1)}, bf16[1,3,48,1024]{3,2,1,0:T(8,128)(2,1)S(1)}, u32[]{:S(2)}) copy-start(bf16[1,3,48,1024]{3,2,1,0:T(8,128)(2,1)S(1)} %collective-permute-done.3) | copy-start | bytes 884740
  99.5 47.5 %copy-start.10 = (bf16[1,3,48,1024]{3,2,1,0:T(8,128)(2,1)S(1)}, bf16[1,3,48,1024]{3,2,1,0:T(8,128)(2,1)}, u32[]{:S(2)}) copy-start(bf16[1,3,48,1024]{3,2,1,0:T(8,128)(2,1)} %convert_element_type.31) | copy-start | bytes 884740
  147.0 20.4 %collective-permute-start.5 = (bf16[1,3,48,1024]{3,2,1,0:T(8,128)(2,1)S(1)}, bf16[1,3,48,1024]{3,2,1,0:T(8,128)(2,1)S(1)}, u32[]{:S(2)}, u32[]{:S(2)}) collective-permute-start(bf16[1,3,48,1024]{3,2,1,0:T(8,128)(2,1)S(1)} %copy-done.10), channel_id=1, source_target_pairs={{0,256},{8,264},{16,272},{24,280},{32,288},{40,296},{48,304},{56,3... | collective-permute-start | bytes 884744 | tf_op jit(solution)/shard_map/ppermute | solution.py:25
  158.3 55.5 %all-to-all-start.2 = ((bf16[32,32,1024]{2,1,0:T(8,128)(2,1)}), bf16[32,32,1024]{2,1,0:T(8,128)(2,1)S(1)}, u32[]{:S(2)}, u32[]{:S(2)}) async-start(bf16[32,32,1024]{2,1,0:T(8,128)(2,1)} %get-tuple-element.42), calls=%async_computation.2 | async-start | bytes 4194304 | tf_op jit(solution)/shard_map/all_to_all | solution.py:258
  163.9 69.8 %reduce-scatter.2.cloned.1.call-start = ((), (), s32[]{:S(2)}) async-start(), calls=%async_computation.5 | async-start | bytes 2654208 | tf_op jit(solution)/shard_map/reduce_scatter | solution.py:296
  213.8 1.4 copy-start.6
  215.2 55.2 %all-to-all-start.3 = ((bf16[32,32,1024]{2,1,0:T(8,128)(2,1)}), bf16[32,32,1024]{2,1,0:T(8,128)(2,1)}, u32[]{:S(2)}, u32[]{:S(2)}) async-start(bf16[32,32,1024]{2,1,0:T(8,128)(2,1)} %get-tuple-element.43), calls=%async_computation.3 | async-start | bytes 4194304 | tf_op jit(solution)/shard_map/all_to_all | solution.py:258
  221.5 12.3 %copy-start = (bf16[1,3,48,1024]{3,2,1,0:T(8,128)(2,1)S(1)}, bf16[1,3,48,1024]{3,2,1,0:T(8,128)(2,1)}, u32[]{:S(2)}) copy-start(bf16[1,3,48,1024]{3,2,1,0:T(8,128)(2,1)} %broadcast_select_fusion) | copy-start | bytes 884740
  221.5 12.3 %copy-start.2 = (f32[1,3,48,1024]{3,2,1,0:T(8,128)S(1)}, f32[1,3,48,1024]{3,2,1,0:T(8,128)}, u32[]{:S(2)}) copy-start(f32[1,3,48,1024]{3,2,1,0:T(8,128)} %param.16) | copy-start | bytes 1769476
  221.5 12.3 %copy-start.4 = (f32[1,3,48,1024]{3,2,1,0:T(8,128)S(1)}, f32[1,3,48,1024]{3,2,1,0:T(8,128)}, u32[]{:S(2)}) copy-start(f32[1,3,48,1024]{3,2,1,0:T(8,128)} %param.17) | copy-start | bytes 1769476
  221.5 12.3 %copy-start.8 = (bf16[1,3,48,1024]{3,2,1,0:T(8,128)(2,1)S(1)}, bf16[1,3,48,1024]{3,2,1,0:T(8,128)(2,1)}, u32[]{:S(2)}) copy-start(bf16[1,3,48,1024]{3,2,1,0:T(8,128)(2,1)} %copy-done.7) | copy-start | bytes 884740
  225.2 27.7 %collective-permute-start.4 = (bf16[256,1024]{1,0:T(8,128)(2,1)}, bf16[256,1024]{1,0:T(8,128)(2,1)S(1)}, u32[]{:S(2)}, u32[]{:S(2)}) collective-permute-start(bf16[256,1024]{1,0:T(8,128)(2,1)} %share.1), channel_id=1, source_target_pairs={{0,32},{8,40},{16,48},{24,56},{32,0},{40,8},{48,16},{56,24},{64,96... | collective-permute-start | bytes 1572872 | tf_op jit(solution)/shard_map/ppermute | solution.py:25
  253.0 17.4 %copy-start.13 = (bf16[256,1024]{1,0:T(8,128)(2,1)}, bf16[256,1024]{1,0:T(8,128)(2,1)S(1)}, u32[]{:S(2)}) copy-start(bf16[256,1024]{1,0:T(8,128)(2,1)S(1)} %collective-permute-done.4.share_ref) | copy-start | bytes 1572868
Sparse Core Ops, SparseCore 0:
  30.5 54.0 all-gather.2
  174.4 37.4 reduce-scatter.1

commit v4 on v3

v4 whole, which is shorter than its diff:
```python
import jax
import jax.numpy as jnp
from jax import lax
from jax.experimental import pallas as pl
from jax.experimental.pallas import tpu as pltpu
from jax.sharding import PartitionSpec as P

BETA_ONE = 0.9
BETA_TWO = 0.95
LEARN_RATE = 0.001
EPSILON = 1e-08
STEP_COUNT = 20.0

X_SIZE = 4
VMEM_LIMIT = 60 * 1024 * 1024
COST = {"route_own": 30, "route_other": 30, "expert_own": 27, "expert_other": 10, "terms": 30, "share": 40, "combine": 10, "assemble": 2, "pair": 2}
PARAMS = pltpu.CompilerParams(vmem_limit_bytes=VMEM_LIMIT)


def cost(name):
    return pl.CostEstimate(flops=COST[name] * 10**9, bytes_accessed=0, transcendentals=0)


def partner(array, apart):
    return lax.ppermute(array, "ep", [(i, i ^ apart) for i in range(lax.axis_size("ep"))])


def dot(a, b):
    return jnp.dot(a, b, preferred_element_type=jnp.float32)


def dot_last(a, b):
    return lax.dot_general(a, b, (((1,), (1,)), ((), ())), preferred_element_type=jnp.float32)


def dot_first(a, b):
    return lax.dot_general(a, b, (((0,), (0,)), ((), ())), preferred_element_type=jnp.float32)


def iota(shape, axis):
    return lax.broadcasted_iota(jnp.int32, shape, axis)


def route_kernel(routes_ref, gates_ref, home_ref, flags_ref, tokens_ref, cotangent_ref, send_ref, mats_ref):
    top_count, tok_rows = routes_ref.shape
    slot_count = home_ref.shape[1]
    pairs = slot_count // 2
    half, double, width = send_ref.shape
    capacity = double // 2
    rows = half * capacity
    z_half = lax.axis_index("ep") // X_SIZE % 2
    place = iota((half, 1), 0)
    slot = (place // X_SIZE * 2 + z_half) * X_SIZE + place % X_SIZE
    flag = jnp.sum(
        jnp.where(iota((half, pairs), 1) == slot % pairs, flags_ref[...].astype(jnp.float32), 0.0),
        axis=1,
        keepdims=True,
    )
    source = jnp.where(flag > 0, (slot + pairs) % slot_count, slot)
    expert = jnp.sum(
        jnp.where(iota((half, slot_count), 1) == source, home_ref[...].astype(jnp.float32), 0.0),
        axis=1,
        keepdims=True,
    )
    routes = routes_ref[...].astype(jnp.float32)
    named = jnp.zeros((half, tok_rows), jnp.float32)
    gate = jnp.zeros((half, tok_rows), jnp.float32)
    for k in range(top_count):
        hit = routes[k : k + 1, :] == expert
        named = named + jnp.where(hit, 1.0, 0.0)
        gate = gate + jnp.where(hit, gates_ref[k : k + 1, :], 0.0)
    earlier = iota((tok_rows, tok_rows), 0) < iota((tok_rows, tok_rows), 1)
    earlier = jnp.where(earlier, 1.0, 0.0).astype(jnp.bfloat16)
    rank = jnp.where(named > 0, dot(named.astype(jnp.bfloat16), earlier), -1.0)
    spread = iota((rows, half), 0) // capacity == iota((rows, half), 1)
    spread = jnp.where(spread, 1.0, 0.0).astype(jnp.bfloat16)
    gate_high = gate.astype(jnp.bfloat16)
    gate_low = (gate - gate_high.astype(jnp.float32)).astype(jnp.bfloat16)
    order = (iota((rows, 1), 0) % capacity).astype(jnp.float32)
    hit = dot(spread, rank.astype(jnp.bfloat16)) == order
    one = jnp.where(hit, 1.0, 0.0).astype(jnp.bfloat16)
    high = jnp.where(hit, dot(spread, gate_high), 0.0).astype(jnp.bfloat16)
    low = jnp.where(hit, dot(spread, gate_low), 0.0).astype(jnp.bfloat16)
    mats_ref[0] = high
    mats_ref[1] = low
    mats_ref[2] = one
    x_rows = dot(one, tokens_ref[...]).astype(jnp.bfloat16)
    send_ref[:, :capacity, :] = x_rows.reshape(half, capacity, width)
    cotangent = cotangent_ref[...]
    upstream = dot(
        jnp.concatenate([high, low], axis=1), jnp.concatenate([cotangent, cotangent], axis=0)
    ).astype(jnp.bfloat16)
    send_ref[:, capacity:, :] = upstream.reshape(half, capacity, width)


def route(routes, gates, home, flags, tokens, cotangent, name):
    top_count, tok_rows = routes.shape
    half = home.shape[1] // 2
    capacity = tok_rows * top_count // home.shape[1]
    return pl.pallas_call(
        route_kernel,
        out_shape=(
            jax.ShapeDtypeStruct((half, 2 * capacity, tokens.shape[1]), jnp.bfloat16),
            jax.ShapeDtypeStruct((3, half * capacity, tok_rows), jnp.bfloat16),
        ),
        compiler_params=PARAMS,
        cost_estimate=cost(name),
        name=name,
    )(routes, gates, home, flags, tokens, cotangent)


def expert_kernel(arrived_ref, weights_ref, back_ref, act_ref):
    sources, double, width = arrived_ref.shape
    capacity = double // 2
    hidden_width = weights_ref.shape[1]
    x_rows = arrived_ref[:, :capacity, :].reshape(sources * capacity, width)
    upstream = arrived_ref[:, capacity:, :].reshape(sources * capacity, width)
    inner = weights_ref[:2].reshape(2 * hidden_width, width)
    w_down = weights_ref[2]
    projected = dot_last(x_rows, inner)
    gate_pre = projected[:, :hidden_width]
    up_pre = projected[:, hidden_width:]
    sigmoid = jax.nn.sigmoid(gate_pre)
    hidden = (gate_pre * sigmoid * up_pre).astype(jnp.bfloat16)
    out = dot(hidden, w_down).astype(jnp.bfloat16)
    back_ref[:, :capacity, :] = out.reshape(sources, capacity, width)
    hidden_grad = dot_last(upstream, w_down)
    gate_grad = hidden_grad * up_pre * sigmoid * (1.0 + gate_pre * (1.0 - sigmoid))
    up_grad = hidden_grad * gate_pre * sigmoid
    act_ref[:, :hidden_width] = gate_grad.astype(jnp.bfloat16)
    act_ref[:, hidden_width : 2 * hidden_width] = up_grad.astype(jnp.bfloat16)
    act_ref[:, 2 * hidden_width :] = hidden
    row_grad = dot(act_ref[:, : 2 * hidden_width], inner).astype(jnp.bfloat16)
    back_ref[:, capacity:, :] = row_grad.reshape(sources, capacity, width)


def expert(arrived, weights, steps, name):
    sources, double, width = arrived.shape
    hidden_width = weights.shape[1]
    block = sources // steps
    rows = block * double // 2
    return pl.pallas_call(
        expert_kernel,
        grid=(steps,),
        in_specs=[
            pl.BlockSpec((block, double, width), lambda i: (i, 0, 0)),
            pl.BlockSpec((3, hidden_width, width), lambda i: (0, 0, 0)),
        ],
        out_specs=(
            pl.BlockSpec((block, double, width), lambda i: (i, 0, 0)),
            pl.BlockSpec((rows, 3 * hidden_width), lambda i: (i, 0)),
        ),
        out_shape=(
            jax.ShapeDtypeStruct(arrived.shape, jnp.bfloat16),
            jax.ShapeDtypeStruct((rows * steps, 3 * hidden_width), jnp.bfloat16),
        ),
        compiler_params=PARAMS,
        cost_estimate=cost(name),
        name=name,
    )(arrived, weights)


def terms_kernel(one_ref, one_act_ref, two_ref, two_act_ref, keep_ref, give_ref):
    sources, double, width = one_ref.shape
    capacity = double // 2
    matrices, half_width, _ = keep_ref.shape
    inner = (matrices - 1) * 2 * half_width

    def kind(ref, low):
        return ref[:, low : low + capacity, :].reshape(sources * capacity, width)

    def store(matrix, terms):
        keep_ref[matrix] = terms[:half_width]
        give_ref[matrix] = terms[half_width:]

    terms = (
        dot_first(one_act_ref[:, :inner], kind(one_ref, 0))
        + dot_first(two_act_ref[:, :inner], kind(two_ref, 0))
    ).astype(jnp.bfloat16)
    for matrix in range(matrices - 1):
        store(matrix, terms[matrix * 2 * half_width : (matrix + 1) * 2 * half_width])
    terms = (
        dot_first(one_act_ref[:, inner:], kind(one_ref, capacity))
        + dot_first(two_act_ref[:, inner:], kind(two_ref, capacity))
    ).astype(jnp.bfloat16)
    store(matrices - 1, terms)


def gradient_terms(one, one_act, two, two_act):
    shape = jax.ShapeDtypeStruct((3, one_act.shape[1] // 6, one.shape[2]), jnp.bfloat16)
    return pl.pallas_call(
        terms_kernel,
        out_shape=(shape, shape),
        compiler_params=PARAMS,
        cost_estimate=cost("terms"),
        name="terms",
    )(one, one_act, two, two_act)


def assemble_kernel(*refs):
    *shard_refs, other_ref, weights_ref = refs
    units = other_ref.shape[2]
    for place, ref in enumerate(shard_refs):
        weights_ref[:, place * units : (place + 1) * units, :] = ref[...]
    for dz in range(other_ref.shape[0]):
        place = len(shard_refs) + dz
        weights_ref[:, place * units : (place + 1) * units, :] = other_ref[dz]


def move_hidden(array, apart):
    return lax.ppermute(array, "tp", [(i, i ^ apart) for i in range(lax.axis_size("tp"))])


def gather_column(weights):
    return [weights] + [move_hidden(weights, 2 * dz) for dz in range(1, lax.axis_size("tp") // 2)]


def gather_hidden(shards):
    tp_count = lax.axis_size("tp")
    other = move_hidden(jnp.stack(shards), 1)
    matrices, units, width = shards[0].shape
    return pl.pallas_call(
        assemble_kernel,
        out_shape=jax.ShapeDtypeStruct((matrices, tp_count * units, width), jnp.bfloat16),
        compiler_params=PARAMS,
        cost_estimate=cost("assemble"),
        name="assemble",
    )(*shards, other)


def pair_kernel(keep_ref, given_ref, *sum_refs):
    units = sum_refs[0].shape[1]
    for dz, ref in enumerate(sum_refs):
        held = slice(dz * units, (dz + 1) * units)
        total = keep_ref[:, held, :].astype(jnp.float32) + given_ref[:, held, :].astype(jnp.float32)
        ref[...] = total.astype(jnp.bfloat16)


def core_sums(keep, give):
    given = move_hidden(give, 1)
    count = lax.axis_size("tp") // 2
    matrices, half_width, width = keep.shape
    shape = jax.ShapeDtypeStruct((matrices, half_width // count, width), jnp.bfloat16)
    return pl.pallas_call(
        pair_kernel,
        out_shape=[shape] * count,
        compiler_params=PARAMS,
        cost_estimate=cost("pair"),
        name="pair",
    )(keep, given)


def weighted_sums(back_ref, mats_ref):
    half, double, width = back_ref.shape
    capacity = double // 2
    out_rows = back_ref[:, :capacity, :].reshape(half * capacity, width)
    grad_rows = back_ref[:, capacity:, :].reshape(half * capacity, width)
    out = dot_first(mats_ref[0], out_rows) + dot_first(mats_ref[1], out_rows)
    return out, dot_first(mats_ref[2], grad_rows)


def share_kernel(back_ref, mats_ref, share_ref):
    tok_rows = mats_ref.shape[2]
    out, grad = weighted_sums(back_ref, mats_ref)
    share_ref[:tok_rows] = out.astype(jnp.bfloat16)
    share_ref[tok_rows:] = grad.astype(jnp.bfloat16)


def share(back, mats):
    return pl.pallas_call(
        share_kernel,
        out_shape=jax.ShapeDtypeStruct((2 * mats.shape[2], back.shape[2]), jnp.bfloat16),
        compiler_params=pltpu.CompilerParams(vmem_limit_bytes=24 * 1024 * 1024),
        cost_estimate=cost("share"),
        name="share",
    )(back, mats)


def combine_kernel(back_ref, mats_ref, share_ref, out_ref, grad_ref):
    tok_rows = mats_ref.shape[2]
    out, grad = weighted_sums(back_ref, mats_ref)
    out_ref[...] = (out + share_ref[:tok_rows].astype(jnp.float32)).astype(jnp.bfloat16)
    grad_ref[...] = (grad + share_ref[tok_rows:].astype(jnp.float32)).astype(jnp.bfloat16)


def combine(back, mats, other_share):
    half, double, width = back.shape
    tok_rows = mats.shape[2]
    shape = jax.ShapeDtypeStruct((tok_rows, width), jnp.bfloat16)
    block = width // 2
    out_spec = pl.BlockSpec((tok_rows, block), lambda i: (0, i))
    return pl.pallas_call(
        combine_kernel,
        grid=(2,),
        in_specs=[
            pl.BlockSpec((half, double, block), lambda i: (0, 0, i)),
            pl.BlockSpec(mats.shape, lambda i: (0, 0, 0)),
            pl.BlockSpec((2 * tok_rows, block), lambda i: (0, i)),
        ],
        out_specs=(out_spec, out_spec),
        out_shape=(shape, shape),
        compiler_params=PARAMS,
        cost_estimate=cost("combine"),
        name="combine",
    )(back, mats, other_share)


def adam_update(weights, first_moment, second_moment, gradient):
    first_new = BETA_ONE * first_moment + (1.0 - BETA_ONE) * gradient
    second_new = BETA_TWO * second_moment + (1.0 - BETA_TWO) * gradient * gradient
    adam_step = (
        LEARN_RATE
        * (first_new / (1.0 - BETA_ONE**STEP_COUNT))
        / (jnp.sqrt(second_new / (1.0 - BETA_TWO**STEP_COUNT)) + EPSILON)
    )
    weight_new = (weights.astype(jnp.float32) - adam_step).astype(jnp.bfloat16)
    return (weight_new, first_new, second_new)


def shards(
    tokens, gates, routes, cotangent, old_home, swap_flags, weights, first_moment, second_moment
):
    slot_count = lax.axis_size("ep")
    half = slot_count // 2
    own = lax.axis_index("ep")
    model_width = tokens.shape[1]
    is_swapped = jnp.sum(jnp.where(jnp.arange(half) == own % half, swap_flags, 0)) == 1
    groups = [
        [i for i in range(slot_count) if i // X_SIZE % 2 == z_half] for z_half in range(2)
    ]

    def exchange(rows):
        return lax.all_to_all(
            rows, "ep", split_axis=0, concat_axis=0, tiled=True, axis_index_groups=groups
        )

    home = old_home.reshape(1, -1)
    flags = swap_flags.reshape(1, -1)
    own_send, own_mats = route(routes.T, gates.T, home, flags, tokens, cotangent, "route_own")
    own_arrived = exchange(own_send)
    weights = jnp.where(is_swapped, partner(weights, half), weights)
    both = jnp.concatenate([tokens, cotangent], axis=0)
    pack = jnp.concatenate([routes.T.astype(jnp.float32), gates.T], axis=0)
    pack, both, _, _ = lax.optimization_barrier((pack, both, own_send, weights))
    pack, both = partner(pack, X_SIZE), partner(both, X_SIZE)
    top_count, tok_rows = routes.shape[1], tokens.shape[0]
    other_send, other_mats = route(
        pack[:top_count], pack[top_count:], home, flags, both[:tok_rows], both[tok_rows:], "route_other"
    )
    first_sent, second_sent = first_moment.astype(jnp.bfloat16), second_moment.astype(jnp.bfloat16)
    weights, _ = lax.optimization_barrier((weights, other_send))
    shards = gather_column(weights[0])
    other_send, own_arrived, first_sent, second_sent = lax.optimization_barrier(
        (other_send, own_arrived, first_sent, second_sent)
    )
    other_first = partner(first_sent, half)
    other_arrived = exchange(other_send)

    other_first, *shards = lax.optimization_barrier((other_first, *shards))
    gathered = gather_hidden(shards)
    own_back, own_act = expert(own_arrived, gathered, 2, "expert_own")
    other_arrived, own_back, own_act, second_sent = lax.optimization_barrier(
        (other_arrived, own_back, own_act, second_sent)
    )
    other_second = partner(second_sent, half)
    other_back, other_act = expert(other_arrived, gathered, 2, "expert_other")
    other_returned = exchange(other_back)
    other_act, other_second = lax.optimization_barrier((other_act, other_second))
    keep, give = gradient_terms(own_arrived, own_act, other_arrived, other_act)
    sums = core_sums(keep, give)
    own_back, other_returned, _ = lax.optimization_barrier((own_back, other_returned, sums[0]))
    own_returned = exchange(own_back)

    sums = [sums[0]] + [move_hidden(sums[dz], 2 * dz) for dz in range(1, len(sums))]
    other_mats, *sums = lax.optimization_barrier((other_mats, *sums))
    gradient = sum(part.astype(jnp.float32) for part in sums)[None]
    first_moment = jnp.where(is_swapped, other_first.astype(jnp.float32), first_moment)
    second_moment = jnp.where(is_swapped, other_second.astype(jnp.float32), second_moment)
    new_weights, new_first, new_second = adam_update(weights, first_moment, second_moment, gradient)

    other_share = partner(share(other_returned, other_mats), X_SIZE)
    layer_output_rows, token_gradient_rows = combine(own_returned, own_mats, other_share)
    return (layer_output_rows, token_gradient_rows, new_weights, new_first, new_second)


def solution(mesh):
    in_specs = (
        P(("ep", "tp"), None),
        P(("ep", "tp"), None),
        P(("ep", "tp"), None),
        P(("ep", "tp"), None),
        P(),
        P(),
        P("ep", None, "tp", None),
        P("ep", None, "tp", None),
        P("ep", None, "tp", None),
    )
    out_specs = (
        P(("ep", "tp"), None),
        P(("ep", "tp"), None),
        P("ep", None, "tp", None),
        P("ep", None, "tp", None),
        P("ep", None, "tp", None),
    )
    return jax.shard_map(shards, mesh=mesh, in_specs=in_specs, out_specs=out_specs, check_vma=False)
```

time: 282 us -> 269 us (0.954)
  the two profiles are of different devices: /device:TPU:128 before, /device:TPU:80 now
where the time goes in v4:
time: 269 us; the launch traced here: 268 us
  waiting for transfers between devices  128 us (48%)
  starting transfers between devices  93.6 us (35%)
  Pallas kernels  37.8 us (14%)
  other arithmetic  4.96 us (2%)
    ppermute x6, waiting for transfers between devices, partner(): lax.ppermute(array, 'ep', [(i, i ^ apart) for i in range(lax.axis_size('e...  50 us
    all_to_all x4, waiting for transfers between devices, exchange(): lax.all_to_all(rows, 'ep', split_axis=0, concat_axis=0, tiled=True, axis_...  45.6 us
    ppermute x6, starting transfers between devices, partner(): lax.ppermute(array, 'ep', [(i, i ^ apart) for i in range(lax.axis_size('e...  38.6 us
    ppermute x8, waiting for transfers between devices, move_hidden(): lax.ppermute(array, 'tp', [(i, i ^ apart) for i in range(lax.axis_size('t...  32.2 us
    all_to_all x4, starting transfers between devices, exchange(): lax.all_to_all(rows, 'ep', split_axis=0, concat_axis=0, tiled=True, axis_...  32 us
    ppermute x8, starting transfers between devices, move_hidden(): lax.ppermute(array, 'tp', [(i, i ^ apart) for i in range(lax.axis_size('t...  23 us
    pallas_call x2, Pallas kernels, expert(): pl.pallas_call(expert_kernel, grid=(steps,), in_specs=[pl.BlockSpec((bloc...  14 us
    pallas_call x2, Pallas kernels, route(): pl.pallas_call(route_kernel, out_shape=(jax.ShapeDtypeStruct((half, 2 * c...  7.17 us
  transfers between devices with their start and end apart: 18, of which 12 were waited for; matrix products, arithmetic and copies ran while one was open for 2% of the time, Pallas kernels for 13%

profile of v4, /device:TPU:80, one launch (start us, length us, event | category | flops | bytes accessed | tf_op | source)
XLA Modules:
  0.0 268.2 jit_solution(5745937831407565136)
XLA Ops:
  0.6 5.9 %collective-permute-start = (bf16[1,3,48,1024]{3,2,1,0:T(8,128)(2,1)}, bf16[1,3,48,1024]{3,2,1,0:T(8,128)(2,1)S(1)}, u32[]{:S(2)}, u32[]{:S(2)}) collective-permute-start(bf16[1,3,48,1024]{3,2,1,0:T(8,128)(2,1)} %param.15), channel_id=1, source_target_pairs={{0,256},{8,264},{16,272},{24,280},{32,288},{40,296},{48,304},{56,3... | collective-permute-start | bytes 884744 | tf_op jit(solution)/shard_map/ppermute | solution.py:25
  6.6 3.6 %route_own.1 = (bf16[32,32,1024]{2,1,0:T(8,128)(2,1)}, bf16[3,512,128]{2,1,0:T(8,128)(2,1)}) custom-call(s32[8,128]{1,0:T(8,128)} %bitcast.24, f32[8,128]{1,0:T(8,128)} %bitcast.25, s32[1,64]{1,0:T(1,128)} %bitcast.27, s32[1,32]{1,0:T(1,128)} %bitcast.29, bf16[128,1024]{1,0:T(8,128)(2,1)} %tokens_ref.1, bf16[128,1024]{1,0:T(8,128)(2,1)} %cotangent_ref.1), custom_call_target="tpu_custom_call" | custom-call | flops 30000001024 | tf_op jit(solution)/shard_map/route_own/pallas_call | solution.py:100
  10.2 0.0 copy-start.17
  10.2 0.0 copy-start.18
  10.2 7.1 %all-to-all-start = ((bf16[32,32,1024]{2,1,0:T(8,128)(2,1)}), bf16[32,32,1024]{2,1,0:T(8,128)(2,1)}, u32[]{:S(2)}, u32[]{:S(2)}) async-start(bf16[32,32,1024]{2,1,0:T(8,128)(2,1)} %get-tuple-element.46), calls=%async_computation | async-start | bytes 4194304 | tf_op jit(solution)/shard_map/all_to_all | solution.py:333
  17.3 0.0 copy-start.15
  17.3 0.0 copy-start.3
  17.4 0.6 fusion.2
  18.7 0.0 copy-start.5
  18.8 3.6 %collective-permute-done = bf16[1,3,48,1024]{3,2,1,0:T(8,128)(2,1)S(1)} collective-permute-done((bf16[1,3,48,1024]{3,2,1,0:T(8,128)(2,1)}, bf16[1,3,48,1024]{3,2,1,0:T(8,128)(2,1)S(1)}, u32[]{:S(2)}, u32[]{:S(2)}) %collective-permute-start) | collective-permute-done | bytes 294944 | tf_op jit(solution)/shard_map/ppermute | solution.py:25
  22.5 0.0 copy-start.1
  22.5 10.0 %collective-permute-start.2 = (bf16[256,1024]{1,0:T(8,128)(2,1)S(1)}, bf16[256,1024]{1,0:T(8,128)(2,1)S(1)}, u32[]{:S(2)}, u32[]{:S(2)}) collective-permute-start(bf16[256,1024]{1,0:T(8,128)(2,1)S(1)} %pad_maximum_fusion.1), channel_id=1, source_target_pairs={{0,32},{8,40},{16,48},{24,56},{32,0},{40,8},{48,16},{56,24},{64,96... | collective-permute-start | bytes 1572872 | tf_op jit(solution)/shard_map/ppermute | solution.py:25
  32.5 1.9 collective-permute-start.1
  34.4 0.8 convert_element_type.34
  35.2 0.0 copy-done.5
  35.2 0.8 convert_element_type.35
  36.0 19.8 %collective-permute-done.1 = f32[16,128]{1,0:T(8,128)S(1)} collective-permute-done((f32[16,128]{1,0:T(8,128)S(1)}, f32[16,128]{1,0:T(8,128)S(1)}, u32[]{:S(2)}, u32[]{:S(2)}) %collective-permute-start.1) | collective-permute-done | bytes 8224 | tf_op jit(solution)/shard_map/ppermute | solution.py:25
  55.8 0.6 fusion.5
  56.4 0.0 collective-permute-done.2
  56.4 0.8 fusion.4
  57.2 3.6 %route_other.1 = (bf16[32,32,1024]{2,1,0:T(8,128)(2,1)}, bf16[3,512,128]{2,1,0:T(8,128)(2,1)}) custom-call(f32[8,128]{1,0:T(8,128)} %get-tuple-element.93.routes_ref, f32[8,128]{1,0:T(8,128)} %get-tuple-element.92.gates_ref, s32[1,64]{1,0:T(1,128)} %bitcast.28, s32[1,32]{1,0:T(1,128)} %bitcast.30, bf16[128,1024]{1,0:T(8,128)(2,1)} %get-tuple-element.91.tokens_ref, ...), custom_call_target="tpu_custom_call" | custom-call | flops 30000001024 | tf_op jit(solution)/shard_map/route_other/pallas_call | solution.py:100
  60.8 3.1 %collective-permute-start.6 = (bf16[3,48,1024]{2,1,0:T(8,128)(2,1)S(1)}, bf16[3,48,1024]{2,1,0:T(8,128)(2,1)S(1)}, u32[]{:S(2)}, u32[]{:S(2)}) collective-permute-start(bf16[3,48,1024]{2,1,0:T(8,128)(2,1)S(1)} %bitcast.18), channel_id=1, source_target_pairs={{0,6},{1,7},{2,4},{3,5},{4,2},{5,3},{6,0},{7,1},{8,14},{9,15},{10,... | collective-permute-start | bytes 884744 | tf_op jit(solution)/shard_map/ppermute | solution.py:211
  64.0 1.9 collective-permute-start.5
  65.9 4.2 %collective-permute-start.4 = (bf16[3,48,1024]{2,1,0:T(8,128)(2,1)S(1)}, bf16[3,48,1024]{2,1,0:T(8,128)(2,1)}, u32[]{:S(2)}, u32[]{:S(2)}) collective-permute-start(bf16[3,48,1024]{2,1,0:T(8,128)(2,1)S(1)} %bitcast.20), channel_id=1, source_target_pairs={{0,2},{1,3},{2,0},{3,1},{4,6},{5,7},{6,4},{7,5},{8,10},{9,11},{10,... | collective-permute-start | bytes 884744 | tf_op jit(solution)/shard_map/ppermute | solution.py:211
  70.1 0.0 all-to-all-done.arrived_ref.one_ref
  70.1 4.8 %collective-permute-start.3 = (bf16[1,3,48,1024]{3,2,1,0:T(8,128)(2,1)}, bf16[1,3,48,1024]{3,2,1,0:T(8,128)(2,1)S(1)}, u32[]{:S(2)}, u32[]{:S(2)}) collective-permute-start(bf16[1,3,48,1024]{3,2,1,0:T(8,128)(2,1)} %convert_element_type.34), channel_id=1, source_target_pairs={{0,256},{8,264},{16,272},{24,280},{32,288},{40,296},{48,304},{56,3... | collective-permute-start | bytes 884744 | tf_op jit(solution)/shard_map/ppermute | solution.py:25
  74.9 7.8 %all-to-all-start.1 = ((bf16[32,32,1024]{2,1,0:T(8,128)(2,1)}), bf16[32,32,1024]{2,1,0:T(8,128)(2,1)S(1)}, u32[]{:S(2)}, u32[]{:S(2)}) async-start(bf16[32,32,1024]{2,1,0:T(8,128)(2,1)} %get-tuple-element.50), calls=%async_computation.1 | async-start | bytes 4194304 | tf_op jit(solution)/shard_map/all_to_all | solution.py:333
  82.7 0.0 collective-permute-done.6.refs_3_
  82.8 1.8 collective-permute-done.5.refs_2_
  84.6 0.0 collective-permute-done.4.refs_1_
  84.6 8.1 %collective-permute-done.3 = bf16[1,3,48,1024]{3,2,1,0:T(8,128)(2,1)S(1)} collective-permute-done((bf16[1,3,48,1024]{3,2,1,0:T(8,128)(2,1)}, bf16[1,3,48,1024]{3,2,1,0:T(8,128)(2,1)S(1)}, u32[]{:S(2)}, u32[]{:S(2)}) %collective-permute-start.3) | collective-permute-done | bytes 294944 | tf_op jit(solution)/shard_map/ppermute | solution.py:25
  92.7 1.1 pad_maximum_fusion
  93.8 1.9 collective-permute-start.7
  95.8 2.9 %collective-permute-done.7.refs_4_ = bf16[4,3,48,1024]{3,2,1,0:T(8,128)(2,1)} collective-permute-done((bf16[4,3,48,1024]{3,2,1,0:T(8,128)(2,1)S(1)}, bf16[4,3,48,1024]{3,2,1,0:T(8,128)(2,1)}, u32[]{:S(2)}, u32[]{:S(2)}) %collective-permute-start.7) | collective-permute-done | bytes 1179680 | tf_op jit(solution)/shard_map/ppermute | solution.py:211
  98.7 3.2 %assemble.1.weights_ref = bf16[3,384,1024]{2,1,0:T(8,128)(2,1)} custom-call(bf16[3,48,1024]{2,1,0:T(8,128)(2,1)} %bitcast.21, bf16[3,48,1024]{2,1,0:T(8,128)(2,1)} %collective-permute-done.4.refs_1_, bf16[3,48,1024]{2,1,0:T(8,128)(2,1)} %copy-done.12, bf16[3,48,1024]{2,1,0:T(8,128)(2,1)} %copy-done.9, bf16[4,3,48,1024]{3,2,1,0:T(8,128)(2,1)} %collective-permute-done.7.refs_4_), custom_call_target="tpu_custom_call" | custom-call | flops 2000000000 | tf_op jit(solution)/shard_map/assemble/pallas_call | solution.py:222
  101.9 7.0 %expert_own.1 = (bf16[32,32,1024]{2,1,0:T(8,128)(2,1)}, bf16[512,1152]{1,0:T(8,128)(2,1)}) custom-call(bf16[32,32,1024]{2,1,0:T(8,128)(2,1)} %all-to-all-done.arrived_ref.one_ref, bf16[3,384,1024]{2,1,0:T(8,128)(2,1)} %assemble.1.weights_ref), custom_call_target="tpu_custom_call" | custom-call | flops 27000000512 | tf_op jit(solution)/shard_map/expert_own/pallas_call | solution.py:142
  108.9 25.1 %all-to-all-done.1.arrived_ref.two_ref = bf16[32,32,1024]{2,1,0:T(8,128)(2,1)S(1)} async-done(((bf16[32,32,1024]{2,1,0:T(8,128)(2,1)}), bf16[32,32,1024]{2,1,0:T(8,128)(2,1)S(1)}, u32[]{:S(2)}, u32[]{:S(2)}) %all-to-all-start.1) | async-done | bytes 2097184 | tf_op jit(solution)/shard_map/all_to_all | solution.py:333
  134.0 7.3 %collective-permute-start.8 = (bf16[1,3,48,1024]{3,2,1,0:T(8,128)(2,1)S(1)}, bf16[1,3,48,1024]{3,2,1,0:T(8,128)(2,1)S(1)}, u32[]{:S(2)}, u32[]{:S(2)}) collective-permute-start(bf16[1,3,48,1024]{3,2,1,0:T(8,128)(2,1)S(1)} %copy-done.16), channel_id=1, source_target_pairs={{0,256},{8,264},{16,272},{24,280},{32,288},{40,296},{48,304},{56,3... | collective-permute-start | bytes 884744 | tf_op jit(solution)/shard_map/ppermute | solution.py:25
  141.3 7.0 %expert_other.1 = (bf16[32,32,1024]{2,1,0:T(8,128)(2,1)}, bf16[512,1152]{1,0:T(8,128)(2,1)}) custom-call(bf16[32,32,1024]{2,1,0:T(8,128)(2,1)} %copy-done.7, bf16[3,384,1024]{2,1,0:T(8,128)(2,1)} %assemble.1.weights_ref), custom_call_target="tpu_custom_call" | custom-call | flops 10000000000 | tf_op jit(solution)/shard_map/expert_other/pallas_call | solution.py:142
  148.3 7.1 %all-to-all-start.2 = ((bf16[32,32,1024]{2,1,0:T(8,128)(2,1)}), bf16[32,32,1024]{2,1,0:T(8,128)(2,1)S(1)}, u32[]{:S(2)}, u32[]{:S(2)}) async-start(bf16[32,32,1024]{2,1,0:T(8,128)(2,1)} %get-tuple-element.63), calls=%async_computation.2 | async-start | bytes 4194304 | tf_op jit(solution)/shard_map/all_to_all | solution.py:333
  155.4 0.0 collective-permute-done.8
  155.4 6.9 %terms.1 = (bf16[3,192,1024]{2,1,0:T(8,128)(2,1)}, bf16[3,192,1024]{2,1,0:T(8,128)(2,1)}) custom-call(bf16[32,32,1024]{2,1,0:T(8,128)(2,1)} %all-to-all-done.arrived_ref.one_ref, bf16[512,1152]{1,0:T(8,128)(2,1)} %get-tuple-element.64.one_act_ref, bf16[32,32,1024]{2,1,0:T(8,128)(2,1)} %copy-done.7, bf16[512,1152]{1,0:T(8,128)(2,1)} %get-tuple-element.67.two_act_ref), custom_call_target="tpu_custom_call" | custom-call | flops 30000001024 | tf_op jit(solution)/shard_map/terms/pallas_call | solution.py:191
  162.3 1.9 collective-permute-start.9
  164.2 3.2 %collective-permute-done.9.given_ref = bf16[3,192,1024]{2,1,0:T(8,128)(2,1)} collective-permute-done((bf16[3,192,1024]{2,1,0:T(8,128)(2,1)}, bf16[3,192,1024]{2,1,0:T(8,128)(2,1)}, u32[]{:S(2)}, u32[]{:S(2)}) %collective-permute-start.9) | collective-permute-done | bytes 1179680 | tf_op jit(solution)/shard_map/ppermute | solution.py:211
  167.3 2.7 %pair.1 = (bf16[3,48,1024]{2,1,0:T(8,128)(2,1)}, bf16[3,48,1024]{2,1,0:T(8,128)(2,1)}, bf16[3,48,1024]{2,1,0:T(8,128)(2,1)}, bf16[3,48,1024]{2,1,0:T(8,128)(2,1)}) custom-call(bf16[3,192,1024]{2,1,0:T(8,128)(2,1)} %get-tuple-element.68.keep_ref, bf16[3,192,1024]{2,1,0:T(8,128)(2,1)} %collective-permute-done.9.given_ref), custom_call_target="tpu_custom_call" | custom-call | flops 2000000000 | tf_op jit(solution)/shard_map/pair/pallas_call | solution.py:244
  170.0 2.8 %collective-permute-start.10 = (bf16[3,48,1024]{2,1,0:T(8,128)(2,1)}, bf16[3,48,1024]{2,1,0:T(8,128)(2,1)S(1)}, u32[]{:S(2)}, u32[]{:S(2)}) collective-permute-start(bf16[3,48,1024]{2,1,0:T(8,128)(2,1)} %get-tuple-element.75), channel_id=1, source_target_pairs={{0,2},{1,3},{2,0},{3,1},{4,6},{5,7},{6,4},{7,5},{8,10},{9,11},{10,... | collective-permute-start | bytes 884744 | tf_op jit(solution)/shard_map/ppermute | solution.py:211
  172.9 5.0 %collective-permute-start.11 = (bf16[3,48,1024]{2,1,0:T(8,128)(2,1)}, bf16[3,48,1024]{2,1,0:T(8,128)(2,1)S(1)}, u32[]{:S(2)}, u32[]{:S(2)}) collective-permute-start(bf16[3,48,1024]{2,1,0:T(8,128)(2,1)} %get-tuple-element.76), channel_id=1, source_target_pairs={{0,4},{1,5},{2,6},{3,7},{4,0},{5,1},{6,2},{7,3},{8,12},{9,13},{10,... | collective-permute-start | bytes 884744 | tf_op jit(solution)/shard_map/ppermute | solution.py:211
  178.0 2.1 collective-permute-start.12
  180.1 3.9 %collective-permute-done.10 = bf16[3,48,1024]{2,1,0:T(8,128)(2,1)S(1)} collective-permute-done((bf16[3,48,1024]{2,1,0:T(8,128)(2,1)}, bf16[3,48,1024]{2,1,0:T(8,128)(2,1)S(1)}, u32[]{:S(2)}, u32[]{:S(2)}) %collective-permute-start.10) | collective-permute-done | bytes 294944 | tf_op jit(solution)/shard_map/ppermute | solution.py:211
  184.0 14.3 %collective-permute-done.11 = bf16[3,48,1024]{2,1,0:T(8,128)(2,1)S(1)} collective-permute-done((bf16[3,48,1024]{2,1,0:T(8,128)(2,1)}, bf16[3,48,1024]{2,1,0:T(8,128)(2,1)S(1)}, u32[]{:S(2)}, u32[]{:S(2)}) %collective-permute-start.11) | collective-permute-done | bytes 294944 | tf_op jit(solution)/shard_map/ppermute | solution.py:211
  198.3 6.1 %collective-permute-done.12 = bf16[3,48,1024]{2,1,0:T(8,128)(2,1)S(1)} collective-permute-done((bf16[3,48,1024]{2,1,0:T(8,128)(2,1)}, bf16[3,48,1024]{2,1,0:T(8,128)(2,1)S(1)}, u32[]{:S(2)}, u32[]{:S(2)}) %collective-permute-start.12) | collective-permute-done | bytes 294944 | tf_op jit(solution)/shard_map/ppermute | solution.py:211
  204.4 0.7 copy-done.13
  205.1 0.0 all-to-all-done.2.back_ref
  205.1 10.0 %all-to-all-start.3 = ((bf16[32,32,1024]{2,1,0:T(8,128)(2,1)}), bf16[32,32,1024]{2,1,0:T(8,128)(2,1)}, u32[]{:S(2)}, u32[]{:S(2)}) async-start(bf16[32,32,1024]{2,1,0:T(8,128)(2,1)} %get-tuple-element.71), calls=%async_computation.3 | async-start | bytes 4194304 | tf_op jit(solution)/shard_map/all_to_all | solution.py:333
  215.1 0.0 copy-start.2
  215.1 0.0 copy-start.4
  215.1 0.0 copy-start.6
  215.1 0.0 copy-start.8
  215.2 0.6 share.1
  215.8 8.6 %collective-permute-start.13 = (bf16[256,1024]{1,0:T(8,128)(2,1)S(1)}, bf16[256,1024]{1,0:T(8,128)(2,1)S(1)}, u32[]{:S(2)}, u32[]{:S(2)}) collective-permute-start(bf16[256,1024]{1,0:T(8,128)(2,1)S(1)} %share.1), channel_id=1, source_target_pairs={{0,32},{8,40},{16,48},{24,56},{32,0},{40,8},{48,16},{56,24},{64,96... | collective-permute-start | bytes 1572872 | tf_op jit(solution)/shard_map/ppermute | solution.py:25
  224.5 1.6 subtract_convert_fusion
  226.0 18.5 %collective-permute-done.13.share_ref = bf16[256,1024]{1,0:T(8,128)(2,1)S(1)} collective-permute-done((bf16[256,1024]{1,0:T(8,128)(2,1)S(1)}, bf16[256,1024]{1,0:T(8,128)(2,1)S(1)}, u32[]{:S(2)}, u32[]{:S(2)}) %collective-permute-start.13) | collective-permute-done | bytes 524320 | tf_op jit(solution)/shard_map/ppermute | solution.py:25
  244.5 20.5 %all-to-all-done.3.back_ref = bf16[32,32,1024]{2,1,0:T(8,128)(2,1)} async-done(((bf16[32,32,1024]{2,1,0:T(8,128)(2,1)}), bf16[32,32,1024]{2,1,0:T(8,128)(2,1)}, u32[]{:S(2)}, u32[]{:S(2)}) %all-to-all-start.3) | async-done | bytes 2097184 | tf_op jit(solution)/shard_map/all_to_all | solution.py:333
  265.0 3.2 %combine.1 = (bf16[128,1024]{1,0:T(8,128)(2,1)}, bf16[128,1024]{1,0:T(8,128)(2,1)}) custom-call(bf16[32,32,1024]{2,1,0:T(8,128)(2,1)} %all-to-all-done.3.back_ref, bf16[3,512,128]{2,1,0:T(8,128)(2,1)} %get-tuple-element.72.mats_ref, bf16[256,1024]{1,0:T(8,128)(2,1)} %copy-done.21), custom_call_target="tpu_custom_call" | custom-call | flops 10000000000 | tf_op jit(solution)/shard_map/combine/pallas_call | solution.py:292
  (38 shorter events, 0.1 us)
Async XLA Ops:
  0.6 21.8 %collective-permute-start = (bf16[1,3,48,1024]{3,2,1,0:T(8,128)(2,1)}, bf16[1,3,48,1024]{3,2,1,0:T(8,128)(2,1)S(1)}, u32[]{:S(2)}, u32[]{:S(2)}) collective-permute-start(bf16[1,3,48,1024]{3,2,1,0:T(8,128)(2,1)} %param.15), channel_id=1, source_target_pairs={{0,256},{8,264},{16,272},{24,280},{32,288},{40,296},{48,304},{56,3... | collective-permute-start | bytes 884744 | tf_op jit(solution)/shard_map/ppermute | solution.py:25
  10.1 7.2 %copy-start.19 = (s32[128,8]{0,1:T(8,128)S(1)}, s32[128,8]{0,1:T(8,128)}, u32[]{:S(2)}) copy-start(s32[128,8]{0,1:T(8,128)} %param.11) | copy-start | bytes 12292
  10.1 7.2 %copy-start.22 = (s32[32]{0:T(128)S(1)}, s32[32]{0:T(128)}, u32[]{:S(2)}) copy-start(s32[32]{0:T(128)} %param.14) | copy-start | bytes 388
  10.1 8.5 %copy-start.20 = (f32[128,8]{0,1:T(8,128)S(1)}, f32[128,8]{0,1:T(8,128)}, u32[]{:S(2)}) copy-start(f32[128,8]{0,1:T(8,128)} %param.10) | copy-start | bytes 12292
  10.2 8.6 %copy-start.17 = (bf16[128,1024]{1,0:T(8,128)(2,1)S(1)}, bf16[128,1024]{1,0:T(8,128)(2,1)}, u32[]{:S(2)}) copy-start(bf16[128,1024]{1,0:T(8,128)(2,1)} %tokens_ref.1) | copy-start | bytes 786436
  10.2 8.5 %copy-start.18 = (bf16[128,1024]{1,0:T(8,128)(2,1)S(1)}, bf16[128,1024]{1,0:T(8,128)(2,1)}, u32[]{:S(2)}) copy-start(bf16[128,1024]{1,0:T(8,128)(2,1)} %cotangent_ref.1) | copy-start | bytes 786436
  10.2 59.9 %all-to-all-start = ((bf16[32,32,1024]{2,1,0:T(8,128)(2,1)}), bf16[32,32,1024]{2,1,0:T(8,128)(2,1)}, u32[]{:S(2)}, u32[]{:S(2)}) async-start(bf16[32,32,1024]{2,1,0:T(8,128)(2,1)} %get-tuple-element.46), calls=%async_computation | async-start | bytes 4194304 | tf_op jit(solution)/shard_map/all_to_all | solution.py:333
  17.3 5.1 %copy-start.15 = (bf16[1,3,48,1024]{3,2,1,0:T(8,128)(2,1)S(1)}, bf16[1,3,48,1024]{3,2,1,0:T(8,128)(2,1)}, u32[]{:S(2)}) copy-start(bf16[1,3,48,1024]{3,2,1,0:T(8,128)(2,1)} %param.15) | copy-start | bytes 884740
  17.3 17.1 %copy-start.3 = (f32[1,3,48,1024]{3,2,1,0:T(8,128)S(1)}, f32[1,3,48,1024]{3,2,1,0:T(8,128)}, u32[]{:S(2)}) copy-start(f32[1,3,48,1024]{3,2,1,0:T(8,128)} %param.16) | copy-start | bytes 1769476
  18.7 16.5 %copy-start.5 = (f32[1,3,48,1024]{3,2,1,0:T(8,128)S(1)}, f32[1,3,48,1024]{3,2,1,0:T(8,128)}, u32[]{:S(2)}) copy-start(f32[1,3,48,1024]{3,2,1,0:T(8,128)} %param.17) | copy-start | bytes 1769476
  22.5 70.2 %copy-start.1 = (bf16[1,3,48,1024]{3,2,1,0:T(8,128)(2,1)}, bf16[1,3,48,1024]{3,2,1,0:T(8,128)(2,1)S(1)}, u32[]{:S(2)}) copy-start(bf16[1,3,48,1024]{3,2,1,0:T(8,128)(2,1)S(1)} %broadcast_select_fusion) | copy-start | bytes 884740
  22.5 33.9 %collective-permute-start.2 = (bf16[256,1024]{1,0:T(8,128)(2,1)S(1)}, bf16[256,1024]{1,0:T(8,128)(2,1)S(1)}, u32[]{:S(2)}, u32[]{:S(2)}) collective-permute-start(bf16[256,1024]{1,0:T(8,128)(2,1)S(1)} %pad_maximum_fusion.1), channel_id=1, source_target_pairs={{0,32},{8,40},{16,48},{24,56},{32,0},{40,8},{48,16},{56,24},{64,96... | collective-permute-start | bytes 1572872 | tf_op jit(solution)/shard_map/ppermute | solution.py:25
  32.5 23.3 %collective-permute-start.1 = (f32[16,128]{1,0:T(8,128)S(1)}, f32[16,128]{1,0:T(8,128)S(1)}, u32[]{:S(2)}, u32[]{:S(2)}) collective-permute-start(f32[16,128]{1,0:T(8,128)S(1)} %pad_maximum_fusion.2), channel_id=1, source_target_pairs={{0,32},{8,40},{16,48},{24,56},{32,0},{40,8},{48,16},{56,24},{64,96... | collective-permute-start | bytes 24584 | tf_op jit(solution)/shard_map/ppermute | solution.py:25
  60.8 21.9 %collective-permute-start.6 = (bf16[3,48,1024]{2,1,0:T(8,128)(2,1)S(1)}, bf16[3,48,1024]{2,1,0:T(8,128)(2,1)S(1)}, u32[]{:S(2)}, u32[]{:S(2)}) collective-permute-start(bf16[3,48,1024]{2,1,0:T(8,128)(2,1)S(1)} %bitcast.18), channel_id=1, source_target_pairs={{0,6},{1,7},{2,4},{3,5},{4,2},{5,3},{6,0},{7,1},{8,14},{9,15},{10,... | collective-permute-start | bytes 884744 | tf_op jit(solution)/shard_map/ppermute | solution.py:211
  64.0 20.6 %collective-permute-start.5 = (bf16[3,48,1024]{2,1,0:T(8,128)(2,1)S(1)}, bf16[3,48,1024]{2,1,0:T(8,128)(2,1)S(1)}, u32[]{:S(2)}, u32[]{:S(2)}) collective-permute-start(bf16[3,48,1024]{2,1,0:T(8,128)(2,1)S(1)} %bitcast.19), channel_id=1, source_target_pairs={{0,4},{1,5},{2,6},{3,7},{4,0},{5,1},{6,2},{7,3},{8,12},{9,13},{10,... | collective-permute-start | bytes 884744 | tf_op jit(solution)/shard_map/ppermute | solution.py:211
  65.9 18.7 %collective-permute-start.4 = (bf16[3,48,1024]{2,1,0:T(8,128)(2,1)S(1)}, bf16[3,48,1024]{2,1,0:T(8,128)(2,1)}, u32[]{:S(2)}, u32[]{:S(2)}) collective-permute-start(bf16[3,48,1024]{2,1,0:T(8,128)(2,1)S(1)} %bitcast.20), channel_id=1, source_target_pairs={{0,2},{1,3},{2,0},{3,1},{4,6},{5,7},{6,4},{7,5},{8,10},{9,11},{10,... | collective-permute-start | bytes 884744 | tf_op jit(solution)/shard_map/ppermute | solution.py:211
  70.1 22.6 %collective-permute-start.3 = (bf16[1,3,48,1024]{3,2,1,0:T(8,128)(2,1)}, bf16[1,3,48,1024]{3,2,1,0:T(8,128)(2,1)S(1)}, u32[]{:S(2)}, u32[]{:S(2)}) collective-permute-start(bf16[1,3,48,1024]{3,2,1,0:T(8,128)(2,1)} %convert_element_type.34), channel_id=1, source_target_pairs={{0,256},{8,264},{16,272},{24,280},{32,288},{40,296},{48,304},{56,3... | collective-permute-start | bytes 884744 | tf_op jit(solution)/shard_map/ppermute | solution.py:25
  74.9 59.1 %all-to-all-start.1 = ((bf16[32,32,1024]{2,1,0:T(8,128)(2,1)}), bf16[32,32,1024]{2,1,0:T(8,128)(2,1)S(1)}, u32[]{:S(2)}, u32[]{:S(2)}) async-start(bf16[32,32,1024]{2,1,0:T(8,128)(2,1)} %get-tuple-element.50), calls=%async_computation.1 | async-start | bytes 4194304 | tf_op jit(solution)/shard_map/all_to_all | solution.py:333
  82.7 11.1 %copy-start.9 = (bf16[3,48,1024]{2,1,0:T(8,128)(2,1)}, bf16[3,48,1024]{2,1,0:T(8,128)(2,1)S(1)}, u32[]{:S(2)}) copy-start(bf16[3,48,1024]{2,1,0:T(8,128)(2,1)S(1)} %collective-permute-done.6.refs_3_) | copy-start | bytes 884740
  84.6 9.3 %copy-start.12 = (bf16[3,48,1024]{2,1,0:T(8,128)(2,1)}, bf16[3,48,1024]{2,1,0:T(8,128)(2,1)S(1)}, u32[]{:S(2)}) copy-start(bf16[3,48,1024]{2,1,0:T(8,128)(2,1)S(1)} %collective-permute-done.5.refs_2_) | copy-start | bytes 884740
  93.8 4.9 %collective-permute-start.7 = (bf16[4,3,48,1024]{3,2,1,0:T(8,128)(2,1)S(1)}, bf16[4,3,48,1024]{3,2,1,0:T(8,128)(2,1)}, u32[]{:S(2)}, u32[]{:S(2)}) collective-permute-start(bf16[4,3,48,1024]{3,2,1,0:T(8,128)(2,1)S(1)} %pad_maximum_fusion), channel_id=1, source_target_pairs={{0,1},{1,0},{2,3},{3,2},{4,5},{5,4},{6,7},{7,6},{8,9},{9,8},{10,11... | collective-permute-start | bytes 3538952 | tf_op jit(solution)/shard_map/ppermute | solution.py:211
  101.9 32.1 %copy-start.16 = (bf16[1,3,48,1024]{3,2,1,0:T(8,128)(2,1)S(1)}, bf16[1,3,48,1024]{3,2,1,0:T(8,128)(2,1)}, u32[]{:S(2)}) copy-start(bf16[1,3,48,1024]{3,2,1,0:T(8,128)(2,1)} %convert_element_type.35) | copy-start | bytes 884740
  134.0 7.3 %copy-start.7 = (bf16[32,32,1024]{2,1,0:T(8,128)(2,1)}, bf16[32,32,1024]{2,1,0:T(8,128)(2,1)S(1)}, u32[]{:S(2)}) copy-start(bf16[32,32,1024]{2,1,0:T(8,128)(2,1)S(1)} %all-to-all-done.1.arrived_ref.two_ref) | copy-start | bytes 6291460
  134.0 21.4 %collective-permute-start.8 = (bf16[1,3,48,1024]{3,2,1,0:T(8,128)(2,1)S(1)}, bf16[1,3,48,1024]{3,2,1,0:T(8,128)(2,1)S(1)}, u32[]{:S(2)}, u32[]{:S(2)}) collective-permute-start(bf16[1,3,48,1024]{3,2,1,0:T(8,128)(2,1)S(1)} %copy-done.16), channel_id=1, source_target_pairs={{0,256},{8,264},{16,272},{24,280},{32,288},{40,296},{48,304},{56,3... | collective-permute-start | bytes 884744 | tf_op jit(solution)/shard_map/ppermute | solution.py:25
  148.3 56.8 %all-to-all-start.2 = ((bf16[32,32,1024]{2,1,0:T(8,128)(2,1)}), bf16[32,32,1024]{2,1,0:T(8,128)(2,1)S(1)}, u32[]{:S(2)}, u32[]{:S(2)}) async-start(bf16[32,32,1024]{2,1,0:T(8,128)(2,1)} %get-tuple-element.63), calls=%async_computation.2 | async-start | bytes 4194304 | tf_op jit(solution)/shard_map/all_to_all | solution.py:333
  162.3 5.1 %collective-permute-start.9 = (bf16[3,192,1024]{2,1,0:T(8,128)(2,1)}, bf16[3,192,1024]{2,1,0:T(8,128)(2,1)}, u32[]{:S(2)}, u32[]{:S(2)}) collective-permute-start(bf16[3,192,1024]{2,1,0:T(8,128)(2,1)} %get-tuple-element.69), channel_id=1, source_target_pairs={{0,1},{1,0},{2,3},{3,2},{4,5},{5,4},{6,7},{7,6},{8,9},{9,8},{10,11... | collective-permute-start | bytes 3538952 | tf_op jit(solution)/shard_map/ppermute | solution.py:211
  170.0 14.0 %collective-permute-start.10 = (bf16[3,48,1024]{2,1,0:T(8,128)(2,1)}, bf16[3,48,1024]{2,1,0:T(8,128)(2,1)S(1)}, u32[]{:S(2)}, u32[]{:S(2)}) collective-permute-start(bf16[3,48,1024]{2,1,0:T(8,128)(2,1)} %get-tuple-element.75), channel_id=1, source_target_pairs={{0,2},{1,3},{2,0},{3,1},{4,6},{5,7},{6,4},{7,5},{8,10},{9,11},{10,... | collective-permute-start | bytes 884744 | tf_op jit(solution)/shard_map/ppermute | solution.py:211
  172.9 25.4 %collective-permute-start.11 = (bf16[3,48,1024]{2,1,0:T(8,128)(2,1)}, bf16[3,48,1024]{2,1,0:T(8,128)(2,1)S(1)}, u32[]{:S(2)}, u32[]{:S(2)}) collective-permute-start(bf16[3,48,1024]{2,1,0:T(8,128)(2,1)} %get-tuple-element.76), channel_id=1, source_target_pairs={{0,4},{1,5},{2,6},{3,7},{4,0},{5,1},{6,2},{7,3},{8,12},{9,13},{10,... | collective-permute-start | bytes 884744 | tf_op jit(solution)/shard_map/ppermute | solution.py:211
  178.0 26.4 %collective-permute-start.12 = (bf16[3,48,1024]{2,1,0:T(8,128)(2,1)}, bf16[3,48,1024]{2,1,0:T(8,128)(2,1)S(1)}, u32[]{:S(2)}, u32[]{:S(2)}) collective-permute-start(bf16[3,48,1024]{2,1,0:T(8,128)(2,1)} %get-tuple-element.77), channel_id=1, source_target_pairs={{0,6},{1,7},{2,4},{3,5},{4,2},{5,3},{6,0},{7,1},{8,14},{9,15},{10,... | collective-permute-start | bytes 884744 | tf_op jit(solution)/shard_map/ppermute | solution.py:211
  198.3 6.1 %copy-start.10 = (bf16[3,48,1024]{2,1,0:T(8,128)(2,1)}, bf16[3,48,1024]{2,1,0:T(8,128)(2,1)S(1)}, u32[]{:S(2)}) copy-start(bf16[3,48,1024]{2,1,0:T(8,128)(2,1)S(1)} %collective-permute-done.11) | copy-start | bytes 884740
  204.4 0.7 copy-start.13
  205.1 10.0 %copy-start = (bf16[3,512,128]{2,1,0:T(8,128)(2,1)S(1)}, bf16[3,512,128]{2,1,0:T(8,128)(2,1)}, u32[]{:S(2)}) copy-start(bf16[3,512,128]{2,1,0:T(8,128)(2,1)} %get-tuple-element.78.mats_ref) | copy-start | bytes 1179652
  205.1 59.9 %all-to-all-start.3 = ((bf16[32,32,1024]{2,1,0:T(8,128)(2,1)}), bf16[32,32,1024]{2,1,0:T(8,128)(2,1)}, u32[]{:S(2)}, u32[]{:S(2)}) async-start(bf16[32,32,1024]{2,1,0:T(8,128)(2,1)} %get-tuple-element.71), calls=%async_computation.3 | async-start | bytes 4194304 | tf_op jit(solution)/shard_map/all_to_all | solution.py:333
  215.1 9.3 %copy-start.2 = (bf16[1,3,48,1024]{3,2,1,0:T(8,128)(2,1)S(1)}, bf16[1,3,48,1024]{3,2,1,0:T(8,128)(2,1)}, u32[]{:S(2)}) copy-start(bf16[1,3,48,1024]{3,2,1,0:T(8,128)(2,1)} %copy-done.1) | copy-start | bytes 884740
  215.1 9.3 %copy-start.4 = (f32[1,3,48,1024]{3,2,1,0:T(8,128)S(1)}, f32[1,3,48,1024]{3,2,1,0:T(8,128)}, u32[]{:S(2)}) copy-start(f32[1,3,48,1024]{3,2,1,0:T(8,128)} %param.16) | copy-start | bytes 1769476
  215.1 9.3 %copy-start.6 = (f32[1,3,48,1024]{3,2,1,0:T(8,128)S(1)}, f32[1,3,48,1024]{3,2,1,0:T(8,128)}, u32[]{:S(2)}) copy-start(f32[1,3,48,1024]{3,2,1,0:T(8,128)} %param.17) | copy-start | bytes 1769476
  215.1 9.3 %copy-start.8 = (bf16[3,48,1024]{2,1,0:T(8,128)(2,1)S(1)}, bf16[3,48,1024]{2,1,0:T(8,128)(2,1)}, u32[]{:S(2)}) copy-start(bf16[3,48,1024]{2,1,0:T(8,128)(2,1)} %get-tuple-element.82) | copy-start | bytes 884740
  215.1 9.3 %copy-start.11 = (bf16[3,48,1024]{2,1,0:T(8,128)(2,1)S(1)}, bf16[3,48,1024]{2,1,0:T(8,128)(2,1)}, u32[]{:S(2)}) copy-start(bf16[3,48,1024]{2,1,0:T(8,128)(2,1)} %copy-done.10) | copy-start | bytes 884740
  215.2 9.3 %copy-start.14 = (bf16[3,48,1024]{2,1,0:T(8,128)(2,1)S(1)}, bf16[3,48,1024]{2,1,0:T(8,128)(2,1)}, u32[]{:S(2)}) copy-start(bf16[3,48,1024]{2,1,0:T(8,128)(2,1)} %copy-done.13) | copy-start | bytes 884740
  215.8 28.7 %collective-permute-start.13 = (bf16[256,1024]{1,0:T(8,128)(2,1)S(1)}, bf16[256,1024]{1,0:T(8,128)(2,1)S(1)}, u32[]{:S(2)}, u32[]{:S(2)}) collective-permute-start(bf16[256,1024]{1,0:T(8,128)(2,1)S(1)} %share.1), channel_id=1, source_target_pairs={{0,32},{8,40},{16,48},{24,56},{32,0},{40,8},{48,16},{56,24},{64,96... | collective-permute-start | bytes 1572872 | tf_op jit(solution)/shard_map/ppermute | solution.py:25
  244.5 20.5 %copy-start.21 = (bf16[256,1024]{1,0:T(8,128)(2,1)}, bf16[256,1024]{1,0:T(8,128)(2,1)S(1)}, u32[]{:S(2)}) copy-start(bf16[256,1024]{1,0:T(8,128)(2,1)S(1)} %collective-permute-done.13.share_ref) | copy-start | bytes 1572868

commit v5 on v4

--- a/solution.py
+++ b/solution.py
@@ -13,7 +13,7 @@
 
 X_SIZE = 4
 VMEM_LIMIT = 60 * 1024 * 1024
-COST = {"route_own": 30, "route_other": 30, "expert_own": 27, "expert_other": 10, "terms": 30, "share": 40, "combine": 10, "assemble": 2, "pair": 2}
+COST = {"route_own": 30, "route_other": 30, "expert_own": 27, "expert_other": 10, "terms": 30, "share": 36, "combine": 10, "assemble": 2, "pair": 2}
 PARAMS = pltpu.CompilerParams(vmem_limit_bytes=VMEM_LIMIT)
 
 

time: 269 us -> 267 us (level)
  the two profiles are of different devices: /device:TPU:80 before, /device:TPU:16 now
where the time goes in v5:
time: 267 us; the launch traced here: 266 us
  starting transfers between devices  109 us (41%)
  waiting for transfers between devices  109 us (41%)
  Pallas kernels  37.9 us (14%)
  other arithmetic  6.2 us (2%)
    all_to_all x4, waiting for transfers between devices, exchange(): lax.all_to_all(rows, 'ep', split_axis=0, concat_axis=0, tiled=True, axis_...  79.7 us
    ppermute x6, starting transfers between devices, partner(): lax.ppermute(array, 'ep', [(i, i ^ apart) for i in range(lax.axis_size('e...  42.2 us
    ppermute x8, starting transfers between devices, move_hidden(): lax.ppermute(array, 'tp', [(i, i ^ apart) for i in range(lax.axis_size('t...  34.9 us
    all_to_all x4, starting transfers between devices, exchange(): lax.all_to_all(rows, 'ep', split_axis=0, concat_axis=0, tiled=True, axis_...  31.7 us
    ppermute x6, waiting for transfers between devices, partner(): lax.ppermute(array, 'ep', [(i, i ^ apart) for i in range(lax.axis_size('e...  20 us
    pallas_call x2, Pallas kernels, expert(): pl.pallas_call(expert_kernel, grid=(steps,), in_specs=[pl.BlockSpec((bloc...  14 us
    ppermute x8, waiting for transfers between devices, move_hidden(): lax.ppermute(array, 'tp', [(i, i ^ apart) for i in range(lax.axis_size('t...  9.29 us
    pallas_call x2, Pallas kernels, route(): pl.pallas_call(route_kernel, out_shape=(jax.ShapeDtypeStruct((half, 2 * c...  7.15 us
  transfers between devices with their start and end apart: 18, of which 9 were waited for; matrix products, arithmetic and copies ran while one was open for 3% of the time, Pallas kernels for 13%

profile of v5, /device:TPU:16, one launch (start us, length us, event | category | flops | bytes accessed | tf_op | source)
XLA Modules:
  0.0 266.0 jit_solution(17386032739500809656)
XLA Ops:
  0.6 5.9 %collective-permute-start = (bf16[1,3,48,1024]{3,2,1,0:T(8,128)(2,1)}, bf16[1,3,48,1024]{3,2,1,0:T(8,128)(2,1)}, u32[]{:S(2)}, u32[]{:S(2)}) collective-permute-start(bf16[1,3,48,1024]{3,2,1,0:T(8,128)(2,1)} %param.15), channel_id=1, source_target_pairs={{0,256},{8,264},{16,272},{24,280},{32,288},{40,296},{48,304},{56,3... | collective-permute-start | bytes 884744 | tf_op jit(solution)/shard_map/ppermute | solution.py:25
  6.6 3.6 %route_own.1 = (bf16[32,32,1024]{2,1,0:T(8,128)(2,1)}, bf16[3,512,128]{2,1,0:T(8,128)(2,1)}) custom-call(s32[8,128]{1,0:T(8,128)} %bitcast.22, f32[8,128]{1,0:T(8,128)} %bitcast.23, s32[1,64]{1,0:T(1,128)} %bitcast.25, s32[1,32]{1,0:T(1,128)} %bitcast.27, bf16[128,1024]{1,0:T(8,128)(2,1)} %tokens_ref.1, bf16[128,1024]{1,0:T(8,128)(2,1)} %cotangent_ref.1), custom_call_target="tpu_custom_call" | custom-call | flops 30000001024 | tf_op jit(solution)/shard_map/route_own/pallas_call | solution.py:100
  10.2 0.0 copy-start.11
  10.2 0.0 copy-start.12
  10.2 9.2 %all-to-all-start = ((bf16[32,32,1024]{2,1,0:T(8,128)(2,1)}), bf16[32,32,1024]{2,1,0:T(8,128)(2,1)S(1)}, u32[]{:S(2)}, u32[]{:S(2)}) async-start(bf16[32,32,1024]{2,1,0:T(8,128)(2,1)} %get-tuple-element.46), calls=%async_computation | async-start | bytes 4194304 | tf_op jit(solution)/shard_map/all_to_all | solution.py:333
  19.4 0.0 copy-start.10
  19.4 0.0 copy-start.3
  19.5 0.6 fusion.2
  20.8 0.0 copy-start.4
  20.9 0.0 collective-permute-done
  20.9 0.0 copy-start.1
  20.9 13.5 %collective-permute-start.2 = (bf16[256,1024]{1,0:T(8,128)(2,1)S(1)}, bf16[256,1024]{1,0:T(8,128)(2,1)S(1)}, u32[]{:S(2)}, u32[]{:S(2)}) collective-permute-start(bf16[256,1024]{1,0:T(8,128)(2,1)S(1)} %pad_maximum_fusion.1), channel_id=1, source_target_pairs={{0,32},{8,40},{16,48},{24,56},{32,0},{40,8},{48,16},{56,24},{64,96... | collective-permute-start | bytes 1572872 | tf_op jit(solution)/shard_map/ppermute | solution.py:25
  34.5 1.9 collective-permute-start.1
  36.4 0.8 convert_element_type.34
  37.2 0.0 copy-done.4
  37.2 0.7 convert_element_type.35
  37.9 8.3 %collective-permute-done.1 = f32[16,128]{1,0:T(8,128)S(1)} collective-permute-done((f32[16,128]{1,0:T(8,128)S(1)}, f32[16,128]{1,0:T(8,128)S(1)}, u32[]{:S(2)}, u32[]{:S(2)}) %collective-permute-start.1) | collective-permute-done | bytes 8224 | tf_op jit(solution)/shard_map/ppermute | solution.py:25
  46.2 0.6 fusion.5
  46.8 0.0 collective-permute-done.2
  46.8 0.8 fusion.4
  47.6 3.6 %route_other.1 = (bf16[32,32,1024]{2,1,0:T(8,128)(2,1)}, bf16[3,512,128]{2,1,0:T(8,128)(2,1)}) custom-call(f32[8,128]{1,0:T(8,128)} %get-tuple-element.93.routes_ref, f32[8,128]{1,0:T(8,128)} %get-tuple-element.92.gates_ref, s32[1,64]{1,0:T(1,128)} %bitcast.26, s32[1,32]{1,0:T(1,128)} %bitcast.28, bf16[128,1024]{1,0:T(8,128)(2,1)} %get-tuple-element.91.tokens_ref, ...), custom_call_target="tpu_custom_call" | custom-call | flops 30000001024 | tf_op jit(solution)/shard_map/route_other/pallas_call | solution.py:100
  51.2 11.3 %collective-permute-start.6 = (bf16[3,48,1024]{2,1,0:T(8,128)(2,1)S(1)}, bf16[3,48,1024]{2,1,0:T(8,128)(2,1)}, u32[]{:S(2)}, u32[]{:S(2)}) collective-permute-start(bf16[3,48,1024]{2,1,0:T(8,128)(2,1)S(1)} %bitcast.18), channel_id=1, source_target_pairs={{0,6},{1,7},{2,4},{3,5},{4,2},{5,3},{6,0},{7,1},{8,14},{9,15},{10,... | collective-permute-start | bytes 884744 | tf_op jit(solution)/shard_map/ppermute | solution.py:211
  62.5 7.0 %collective-permute-start.5 = (bf16[3,48,1024]{2,1,0:T(8,128)(2,1)S(1)}, bf16[3,48,1024]{2,1,0:T(8,128)(2,1)}, u32[]{:S(2)}, u32[]{:S(2)}) collective-permute-start(bf16[3,48,1024]{2,1,0:T(8,128)(2,1)S(1)} %bitcast.19), channel_id=1, source_target_pairs={{0,4},{1,5},{2,6},{3,7},{4,0},{5,1},{6,2},{7,3},{8,12},{9,13},{10,... | collective-permute-start | bytes 884744 | tf_op jit(solution)/shard_map/ppermute | solution.py:211
  69.5 1.9 collective-permute-start.4
  71.5 0.0 all-to-all-done.arrived_ref.one_ref
  71.5 0.0 copy-start.6
  71.5 4.8 %collective-permute-start.3 = (bf16[1,3,48,1024]{3,2,1,0:T(8,128)(2,1)}, bf16[1,3,48,1024]{3,2,1,0:T(8,128)(2,1)S(1)}, u32[]{:S(2)}, u32[]{:S(2)}) collective-permute-start(bf16[1,3,48,1024]{3,2,1,0:T(8,128)(2,1)} %convert_element_type.34), channel_id=1, source_target_pairs={{0,256},{8,264},{16,272},{24,280},{32,288},{40,296},{48,304},{56,3... | collective-permute-start | bytes 884744 | tf_op jit(solution)/shard_map/ppermute | solution.py:25
  76.3 7.6 %all-to-all-start.1 = ((bf16[32,32,1024]{2,1,0:T(8,128)(2,1)}), bf16[32,32,1024]{2,1,0:T(8,128)(2,1)}, u32[]{:S(2)}, u32[]{:S(2)}) async-start(bf16[32,32,1024]{2,1,0:T(8,128)(2,1)} %get-tuple-element.50), calls=%async_computation.1 | async-start | bytes 4194304 | tf_op jit(solution)/shard_map/all_to_all | solution.py:333
  83.9 0.0 collective-permute-done.6.refs_3_
  84.0 3.3 %collective-permute-done.5.refs_2_ = bf16[3,48,1024]{2,1,0:T(8,128)(2,1)} collective-permute-done((bf16[3,48,1024]{2,1,0:T(8,128)(2,1)S(1)}, bf16[3,48,1024]{2,1,0:T(8,128)(2,1)}, u32[]{:S(2)}, u32[]{:S(2)}) %collective-permute-start.5) | collective-permute-done | bytes 294944 | tf_op jit(solution)/shard_map/ppermute | solution.py:211
  87.3 0.0 collective-permute-done.4.refs_1_
  87.3 4.0 %collective-permute-done.3 = bf16[1,3,48,1024]{3,2,1,0:T(8,128)(2,1)S(1)} collective-permute-done((bf16[1,3,48,1024]{3,2,1,0:T(8,128)(2,1)}, bf16[1,3,48,1024]{3,2,1,0:T(8,128)(2,1)S(1)}, u32[]{:S(2)}, u32[]{:S(2)}) %collective-permute-start.3) | collective-permute-done | bytes 294944 | tf_op jit(solution)/shard_map/ppermute | solution.py:25
  91.3 1.3 pad_maximum_fusion
  92.6 1.9 collective-permute-start.7
  94.5 2.8 %collective-permute-done.7.refs_4_ = bf16[4,3,48,1024]{3,2,1,0:T(8,128)(2,1)S(1)} collective-permute-done((bf16[4,3,48,1024]{3,2,1,0:T(8,128)(2,1)S(1)}, bf16[4,3,48,1024]{3,2,1,0:T(8,128)(2,1)S(1)}, u32[]{:S(2)}, u32[]{:S(2)}) %collective-permute-start.7) | collective-permute-done | bytes 1179680 | tf_op jit(solution)/shard_map/ppermute | solution.py:211
  97.4 1.0 copy-done.15
  98.4 3.2 %assemble.1.weights_ref = bf16[3,384,1024]{2,1,0:T(8,128)(2,1)} custom-call(bf16[3,48,1024]{2,1,0:T(8,128)(2,1)} %bitcast.21, bf16[3,48,1024]{2,1,0:T(8,128)(2,1)} %collective-permute-done.4.refs_1_, bf16[3,48,1024]{2,1,0:T(8,128)(2,1)} %collective-permute-done.5.refs_2_, bf16[3,48,1024]{2,1,0:T(8,128)(2,1)} %collective-permute-done.6.refs_3_, ...), custom_call_target="tpu_custom_call" | custom-call | flops 2000000000 | tf_op jit(solution)/shard_map/assemble/pallas_call | solution.py:222
  101.6 7.0 %expert_own.1 = (bf16[32,32,1024]{2,1,0:T(8,128)(2,1)}, bf16[512,1152]{1,0:T(8,128)(2,1)}) custom-call(bf16[32,32,1024]{2,1,0:T(8,128)(2,1)} %copy-done.6, bf16[3,384,1024]{2,1,0:T(8,128)(2,1)} %assemble.1.weights_ref), custom_call_target="tpu_custom_call" | custom-call | flops 27000000512 | tf_op jit(solution)/shard_map/expert_own/pallas_call | solution.py:142
  108.6 26.4 %all-to-all-done.1.arrived_ref.two_ref = bf16[32,32,1024]{2,1,0:T(8,128)(2,1)} async-done(((bf16[32,32,1024]{2,1,0:T(8,128)(2,1)}), bf16[32,32,1024]{2,1,0:T(8,128)(2,1)}, u32[]{:S(2)}, u32[]{:S(2)}) %all-to-all-start.1) | async-done | bytes 2097184 | tf_op jit(solution)/shard_map/all_to_all | solution.py:333
  135.0 6.8 %collective-permute-start.8 = (bf16[1,3,48,1024]{3,2,1,0:T(8,128)(2,1)}, bf16[1,3,48,1024]{3,2,1,0:T(8,128)(2,1)S(1)}, u32[]{:S(2)}, u32[]{:S(2)}) collective-permute-start(bf16[1,3,48,1024]{3,2,1,0:T(8,128)(2,1)} %convert_element_type.35), channel_id=1, source_target_pairs={{0,256},{8,264},{16,272},{24,280},{32,288},{40,296},{48,304},{56,3... | collective-permute-start | bytes 884744 | tf_op jit(solution)/shard_map/ppermute | solution.py:25
  141.8 7.0 %expert_other.1 = (bf16[32,32,1024]{2,1,0:T(8,128)(2,1)}, bf16[512,1152]{1,0:T(8,128)(2,1)}) custom-call(bf16[32,32,1024]{2,1,0:T(8,128)(2,1)} %all-to-all-done.1.arrived_ref.two_ref, bf16[3,384,1024]{2,1,0:T(8,128)(2,1)} %assemble.1.weights_ref), custom_call_target="tpu_custom_call" | custom-call | flops 10000000000 | tf_op jit(solution)/shard_map/expert_other/pallas_call | solution.py:142
  148.9 8.8 %all-to-all-start.2 = ((bf16[32,32,1024]{2,1,0:T(8,128)(2,1)}), bf16[32,32,1024]{2,1,0:T(8,128)(2,1)S(1)}, u32[]{:S(2)}, u32[]{:S(2)}) async-start(bf16[32,32,1024]{2,1,0:T(8,128)(2,1)} %get-tuple-element.63), calls=%async_computation.2 | async-start | bytes 4194304 | tf_op jit(solution)/shard_map/all_to_all | solution.py:333
  157.6 0.0 collective-permute-done.8
  157.6 7.0 %terms.1 = (bf16[3,192,1024]{2,1,0:T(8,128)(2,1)}, bf16[3,192,1024]{2,1,0:T(8,128)(2,1)}) custom-call(bf16[32,32,1024]{2,1,0:T(8,128)(2,1)} %copy-done.6, bf16[512,1152]{1,0:T(8,128)(2,1)} %get-tuple-element.64.one_act_ref, bf16[32,32,1024]{2,1,0:T(8,128)(2,1)} %all-to-all-done.1.arrived_ref.two_ref, bf16[512,1152]{1,0:T(8,128)(2,1)} %get-tuple-element.67.two_act_ref), custom_call_target="tpu_custom_call" | custom-call | flops 30000001024 | tf_op jit(solution)/shard_map/terms/pallas_call | solution.py:191
  164.7 1.9 collective-permute-start.9
  166.6 3.2 %collective-permute-done.9.given_ref = bf16[3,192,1024]{2,1,0:T(8,128)(2,1)} collective-permute-done((bf16[3,192,1024]{2,1,0:T(8,128)(2,1)}, bf16[3,192,1024]{2,1,0:T(8,128)(2,1)}, u32[]{:S(2)}, u32[]{:S(2)}) %collective-permute-start.9) | collective-permute-done | bytes 1179680 | tf_op jit(solution)/shard_map/ppermute | solution.py:211
  169.7 2.7 %pair.1 = (bf16[3,48,1024]{2,1,0:T(8,128)(2,1)}, bf16[3,48,1024]{2,1,0:T(8,128)(2,1)}, bf16[3,48,1024]{2,1,0:T(8,128)(2,1)}, bf16[3,48,1024]{2,1,0:T(8,128)(2,1)}) custom-call(bf16[3,192,1024]{2,1,0:T(8,128)(2,1)} %get-tuple-element.68.keep_ref, bf16[3,192,1024]{2,1,0:T(8,128)(2,1)} %collective-permute-done.9.given_ref), custom_call_target="tpu_custom_call" | custom-call | flops 2000000000 | tf_op jit(solution)/shard_map/pair/pallas_call | solution.py:244
  172.5 2.3 collective-permute-start.10
  174.8 6.5 %collective-permute-start.11 = (bf16[3,48,1024]{2,1,0:T(8,128)(2,1)}, bf16[3,48,1024]{2,1,0:T(8,128)(2,1)}, u32[]{:S(2)}, u32[]{:S(2)}) collective-permute-start(bf16[3,48,1024]{2,1,0:T(8,128)(2,1)} %get-tuple-element.76), channel_id=1, source_target_pairs={{0,4},{1,5},{2,6},{3,7},{4,0},{5,1},{6,2},{7,3},{8,12},{9,13},{10,... | collective-permute-start | bytes 884744 | tf_op jit(solution)/shard_map/ppermute | solution.py:211
  181.3 1.9 collective-permute-start.12
  183.3 24.4 %all-to-all-done.2.back_ref = bf16[32,32,1024]{2,1,0:T(8,128)(2,1)S(1)} async-done(((bf16[32,32,1024]{2,1,0:T(8,128)(2,1)}), bf16[32,32,1024]{2,1,0:T(8,128)(2,1)S(1)}, u32[]{:S(2)}, u32[]{:S(2)}) %all-to-all-start.2) | async-done | bytes 2097184 | tf_op jit(solution)/shard_map/all_to_all | solution.py:333
  207.7 6.1 %all-to-all-start.3 = ((bf16[32,32,1024]{2,1,0:T(8,128)(2,1)}), bf16[32,32,1024]{2,1,0:T(8,128)(2,1)}, u32[]{:S(2)}, u32[]{:S(2)}) async-start(bf16[32,32,1024]{2,1,0:T(8,128)(2,1)} %get-tuple-element.71), calls=%async_computation.3 | async-start | bytes 4194304 | tf_op jit(solution)/shard_map/all_to_all | solution.py:333
  213.8 0.0 collective-permute-done.10
  213.8 0.0 collective-permute-done.11
  213.8 0.0 collective-permute-done.12
  213.8 0.0 copy-start.2
  213.8 0.0 copy-start.5
  213.9 0.0 copy-start.9
  213.9 0.6 share.1
  214.5 9.1 %collective-permute-start.13 = (bf16[256,1024]{1,0:T(8,128)(2,1)S(1)}, bf16[256,1024]{1,0:T(8,128)(2,1)S(1)}, u32[]{:S(2)}, u32[]{:S(2)}) collective-permute-start(bf16[256,1024]{1,0:T(8,128)(2,1)S(1)} %share.1), channel_id=1, source_target_pairs={{0,32},{8,40},{16,48},{24,56},{32,0},{40,8},{48,16},{56,24},{64,96... | collective-permute-start | bytes 1572872 | tf_op jit(solution)/shard_map/ppermute | solution.py:25
  223.7 2.7 %subtract_convert_fusion = (bf16[1,3,48,1024]{3,2,1,0:T(8,128)(2,1)}, f32[1,3,48,1024]{3,2,1,0:T(8,128)}, f32[1,3,48,1024]{3,2,1,0:T(8,128)}) fusion(bf16[1,3,48,1024]{3,2,1,0:T(8,128)(2,1)S(1)} %copy-done.2, bf16[3,48,1024]{2,1,0:T(8,128)(2,1)} %collective-permute-done.12, bf16[3,48,1024]{2,1,0:T(8,128)(2,1)} %collective-permute-done.11, ...), kind=kLoop, calls=%fused_computation.5 | loop fusion | flops 3686400 | bytes 4718593 | tf_op jit(solution)/shard_map/convert_element_type | solution.py:316
  226.4 7.6 %collective-permute-done.13.share_ref = bf16[256,1024]{1,0:T(8,128)(2,1)S(1)} collective-permute-done((bf16[256,1024]{1,0:T(8,128)(2,1)S(1)}, bf16[256,1024]{1,0:T(8,128)(2,1)S(1)}, u32[]{:S(2)}, u32[]{:S(2)}) %collective-permute-start.13) | collective-permute-done | bytes 524320 | tf_op jit(solution)/shard_map/ppermute | solution.py:25
  234.0 28.8 %all-to-all-done.3.back_ref = bf16[32,32,1024]{2,1,0:T(8,128)(2,1)} async-done(((bf16[32,32,1024]{2,1,0:T(8,128)(2,1)}), bf16[32,32,1024]{2,1,0:T(8,128)(2,1)}, u32[]{:S(2)}, u32[]{:S(2)}) %all-to-all-start.3) | async-done | bytes 2097184 | tf_op jit(solution)/shard_map/all_to_all | solution.py:333
  262.8 3.2 %combine.1 = (bf16[128,1024]{1,0:T(8,128)(2,1)}, bf16[128,1024]{1,0:T(8,128)(2,1)}) custom-call(bf16[32,32,1024]{2,1,0:T(8,128)(2,1)} %all-to-all-done.3.back_ref, bf16[3,512,128]{2,1,0:T(8,128)(2,1)} %get-tuple-element.72.mats_ref, bf16[256,1024]{1,0:T(8,128)(2,1)} %copy-done.16), custom_call_target="tpu_custom_call" | custom-call | flops 10000000000 | tf_op jit(solution)/shard_map/combine/pallas_call | solution.py:292
  (28 shorter events, 0.1 us)
Async XLA Ops:
  0.6 20.3 %collective-permute-start = (bf16[1,3,48,1024]{3,2,1,0:T(8,128)(2,1)}, bf16[1,3,48,1024]{3,2,1,0:T(8,128)(2,1)}, u32[]{:S(2)}, u32[]{:S(2)}) collective-permute-start(bf16[1,3,48,1024]{3,2,1,0:T(8,128)(2,1)} %param.15), channel_id=1, source_target_pairs={{0,256},{8,264},{16,272},{24,280},{32,288},{40,296},{48,304},{56,3... | collective-permute-start | bytes 884744 | tf_op jit(solution)/shard_map/ppermute | solution.py:25
  10.2 9.3 %copy-start.13 = (s32[128,8]{0,1:T(8,128)S(1)}, s32[128,8]{0,1:T(8,128)}, u32[]{:S(2)}) copy-start(s32[128,8]{0,1:T(8,128)} %param.11) | copy-start | bytes 12292
  10.2 9.3 %copy-start.17 = (s32[32]{0:T(128)S(1)}, s32[32]{0:T(128)}, u32[]{:S(2)}) copy-start(s32[32]{0:T(128)} %param.14) | copy-start | bytes 388
  10.2 10.6 %copy-start.14 = (f32[128,8]{0,1:T(8,128)S(1)}, f32[128,8]{0,1:T(8,128)}, u32[]{:S(2)}) copy-start(f32[128,8]{0,1:T(8,128)} %param.10) | copy-start | bytes 12292
  10.2 10.6 %copy-start.11 = (bf16[128,1024]{1,0:T(8,128)(2,1)S(1)}, bf16[128,1024]{1,0:T(8,128)(2,1)}, u32[]{:S(2)}) copy-start(bf16[128,1024]{1,0:T(8,128)(2,1)} %tokens_ref.1) | copy-start | bytes 786436
  10.2 10.6 %copy-start.12 = (bf16[128,1024]{1,0:T(8,128)(2,1)S(1)}, bf16[128,1024]{1,0:T(8,128)(2,1)}, u32[]{:S(2)}) copy-start(bf16[128,1024]{1,0:T(8,128)(2,1)} %cotangent_ref.1) | copy-start | bytes 786436
  10.2 61.3 %all-to-all-start = ((bf16[32,32,1024]{2,1,0:T(8,128)(2,1)}), bf16[32,32,1024]{2,1,0:T(8,128)(2,1)S(1)}, u32[]{:S(2)}, u32[]{:S(2)}) async-start(bf16[32,32,1024]{2,1,0:T(8,128)(2,1)} %get-tuple-element.46), calls=%async_computation | async-start | bytes 4194304 | tf_op jit(solution)/shard_map/all_to_all | solution.py:333
  19.4 1.5 copy-start.10
  19.4 17.0 %copy-start.3 = (f32[1,3,48,1024]{3,2,1,0:T(8,128)S(1)}, f32[1,3,48,1024]{3,2,1,0:T(8,128)}, u32[]{:S(2)}) copy-start(f32[1,3,48,1024]{3,2,1,0:T(8,128)} %param.16) | copy-start | bytes 1769476
  20.8 16.4 %copy-start.4 = (f32[1,3,48,1024]{3,2,1,0:T(8,128)S(1)}, f32[1,3,48,1024]{3,2,1,0:T(8,128)}, u32[]{:S(2)}) copy-start(f32[1,3,48,1024]{3,2,1,0:T(8,128)} %param.17) | copy-start | bytes 1769476
  20.9 70.4 %copy-start.1 = (bf16[1,3,48,1024]{3,2,1,0:T(8,128)(2,1)}, bf16[1,3,48,1024]{3,2,1,0:T(8,128)(2,1)S(1)}, u32[]{:S(2)}) copy-start(bf16[1,3,48,1024]{3,2,1,0:T(8,128)(2,1)S(1)} %broadcast_select_fusion) | copy-start | bytes 884740
  20.9 25.9 %collective-permute-start.2 = (bf16[256,1024]{1,0:T(8,128)(2,1)S(1)}, bf16[256,1024]{1,0:T(8,128)(2,1)S(1)}, u32[]{:S(2)}, u32[]{:S(2)}) collective-permute-start(bf16[256,1024]{1,0:T(8,128)(2,1)S(1)} %pad_maximum_fusion.1), channel_id=1, source_target_pairs={{0,32},{8,40},{16,48},{24,56},{32,0},{40,8},{48,16},{56,24},{64,96... | collective-permute-start | bytes 1572872 | tf_op jit(solution)/shard_map/ppermute | solution.py:25
  34.5 11.7 %collective-permute-start.1 = (f32[16,128]{1,0:T(8,128)S(1)}, f32[16,128]{1,0:T(8,128)S(1)}, u32[]{:S(2)}, u32[]{:S(2)}) collective-permute-start(f32[16,128]{1,0:T(8,128)S(1)} %pad_maximum_fusion.2), channel_id=1, source_target_pairs={{0,32},{8,40},{16,48},{24,56},{32,0},{40,8},{48,16},{56,24},{64,96... | collective-permute-start | bytes 24584 | tf_op jit(solution)/shard_map/ppermute | solution.py:25
  51.2 32.7 %collective-permute-start.6 = (bf16[3,48,1024]{2,1,0:T(8,128)(2,1)S(1)}, bf16[3,48,1024]{2,1,0:T(8,128)(2,1)}, u32[]{:S(2)}, u32[]{:S(2)}) collective-permute-start(bf16[3,48,1024]{2,1,0:T(8,128)(2,1)S(1)} %bitcast.18), channel_id=1, source_target_pairs={{0,6},{1,7},{2,4},{3,5},{4,2},{5,3},{6,0},{7,1},{8,14},{9,15},{10,... | collective-permute-start | bytes 884744 | tf_op jit(solution)/shard_map/ppermute | solution.py:211
  62.5 24.8 %collective-permute-start.5 = (bf16[3,48,1024]{2,1,0:T(8,128)(2,1)S(1)}, bf16[3,48,1024]{2,1,0:T(8,128)(2,1)}, u32[]{:S(2)}, u32[]{:S(2)}) collective-permute-start(bf16[3,48,1024]{2,1,0:T(8,128)(2,1)S(1)} %bitcast.19), channel_id=1, source_target_pairs={{0,4},{1,5},{2,6},{3,7},{4,0},{5,1},{6,2},{7,3},{8,12},{9,13},{10,... | collective-permute-start | bytes 884744 | tf_op jit(solution)/shard_map/ppermute | solution.py:211
  69.5 17.7 %collective-permute-start.4 = (bf16[3,48,1024]{2,1,0:T(8,128)(2,1)S(1)}, bf16[3,48,1024]{2,1,0:T(8,128)(2,1)}, u32[]{:S(2)}, u32[]{:S(2)}) collective-permute-start(bf16[3,48,1024]{2,1,0:T(8,128)(2,1)S(1)} %bitcast.20), channel_id=1, source_target_pairs={{0,2},{1,3},{2,0},{3,1},{4,6},{5,7},{6,4},{7,5},{8,10},{9,11},{10,... | collective-permute-start | bytes 884744 | tf_op jit(solution)/shard_map/ppermute | solution.py:211
  71.5 4.8 %copy-start.6 = (bf16[32,32,1024]{2,1,0:T(8,128)(2,1)}, bf16[32,32,1024]{2,1,0:T(8,128)(2,1)S(1)}, u32[]{:S(2)}) copy-start(bf16[32,32,1024]{2,1,0:T(8,128)(2,1)S(1)} %all-to-all-done.arrived_ref.one_ref) | copy-start | bytes 6291460
  71.5 19.8 %collective-permute-start.3 = (bf16[1,3,48,1024]{3,2,1,0:T(8,128)(2,1)}, bf16[1,3,48,1024]{3,2,1,0:T(8,128)(2,1)S(1)}, u32[]{:S(2)}, u32[]{:S(2)}) collective-permute-start(bf16[1,3,48,1024]{3,2,1,0:T(8,128)(2,1)} %convert_element_type.34), channel_id=1, source_target_pairs={{0,256},{8,264},{16,272},{24,280},{32,288},{40,296},{48,304},{56,3... | collective-permute-start | bytes 884744 | tf_op jit(solution)/shard_map/ppermute | solution.py:25
  76.3 58.7 %all-to-all-start.1 = ((bf16[32,32,1024]{2,1,0:T(8,128)(2,1)}), bf16[32,32,1024]{2,1,0:T(8,128)(2,1)}, u32[]{:S(2)}, u32[]{:S(2)}) async-start(bf16[32,32,1024]{2,1,0:T(8,128)(2,1)} %get-tuple-element.50), calls=%async_computation.1 | async-start | bytes 4194304 | tf_op jit(solution)/shard_map/all_to_all | solution.py:333
  92.6 4.7 %collective-permute-start.7 = (bf16[4,3,48,1024]{3,2,1,0:T(8,128)(2,1)S(1)}, bf16[4,3,48,1024]{3,2,1,0:T(8,128)(2,1)S(1)}, u32[]{:S(2)}, u32[]{:S(2)}) collective-permute-start(bf16[4,3,48,1024]{3,2,1,0:T(8,128)(2,1)S(1)} %pad_maximum_fusion), channel_id=1, source_target_pairs={{0,1},{1,0},{2,3},{3,2},{4,5},{5,4},{6,7},{7,6},{8,9},{9,8},{10,11... | collective-permute-start | bytes 3538952 | tf_op jit(solution)/shard_map/ppermute | solution.py:211
  97.4 1.0 copy-start.15
  135.0 22.6 %collective-permute-start.8 = (bf16[1,3,48,1024]{3,2,1,0:T(8,128)(2,1)}, bf16[1,3,48,1024]{3,2,1,0:T(8,128)(2,1)S(1)}, u32[]{:S(2)}, u32[]{:S(2)}) collective-permute-start(bf16[1,3,48,1024]{3,2,1,0:T(8,128)(2,1)} %convert_element_type.35), channel_id=1, source_target_pairs={{0,256},{8,264},{16,272},{24,280},{32,288},{40,296},{48,304},{56,3... | collective-permute-start | bytes 884744 | tf_op jit(solution)/shard_map/ppermute | solution.py:25
  148.9 58.8 %all-to-all-start.2 = ((bf16[32,32,1024]{2,1,0:T(8,128)(2,1)}), bf16[32,32,1024]{2,1,0:T(8,128)(2,1)S(1)}, u32[]{:S(2)}, u32[]{:S(2)}) async-start(bf16[32,32,1024]{2,1,0:T(8,128)(2,1)} %get-tuple-element.63), calls=%async_computation.2 | async-start | bytes 4194304 | tf_op jit(solution)/shard_map/all_to_all | solution.py:333
  157.6 7.0 %copy-start.7 = (bf16[1,3,48,1024]{3,2,1,0:T(8,128)(2,1)}, bf16[1,3,48,1024]{3,2,1,0:T(8,128)(2,1)S(1)}, u32[]{:S(2)}) copy-start(bf16[1,3,48,1024]{3,2,1,0:T(8,128)(2,1)S(1)} %collective-permute-done.8) | copy-start | bytes 884740
  164.7 5.1 %collective-permute-start.9 = (bf16[3,192,1024]{2,1,0:T(8,128)(2,1)}, bf16[3,192,1024]{2,1,0:T(8,128)(2,1)}, u32[]{:S(2)}, u32[]{:S(2)}) collective-permute-start(bf16[3,192,1024]{2,1,0:T(8,128)(2,1)} %get-tuple-element.69), channel_id=1, source_target_pairs={{0,1},{1,0},{2,3},{3,2},{4,5},{5,4},{6,7},{7,6},{8,9},{9,8},{10,11... | collective-permute-start | bytes 3538952 | tf_op jit(solution)/shard_map/ppermute | solution.py:211
  172.5 41.3 %collective-permute-start.10 = (bf16[3,48,1024]{2,1,0:T(8,128)(2,1)}, bf16[3,48,1024]{2,1,0:T(8,128)(2,1)}, u32[]{:S(2)}, u32[]{:S(2)}) collective-permute-start(bf16[3,48,1024]{2,1,0:T(8,128)(2,1)} %get-tuple-element.75), channel_id=1, source_target_pairs={{0,2},{1,3},{2,0},{3,1},{4,6},{5,7},{6,4},{7,5},{8,10},{9,11},{10,... | collective-permute-start | bytes 884744 | tf_op jit(solution)/shard_map/ppermute | solution.py:211
  174.8 39.0 %collective-permute-start.11 = (bf16[3,48,1024]{2,1,0:T(8,128)(2,1)}, bf16[3,48,1024]{2,1,0:T(8,128)(2,1)}, u32[]{:S(2)}, u32[]{:S(2)}) collective-permute-start(bf16[3,48,1024]{2,1,0:T(8,128)(2,1)} %get-tuple-element.76), channel_id=1, source_target_pairs={{0,4},{1,5},{2,6},{3,7},{4,0},{5,1},{6,2},{7,3},{8,12},{9,13},{10,... | collective-permute-start | bytes 884744 | tf_op jit(solution)/shard_map/ppermute | solution.py:211
  181.3 32.5 %collective-permute-start.12 = (bf16[3,48,1024]{2,1,0:T(8,128)(2,1)}, bf16[3,48,1024]{2,1,0:T(8,128)(2,1)}, u32[]{:S(2)}, u32[]{:S(2)}) collective-permute-start(bf16[3,48,1024]{2,1,0:T(8,128)(2,1)} %get-tuple-element.77), channel_id=1, source_target_pairs={{0,6},{1,7},{2,4},{3,5},{4,2},{5,3},{6,0},{7,1},{8,14},{9,15},{10,... | collective-permute-start | bytes 884744 | tf_op jit(solution)/shard_map/ppermute | solution.py:211
  207.7 6.2 %copy-start = (bf16[3,512,128]{2,1,0:T(8,128)(2,1)S(1)}, bf16[3,512,128]{2,1,0:T(8,128)(2,1)}, u32[]{:S(2)}) copy-start(bf16[3,512,128]{2,1,0:T(8,128)(2,1)} %get-tuple-element.78.mats_ref) | copy-start | bytes 1179652
  207.7 55.1 %all-to-all-start.3 = ((bf16[32,32,1024]{2,1,0:T(8,128)(2,1)}), bf16[32,32,1024]{2,1,0:T(8,128)(2,1)}, u32[]{:S(2)}, u32[]{:S(2)}) async-start(bf16[32,32,1024]{2,1,0:T(8,128)(2,1)} %get-tuple-element.71), calls=%async_computation.3 | async-start | bytes 4194304 | tf_op jit(solution)/shard_map/all_to_all | solution.py:333
  213.8 9.8 %copy-start.2 = (bf16[1,3,48,1024]{3,2,1,0:T(8,128)(2,1)S(1)}, bf16[1,3,48,1024]{3,2,1,0:T(8,128)(2,1)}, u32[]{:S(2)}) copy-start(bf16[1,3,48,1024]{3,2,1,0:T(8,128)(2,1)} %copy-done.1) | copy-start | bytes 884740
  213.8 9.8 %copy-start.5 = (f32[1,3,48,1024]{3,2,1,0:T(8,128)S(1)}, f32[1,3,48,1024]{3,2,1,0:T(8,128)}, u32[]{:S(2)}) copy-start(f32[1,3,48,1024]{3,2,1,0:T(8,128)} %param.17) | copy-start | bytes 1769476
  213.9 9.8 %copy-start.8 = (bf16[1,3,48,1024]{3,2,1,0:T(8,128)(2,1)S(1)}, bf16[1,3,48,1024]{3,2,1,0:T(8,128)(2,1)}, u32[]{:S(2)}) copy-start(bf16[1,3,48,1024]{3,2,1,0:T(8,128)(2,1)} %copy-done.7) | copy-start | bytes 884740
  213.9 9.8 %copy-start.9 = (bf16[3,48,1024]{2,1,0:T(8,128)(2,1)S(1)}, bf16[3,48,1024]{2,1,0:T(8,128)(2,1)}, u32[]{:S(2)}) copy-start(bf16[3,48,1024]{2,1,0:T(8,128)(2,1)} %get-tuple-element.82) | copy-start | bytes 884740
  214.5 19.5 %collective-permute-start.13 = (bf16[256,1024]{1,0:T(8,128)(2,1)S(1)}, bf16[256,1024]{1,0:T(8,128)(2,1)S(1)}, u32[]{:S(2)}, u32[]{:S(2)}) collective-permute-start(bf16[256,1024]{1,0:T(8,128)(2,1)S(1)} %share.1), channel_id=1, source_target_pairs={{0,32},{8,40},{16,48},{24,56},{32,0},{40,8},{48,16},{56,24},{64,96... | collective-permute-start | bytes 1572872 | tf_op jit(solution)/shard_map/ppermute | solution.py:25
  234.0 28.8 %copy-start.16 = (bf16[256,1024]{1,0:T(8,128)(2,1)}, bf16[256,1024]{1,0:T(8,128)(2,1)S(1)}, u32[]{:S(2)}) copy-start(bf16[256,1024]{1,0:T(8,128)(2,1)S(1)} %collective-permute-done.13.share_ref) | copy-start | bytes 1572868

commit v6 on v5

--- a/solution.py
+++ b/solution.py
@@ -15,6 +15,7 @@
 VMEM_LIMIT = 60 * 1024 * 1024
 COST = {"route_own": 30, "route_other": 30, "expert_own": 27, "expert_other": 10, "terms": 30, "share": 36, "combine": 10, "assemble": 2, "pair": 2}
 PARAMS = pltpu.CompilerParams(vmem_limit_bytes=VMEM_LIMIT)
+SMALL = pltpu.CompilerParams(vmem_limit_bytes=24 * 1024 * 1024)
 
 
 def cost(name):
@@ -255,12 +256,12 @@
     capacity = double // 2
     out_rows = back_ref[:, :capacity, :].reshape(half * capacity, width)
     grad_rows = back_ref[:, capacity:, :].reshape(half * capacity, width)
-    out = dot_first(mats_ref[0], out_rows) + dot_first(mats_ref[1], out_rows)
-    return out, dot_first(mats_ref[2], grad_rows)
+    out = dot(mats_ref[0], out_rows) + dot(mats_ref[1], out_rows)
+    return out, dot(mats_ref[2], grad_rows)
 
 
 def share_kernel(back_ref, mats_ref, share_ref):
-    tok_rows = mats_ref.shape[2]
+    tok_rows = mats_ref.shape[1]
     out, grad = weighted_sums(back_ref, mats_ref)
     share_ref[:tok_rows] = out.astype(jnp.bfloat16)
     share_ref[tok_rows:] = grad.astype(jnp.bfloat16)
@@ -269,37 +270,26 @@
 def share(back, mats):
     return pl.pallas_call(
         share_kernel,
-        out_shape=jax.ShapeDtypeStruct((2 * mats.shape[2], back.shape[2]), jnp.bfloat16),
-        compiler_params=pltpu.CompilerParams(vmem_limit_bytes=24 * 1024 * 1024),
+        out_shape=jax.ShapeDtypeStruct((2 * mats.shape[1], back.shape[2]), jnp.bfloat16),
+        compiler_params=SMALL,
         cost_estimate=cost("share"),
         name="share",
     )(back, mats)
 
 
 def combine_kernel(back_ref, mats_ref, share_ref, out_ref, grad_ref):
-    tok_rows = mats_ref.shape[2]
+    tok_rows = mats_ref.shape[1]
     out, grad = weighted_sums(back_ref, mats_ref)
     out_ref[...] = (out + share_ref[:tok_rows].astype(jnp.float32)).astype(jnp.bfloat16)
     grad_ref[...] = (grad + share_ref[tok_rows:].astype(jnp.float32)).astype(jnp.bfloat16)
 
 
 def combine(back, mats, other_share):
-    half, double, width = back.shape
-    tok_rows = mats.shape[2]
-    shape = jax.ShapeDtypeStruct((tok_rows, width), jnp.bfloat16)
-    block = width // 2
-    out_spec = pl.BlockSpec((tok_rows, block), lambda i: (0, i))
+    shape = jax.ShapeDtypeStruct((mats.shape[1], back.shape[2]), jnp.bfloat16)
     return pl.pallas_call(
         combine_kernel,
-        grid=(2,),
-        in_specs=[
-            pl.BlockSpec((half, double, block), lambda i: (0, 0, i)),
-            pl.BlockSpec(mats.shape, lambda i: (0, 0, 0)),
-            pl.BlockSpec((2 * tok_rows, block), lambda i: (0, i)),
-        ],
-        out_specs=(out_spec, out_spec),
         out_shape=(shape, shape),
-        compiler_params=PARAMS,
+        compiler_params=SMALL,
         cost_estimate=cost("combine"),
         name="combine",
     )(back, mats, other_share)
@@ -372,14 +362,16 @@
     own_returned = exchange(own_back)
 
     sums = [sums[0]] + [move_hidden(sums[dz], 2 * dz) for dz in range(1, len(sums))]
-    other_mats, *sums = lax.optimization_barrier((other_mats, *sums))
+    other_mats, *sums = lax.optimization_barrier((jnp.swapaxes(other_mats, 1, 2), *sums))
     gradient = sum(part.astype(jnp.float32) for part in sums)[None]
     first_moment = jnp.where(is_swapped, other_first.astype(jnp.float32), first_moment)
     second_moment = jnp.where(is_swapped, other_second.astype(jnp.float32), second_moment)
     new_weights, new_first, new_second = adam_update(weights, first_moment, second_moment, gradient)
 
     other_share = partner(share(other_returned, other_mats), X_SIZE)
-    layer_output_rows, token_gradient_rows = combine(own_returned, own_mats, other_share)
+    layer_output_rows, token_gradient_rows = combine(
+        own_returned, jnp.swapaxes(own_mats, 1, 2), other_share
+    )
     return (layer_output_rows, token_gradient_rows, new_weights, new_first, new_second)
 
 

time: 267 us -> 267 us (level)
  local copies, waits for them, and re-layouts: 2.53 us -> 5.62 us
  waiting for transfers between devices: 109 us -> 106 us
  transfers between devices with their start and end apart: 18 -> 18, of which waited for: 9 -> 9; matrix products, arithmetic and copies ran while one was open for 3% -> 4% of each run, Pallas kernels for 13% -> 13%
where the time goes in v6:
time: 267 us; the launch traced here: 266 us
  starting transfers between devices  108 us (40%)
  waiting for transfers between devices  106 us (40%)
  Pallas kernels  37.5 us (14%)
  other arithmetic  7.42 us (3%)
  local copies, waits for them, and re-layouts  5.62 us (2%)
    all_to_all x4, waiting for transfers between devices, exchange(): lax.all_to_all(rows, 'ep', split_axis=0, concat_axis=0, tiled=True, axis_...  78.5 us
    ppermute x6, starting transfers between devices, partner(): lax.ppermute(array, 'ep', [(i, i ^ apart) for i in range(lax.axis_size('e...  41.9 us
    ppermute x8, starting transfers between devices, move_hidden(): lax.ppermute(array, 'tp', [(i, i ^ apart) for i in range(lax.axis_size('t...  34.5 us
    all_to_all x4, starting transfers between devices, exchange(): lax.all_to_all(rows, 'ep', split_axis=0, concat_axis=0, tiled=True, axis_...  31.3 us
    ppermute x6, waiting for transfers between devices, partner(): lax.ppermute(array, 'ep', [(i, i ^ apart) for i in range(lax.axis_size('e...  18.4 us
    pallas_call x2, Pallas kernels, expert(): pl.pallas_call(expert_kernel, grid=(steps,), in_specs=[pl.BlockSpec((bloc...  14 us
    ppermute x8, waiting for transfers between devices, move_hidden(): lax.ppermute(array, 'tp', [(i, i ^ apart) for i in range(lax.axis_size('t...  8.77 us
    pallas_call x2, Pallas kernels, route(): pl.pallas_call(route_kernel, out_shape=(jax.ShapeDtypeStruct((half, 2 * c...  7.11 us
  transfers between devices with their start and end apart: 18, of which 9 were waited for; matrix products, arithmetic and copies ran while one was open for 4% of the time, Pallas kernels for 13%

profile of v6, /device:TPU:16, one launch (start us, length us, event | category | flops | bytes accessed | tf_op | source)
XLA Modules:
  0.0 265.8 jit_solution(2715287138845908346)
XLA Ops:
  0.6 5.9 %collective-permute-start = (bf16[1,3,48,1024]{3,2,1,0:T(8,128)(2,1)}, bf16[1,3,48,1024]{3,2,1,0:T(8,128)(2,1)}, u32[]{:S(2)}, u32[]{:S(2)}) collective-permute-start(bf16[1,3,48,1024]{3,2,1,0:T(8,128)(2,1)} %param.15), channel_id=1, source_target_pairs={{0,256},{8,264},{16,272},{24,280},{32,288},{40,296},{48,304},{56,3... | collective-permute-start | bytes 884744 | tf_op jit(solution)/shard_map/ppermute | solution.py:26
  6.6 3.6 %route_own.1 = (bf16[32,32,1024]{2,1,0:T(8,128)(2,1)}, bf16[3,512,128]{2,1,0:T(8,128)(2,1)}) custom-call(s32[8,128]{1,0:T(8,128)} %bitcast.28, f32[8,128]{1,0:T(8,128)} %bitcast.29, s32[1,64]{1,0:T(1,128)} %bitcast.31, s32[1,32]{1,0:T(1,128)} %bitcast.33, bf16[128,1024]{1,0:T(8,128)(2,1)} %tokens_ref.1, bf16[128,1024]{1,0:T(8,128)(2,1)} %cotangent_ref.1), custom_call_target="tpu_custom_call" | custom-call | flops 30000001024 | tf_op jit(solution)/shard_map/route_own/pallas_call | solution.py:101
  10.2 0.0 copy-start.14
  10.2 0.0 copy-start.15
  10.2 9.2 %all-to-all-start = ((bf16[32,32,1024]{2,1,0:T(8,128)(2,1)}), bf16[32,32,1024]{2,1,0:T(8,128)(2,1)S(1)}, u32[]{:S(2)}, u32[]{:S(2)}) async-start(bf16[32,32,1024]{2,1,0:T(8,128)(2,1)} %get-tuple-element.46), calls=%async_computation | async-start | bytes 4194304 | tf_op jit(solution)/shard_map/all_to_all | solution.py:323
  19.4 0.0 copy-start.12
  19.4 0.0 copy-start.2
  19.5 0.6 fusion.2
  20.8 0.0 copy-start.4
  20.9 0.0 collective-permute-done
  20.9 1.0 broadcast_select_fusion
  21.9 0.0 copy-start
  21.9 12.5 %collective-permute-start.2 = (bf16[256,1024]{1,0:T(8,128)(2,1)S(1)}, bf16[256,1024]{1,0:T(8,128)(2,1)S(1)}, u32[]{:S(2)}, u32[]{:S(2)}) collective-permute-start(bf16[256,1024]{1,0:T(8,128)(2,1)S(1)} %pad_maximum_fusion.1), channel_id=1, source_target_pairs={{0,32},{8,40},{16,48},{24,56},{32,0},{40,8},{48,16},{56,24},{64,96... | collective-permute-start | bytes 1572872 | tf_op jit(solution)/shard_map/ppermute | solution.py:26
  34.5 1.9 collective-permute-start.1
  36.4 0.8 convert_element_type.34
  37.2 0.8 convert_element_type.35
  37.9 8.3 %collective-permute-done.1 = f32[16,128]{1,0:T(8,128)S(1)} collective-permute-done((f32[16,128]{1,0:T(8,128)S(1)}, f32[16,128]{1,0:T(8,128)S(1)}, u32[]{:S(2)}, u32[]{:S(2)}) %collective-permute-start.1) | collective-permute-done | bytes 8224 | tf_op jit(solution)/shard_map/ppermute | solution.py:26
  46.2 0.6 fusion.5
  46.8 0.0 collective-permute-done.2
  46.8 0.8 fusion.4
  47.6 3.5 %route_other.1 = (bf16[32,32,1024]{2,1,0:T(8,128)(2,1)}, bf16[3,512,128]{2,1,0:T(8,128)(2,1)}) custom-call(f32[8,128]{1,0:T(8,128)} %get-tuple-element.93.routes_ref, f32[8,128]{1,0:T(8,128)} %get-tuple-element.92.gates_ref, s32[1,64]{1,0:T(1,128)} %bitcast.32, s32[1,32]{1,0:T(1,128)} %bitcast.34, bf16[128,1024]{1,0:T(8,128)(2,1)} %get-tuple-element.91.tokens_ref, ...), custom_call_target="tpu_custom_call" | custom-call | flops 30000001024 | tf_op jit(solution)/shard_map/route_other/pallas_call | solution.py:101
  51.2 11.3 %collective-permute-start.6 = (bf16[3,48,1024]{2,1,0:T(8,128)(2,1)S(1)}, bf16[3,48,1024]{2,1,0:T(8,128)(2,1)S(1)}, u32[]{:S(2)}, u32[]{:S(2)}) collective-permute-start(bf16[3,48,1024]{2,1,0:T(8,128)(2,1)S(1)} %bitcast.22), channel_id=1, source_target_pairs={{0,6},{1,7},{2,4},{3,5},{4,2},{5,3},{6,0},{7,1},{8,14},{9,15},{10,... | collective-permute-start | bytes 884744 | tf_op jit(solution)/shard_map/ppermute | solution.py:212
  62.4 7.0 %collective-permute-start.5 = (bf16[3,48,1024]{2,1,0:T(8,128)(2,1)S(1)}, bf16[3,48,1024]{2,1,0:T(8,128)(2,1)S(1)}, u32[]{:S(2)}, u32[]{:S(2)}) collective-permute-start(bf16[3,48,1024]{2,1,0:T(8,128)(2,1)S(1)} %bitcast.23), channel_id=1, source_target_pairs={{0,4},{1,5},{2,6},{3,7},{4,0},{5,1},{6,2},{7,3},{8,12},{9,13},{10,... | collective-permute-start | bytes 884744 | tf_op jit(solution)/shard_map/ppermute | solution.py:212
  69.5 1.9 collective-permute-start.4
  71.4 0.0 all-to-all-done.arrived_ref.one_ref
  71.4 4.8 %collective-permute-start.3 = (bf16[1,3,48,1024]{3,2,1,0:T(8,128)(2,1)}, bf16[1,3,48,1024]{3,2,1,0:T(8,128)(2,1)S(1)}, u32[]{:S(2)}, u32[]{:S(2)}) collective-permute-start(bf16[1,3,48,1024]{3,2,1,0:T(8,128)(2,1)} %convert_element_type.34), channel_id=1, source_target_pairs={{0,256},{8,264},{16,272},{24,280},{32,288},{40,296},{48,304},{56,3... | collective-permute-start | bytes 884744 | tf_op jit(solution)/shard_map/ppermute | solution.py:26
  76.3 7.9 %all-to-all-start.1 = ((bf16[32,32,1024]{2,1,0:T(8,128)(2,1)}), bf16[32,32,1024]{2,1,0:T(8,128)(2,1)}, u32[]{:S(2)}, u32[]{:S(2)}) async-start(bf16[32,32,1024]{2,1,0:T(8,128)(2,1)} %get-tuple-element.50), calls=%async_computation.1 | async-start | bytes 4194304 | tf_op jit(solution)/shard_map/all_to_all | solution.py:323
  84.2 0.0 collective-permute-done.6.refs_3_
  84.2 2.9 %collective-permute-done.5.refs_2_ = bf16[3,48,1024]{2,1,0:T(8,128)(2,1)S(1)} collective-permute-done((bf16[3,48,1024]{2,1,0:T(8,128)(2,1)S(1)}, bf16[3,48,1024]{2,1,0:T(8,128)(2,1)S(1)}, u32[]{:S(2)}, u32[]{:S(2)}) %collective-permute-start.5) | collective-permute-done | bytes 294944 | tf_op jit(solution)/shard_map/ppermute | solution.py:212
  87.1 0.0 collective-permute-done.4.refs_1_
  87.1 3.9 %collective-permute-done.3 = bf16[1,3,48,1024]{3,2,1,0:T(8,128)(2,1)S(1)} collective-permute-done((bf16[1,3,48,1024]{3,2,1,0:T(8,128)(2,1)}, bf16[1,3,48,1024]{3,2,1,0:T(8,128)(2,1)S(1)}, u32[]{:S(2)}, u32[]{:S(2)}) %collective-permute-start.3) | collective-permute-done | bytes 294944 | tf_op jit(solution)/shard_map/ppermute | solution.py:26
  91.1 1.2 pad_maximum_fusion
  92.3 1.9 collective-permute-start.7
  94.3 2.8 %collective-permute-done.7.refs_4_ = bf16[4,3,48,1024]{3,2,1,0:T(8,128)(2,1)S(1)} collective-permute-done((bf16[4,3,48,1024]{3,2,1,0:T(8,128)(2,1)S(1)}, bf16[4,3,48,1024]{3,2,1,0:T(8,128)(2,1)S(1)}, u32[]{:S(2)}, u32[]{:S(2)}) %collective-permute-start.7) | collective-permute-done | bytes 1179680 | tf_op jit(solution)/shard_map/ppermute | solution.py:212
  97.1 1.0 copy-done.19
  98.1 3.2 %assemble.1.weights_ref = bf16[3,384,1024]{2,1,0:T(8,128)(2,1)} custom-call(bf16[3,48,1024]{2,1,0:T(8,128)(2,1)} %bitcast.25, bf16[3,48,1024]{2,1,0:T(8,128)(2,1)} %collective-permute-done.4.refs_1_, bf16[3,48,1024]{2,1,0:T(8,128)(2,1)} %copy-done.11, bf16[3,48,1024]{2,1,0:T(8,128)(2,1)} %copy-done.10, bf16[4,3,48,1024]{3,2,1,0:T(8,128)(2,1)} %copy-done.19), custom_call_target="tpu_custom_call" | custom-call | flops 2000000000 | tf_op jit(solution)/shard_map/assemble/pallas_call | solution.py:223
  101.3 7.0 %expert_own.1 = (bf16[32,32,1024]{2,1,0:T(8,128)(2,1)}, bf16[512,1152]{1,0:T(8,128)(2,1)}) custom-call(bf16[32,32,1024]{2,1,0:T(8,128)(2,1)} %copy-done.5, bf16[3,384,1024]{2,1,0:T(8,128)(2,1)} %assemble.1.weights_ref), custom_call_target="tpu_custom_call" | custom-call | flops 27000000512 | tf_op jit(solution)/shard_map/expert_own/pallas_call | solution.py:143
  108.3 27.0 %all-to-all-done.1.arrived_ref.two_ref = bf16[32,32,1024]{2,1,0:T(8,128)(2,1)} async-done(((bf16[32,32,1024]{2,1,0:T(8,128)(2,1)}), bf16[32,32,1024]{2,1,0:T(8,128)(2,1)}, u32[]{:S(2)}, u32[]{:S(2)}) %all-to-all-start.1) | async-done | bytes 2097184 | tf_op jit(solution)/shard_map/all_to_all | solution.py:323
  135.2 7.3 %collective-permute-start.8 = (bf16[1,3,48,1024]{3,2,1,0:T(8,128)(2,1)S(1)}, bf16[1,3,48,1024]{3,2,1,0:T(8,128)(2,1)S(1)}, u32[]{:S(2)}, u32[]{:S(2)}) collective-permute-start(bf16[1,3,48,1024]{3,2,1,0:T(8,128)(2,1)S(1)} %copy-done.13), channel_id=1, source_target_pairs={{0,256},{8,264},{16,272},{24,280},{32,288},{40,296},{48,304},{56,3... | collective-permute-start | bytes 884744 | tf_op jit(solution)/shard_map/ppermute | solution.py:26
  142.6 7.0 %expert_other.1 = (bf16[32,32,1024]{2,1,0:T(8,128)(2,1)}, bf16[512,1152]{1,0:T(8,128)(2,1)}) custom-call(bf16[32,32,1024]{2,1,0:T(8,128)(2,1)} %all-to-all-done.1.arrived_ref.two_ref, bf16[3,384,1024]{2,1,0:T(8,128)(2,1)} %assemble.1.weights_ref), custom_call_target="tpu_custom_call" | custom-call | flops 10000000000 | tf_op jit(solution)/shard_map/expert_other/pallas_call | solution.py:143
  149.5 8.1 %all-to-all-start.2 = ((bf16[32,32,1024]{2,1,0:T(8,128)(2,1)}), bf16[32,32,1024]{2,1,0:T(8,128)(2,1)S(1)}, u32[]{:S(2)}, u32[]{:S(2)}) async-start(bf16[32,32,1024]{2,1,0:T(8,128)(2,1)} %get-tuple-element.63), calls=%async_computation.2 | async-start | bytes 4194304 | tf_op jit(solution)/shard_map/all_to_all | solution.py:323
  157.7 0.0 collective-permute-done.8
  157.7 7.0 %terms.1 = (bf16[3,192,1024]{2,1,0:T(8,128)(2,1)}, bf16[3,192,1024]{2,1,0:T(8,128)(2,1)}) custom-call(bf16[32,32,1024]{2,1,0:T(8,128)(2,1)} %copy-done.5, bf16[512,1152]{1,0:T(8,128)(2,1)} %get-tuple-element.64.one_act_ref, bf16[32,32,1024]{2,1,0:T(8,128)(2,1)} %all-to-all-done.1.arrived_ref.two_ref, bf16[512,1152]{1,0:T(8,128)(2,1)} %get-tuple-element.67.two_act_ref), custom_call_target="tpu_custom_call" | custom-call | flops 30000001024 | tf_op jit(solution)/shard_map/terms/pallas_call | solution.py:192
  164.7 1.9 collective-permute-start.9
  166.6 3.0 %collective-permute-done.9.given_ref = bf16[3,192,1024]{2,1,0:T(8,128)(2,1)S(1)} collective-permute-done((bf16[3,192,1024]{2,1,0:T(8,128)(2,1)}, bf16[3,192,1024]{2,1,0:T(8,128)(2,1)S(1)}, u32[]{:S(2)}, u32[]{:S(2)}) %collective-permute-start.9) | collective-permute-done | bytes 1179680 | tf_op jit(solution)/shard_map/ppermute | solution.py:212
  169.7 1.0 copy-done.18
  170.7 2.8 %pair.1 = (bf16[3,48,1024]{2,1,0:T(8,128)(2,1)}, bf16[3,48,1024]{2,1,0:T(8,128)(2,1)}, bf16[3,48,1024]{2,1,0:T(8,128)(2,1)}, bf16[3,48,1024]{2,1,0:T(8,128)(2,1)}) custom-call(bf16[3,192,1024]{2,1,0:T(8,128)(2,1)} %get-tuple-element.68.keep_ref, bf16[3,192,1024]{2,1,0:T(8,128)(2,1)} %copy-done.18), custom_call_target="tpu_custom_call" | custom-call | flops 2000000000 | tf_op jit(solution)/shard_map/pair/pallas_call | solution.py:245
  173.5 2.8 %collective-permute-start.10 = (bf16[3,48,1024]{2,1,0:T(8,128)(2,1)}, bf16[3,48,1024]{2,1,0:T(8,128)(2,1)S(1)}, u32[]{:S(2)}, u32[]{:S(2)}) collective-permute-start(bf16[3,48,1024]{2,1,0:T(8,128)(2,1)} %get-tuple-element.75), channel_id=1, source_target_pairs={{0,2},{1,3},{2,0},{3,1},{4,6},{5,7},{6,4},{7,5},{8,10},{9,11},{10,... | collective-permute-start | bytes 884744 | tf_op jit(solution)/shard_map/ppermute | solution.py:212
  176.2 5.7 %collective-permute-start.11 = (bf16[3,48,1024]{2,1,0:T(8,128)(2,1)}, bf16[3,48,1024]{2,1,0:T(8,128)(2,1)}, u32[]{:S(2)}, u32[]{:S(2)}) collective-permute-start(bf16[3,48,1024]{2,1,0:T(8,128)(2,1)} %get-tuple-element.76), channel_id=1, source_target_pairs={{0,4},{1,5},{2,6},{3,7},{4,0},{5,1},{6,2},{7,3},{8,12},{9,13},{10,... | collective-permute-start | bytes 884744 | tf_op jit(solution)/shard_map/ppermute | solution.py:212
  181.9 1.9 collective-permute-start.12
  183.9 23.8 %all-to-all-done.2.back_ref = bf16[32,32,1024]{2,1,0:T(8,128)(2,1)S(1)} async-done(((bf16[32,32,1024]{2,1,0:T(8,128)(2,1)}), bf16[32,32,1024]{2,1,0:T(8,128)(2,1)S(1)}, u32[]{:S(2)}, u32[]{:S(2)}) %all-to-all-start.2) | async-done | bytes 2097184 | tf_op jit(solution)/shard_map/all_to_all | solution.py:323
  207.7 6.1 %all-to-all-start.3 = ((bf16[32,32,1024]{2,1,0:T(8,128)(2,1)}), bf16[32,32,1024]{2,1,0:T(8,128)(2,1)}, u32[]{:S(2)}, u32[]{:S(2)}) async-start(bf16[32,32,1024]{2,1,0:T(8,128)(2,1)} %get-tuple-element.71), calls=%async_computation.3 | async-start | bytes 4194304 | tf_op jit(solution)/shard_map/all_to_all | solution.py:323
  213.8 0.2 copy.15
  214.0 0.0 collective-permute-done.11
  214.0 0.0 collective-permute-done.12
  214.1 0.7 copy-done.9
  214.8 0.6 share.1
  215.3 0.0 copy-start.3
  215.4 9.4 %collective-permute-start.13 = (bf16[256,1024]{1,0:T(8,128)(2,1)S(1)}, bf16[256,1024]{1,0:T(8,128)(2,1)S(1)}, u32[]{:S(2)}, u32[]{:S(2)}) collective-permute-start(bf16[256,1024]{1,0:T(8,128)(2,1)S(1)} %share.1), channel_id=1, source_target_pairs={{0,32},{8,40},{16,48},{24,56},{32,0},{40,8},{48,16},{56,24},{64,96... | collective-permute-start | bytes 1572872 | tf_op jit(solution)/shard_map/ppermute | solution.py:26
  224.8 1.2 copy.14
  226.0 3.0 %subtract_convert_fusion = (bf16[1,3,48,1024]{3,2,1,0:T(8,128)(2,1)}, f32[1,3,48,1024]{3,2,1,0:T(8,128)}, f32[1,3,48,1024]{3,2,1,0:T(8,128)}) fusion(bf16[1,3,48,1024]{3,2,1,0:T(8,128)(2,1)S(1)} %copy-done.1, bf16[3,48,1024]{2,1,0:T(8,128)(2,1)} %collective-permute-done.12, bf16[3,48,1024]{2,1,0:T(8,128)(2,1)} %collective-permute-done.11, ...), kind=kLoop, calls=%fused_computation.5 | loop fusion | flops 3686400 | bytes 4718593 | tf_op jit(solution)/shard_map/convert_element_type | solution.py:306
  229.0 6.2 %collective-permute-done.13.share_ref = bf16[256,1024]{1,0:T(8,128)(2,1)S(1)} collective-permute-done((bf16[256,1024]{1,0:T(8,128)(2,1)S(1)}, bf16[256,1024]{1,0:T(8,128)(2,1)S(1)}, u32[]{:S(2)}, u32[]{:S(2)}) %collective-permute-start.13) | collective-permute-done | bytes 524320 | tf_op jit(solution)/shard_map/ppermute | solution.py:26
  235.1 27.8 %all-to-all-done.3.back_ref = bf16[32,32,1024]{2,1,0:T(8,128)(2,1)} async-done(((bf16[32,32,1024]{2,1,0:T(8,128)(2,1)}), bf16[32,32,1024]{2,1,0:T(8,128)(2,1)}, u32[]{:S(2)}, u32[]{:S(2)}) %all-to-all-start.3) | async-done | bytes 2097184 | tf_op jit(solution)/shard_map/all_to_all | solution.py:323
  262.9 2.9 %combine.1 = (bf16[128,1024]{1,0:T(8,128)(2,1)}, bf16[128,1024]{1,0:T(8,128)(2,1)}) custom-call(bf16[32,32,1024]{2,1,0:T(8,128)(2,1)} %all-to-all-done.3.back_ref, bf16[3,128,512]{2,1,0:T(8,128)(2,1)S(1)} %bitcast.20, bf16[256,1024]{1,0:T(8,128)(2,1)S(1)} %collective-permute-done.13.share_ref), custom_call_target="tpu_custom_call" | custom-call | flops 10000000000 | tf_op jit(solution)/shard_map/combine/pallas_call | solution.py:289
  (36 shorter events, 0.1 us)
Async XLA Ops:
  0.6 20.3 %collective-permute-start = (bf16[1,3,48,1024]{3,2,1,0:T(8,128)(2,1)}, bf16[1,3,48,1024]{3,2,1,0:T(8,128)(2,1)}, u32[]{:S(2)}, u32[]{:S(2)}) collective-permute-start(bf16[1,3,48,1024]{3,2,1,0:T(8,128)(2,1)} %param.15), channel_id=1, source_target_pairs={{0,256},{8,264},{16,272},{24,280},{32,288},{40,296},{48,304},{56,3... | collective-permute-start | bytes 884744 | tf_op jit(solution)/shard_map/ppermute | solution.py:26
  10.2 9.3 %copy-start.16 = (s32[128,8]{0,1:T(8,128)S(1)}, s32[128,8]{0,1:T(8,128)}, u32[]{:S(2)}) copy-start(s32[128,8]{0,1:T(8,128)} %param.11) | copy-start | bytes 12292
  10.2 9.3 %copy-start.20 = (s32[32]{0:T(128)S(1)}, s32[32]{0:T(128)}, u32[]{:S(2)}) copy-start(s32[32]{0:T(128)} %param.14) | copy-start | bytes 388
  10.2 10.6 %copy-start.17 = (f32[128,8]{0,1:T(8,128)S(1)}, f32[128,8]{0,1:T(8,128)}, u32[]{:S(2)}) copy-start(f32[128,8]{0,1:T(8,128)} %param.10) | copy-start | bytes 12292
  10.2 10.6 %copy-start.14 = (bf16[128,1024]{1,0:T(8,128)(2,1)S(1)}, bf16[128,1024]{1,0:T(8,128)(2,1)}, u32[]{:S(2)}) copy-start(bf16[128,1024]{1,0:T(8,128)(2,1)} %tokens_ref.1) | copy-start | bytes 786436
  10.2 10.6 %copy-start.15 = (bf16[128,1024]{1,0:T(8,128)(2,1)S(1)}, bf16[128,1024]{1,0:T(8,128)(2,1)}, u32[]{:S(2)}) copy-start(bf16[128,1024]{1,0:T(8,128)(2,1)} %cotangent_ref.1) | copy-start | bytes 786436
  10.2 61.2 %all-to-all-start = ((bf16[32,32,1024]{2,1,0:T(8,128)(2,1)}), bf16[32,32,1024]{2,1,0:T(8,128)(2,1)S(1)}, u32[]{:S(2)}, u32[]{:S(2)}) async-start(bf16[32,32,1024]{2,1,0:T(8,128)(2,1)} %get-tuple-element.46), calls=%async_computation | async-start | bytes 4194304 | tf_op jit(solution)/shard_map/all_to_all | solution.py:323
  19.4 1.5 copy-start.12
  19.4 17.0 %copy-start.2 = (f32[1,3,48,1024]{3,2,1,0:T(8,128)S(1)}, f32[1,3,48,1024]{3,2,1,0:T(8,128)}, u32[]{:S(2)}) copy-start(f32[1,3,48,1024]{3,2,1,0:T(8,128)} %param.16) | copy-start | bytes 1769476
  20.8 16.4 %copy-start.4 = (f32[1,3,48,1024]{3,2,1,0:T(8,128)S(1)}, f32[1,3,48,1024]{3,2,1,0:T(8,128)}, u32[]{:S(2)}) copy-start(f32[1,3,48,1024]{3,2,1,0:T(8,128)} %param.17) | copy-start | bytes 1769476
  21.9 69.1 %copy-start = (bf16[1,3,48,1024]{3,2,1,0:T(8,128)(2,1)}, bf16[1,3,48,1024]{3,2,1,0:T(8,128)(2,1)S(1)}, u32[]{:S(2)}) copy-start(bf16[1,3,48,1024]{3,2,1,0:T(8,128)(2,1)S(1)} %broadcast_select_fusion) | copy-start | bytes 884740
  21.9 24.9 %collective-permute-start.2 = (bf16[256,1024]{1,0:T(8,128)(2,1)S(1)}, bf16[256,1024]{1,0:T(8,128)(2,1)S(1)}, u32[]{:S(2)}, u32[]{:S(2)}) collective-permute-start(bf16[256,1024]{1,0:T(8,128)(2,1)S(1)} %pad_maximum_fusion.1), channel_id=1, source_target_pairs={{0,32},{8,40},{16,48},{24,56},{32,0},{40,8},{48,16},{56,24},{64,96... | collective-permute-start | bytes 1572872 | tf_op jit(solution)/shard_map/ppermute | solution.py:26
  34.5 11.8 %collective-permute-start.1 = (f32[16,128]{1,0:T(8,128)S(1)}, f32[16,128]{1,0:T(8,128)S(1)}, u32[]{:S(2)}, u32[]{:S(2)}) collective-permute-start(f32[16,128]{1,0:T(8,128)S(1)} %pad_maximum_fusion.2), channel_id=1, source_target_pairs={{0,32},{8,40},{16,48},{24,56},{32,0},{40,8},{48,16},{56,24},{64,96... | collective-permute-start | bytes 24584 | tf_op jit(solution)/shard_map/ppermute | solution.py:26
  51.2 33.0 %collective-permute-start.6 = (bf16[3,48,1024]{2,1,0:T(8,128)(2,1)S(1)}, bf16[3,48,1024]{2,1,0:T(8,128)(2,1)S(1)}, u32[]{:S(2)}, u32[]{:S(2)}) collective-permute-start(bf16[3,48,1024]{2,1,0:T(8,128)(2,1)S(1)} %bitcast.22), channel_id=1, source_target_pairs={{0,6},{1,7},{2,4},{3,5},{4,2},{5,3},{6,0},{7,1},{8,14},{9,15},{10,... | collective-permute-start | bytes 884744 | tf_op jit(solution)/shard_map/ppermute | solution.py:212
  62.4 24.7 %collective-permute-start.5 = (bf16[3,48,1024]{2,1,0:T(8,128)(2,1)S(1)}, bf16[3,48,1024]{2,1,0:T(8,128)(2,1)S(1)}, u32[]{:S(2)}, u32[]{:S(2)}) collective-permute-start(bf16[3,48,1024]{2,1,0:T(8,128)(2,1)S(1)} %bitcast.23), channel_id=1, source_target_pairs={{0,4},{1,5},{2,6},{3,7},{4,0},{5,1},{6,2},{7,3},{8,12},{9,13},{10,... | collective-permute-start | bytes 884744 | tf_op jit(solution)/shard_map/ppermute | solution.py:212
  69.5 17.6 %collective-permute-start.4 = (bf16[3,48,1024]{2,1,0:T(8,128)(2,1)S(1)}, bf16[3,48,1024]{2,1,0:T(8,128)(2,1)}, u32[]{:S(2)}, u32[]{:S(2)}) collective-permute-start(bf16[3,48,1024]{2,1,0:T(8,128)(2,1)S(1)} %bitcast.24), channel_id=1, source_target_pairs={{0,2},{1,3},{2,0},{3,1},{4,6},{5,7},{6,4},{7,5},{8,10},{9,11},{10,... | collective-permute-start | bytes 884744 | tf_op jit(solution)/shard_map/ppermute | solution.py:212
  71.4 4.8 %copy-start.5 = (bf16[32,32,1024]{2,1,0:T(8,128)(2,1)}, bf16[32,32,1024]{2,1,0:T(8,128)(2,1)S(1)}, u32[]{:S(2)}) copy-start(bf16[32,32,1024]{2,1,0:T(8,128)(2,1)S(1)} %all-to-all-done.arrived_ref.one_ref) | copy-start | bytes 6291460
  71.4 19.6 %collective-permute-start.3 = (bf16[1,3,48,1024]{3,2,1,0:T(8,128)(2,1)}, bf16[1,3,48,1024]{3,2,1,0:T(8,128)(2,1)S(1)}, u32[]{:S(2)}, u32[]{:S(2)}) collective-permute-start(bf16[1,3,48,1024]{3,2,1,0:T(8,128)(2,1)} %convert_element_type.34), channel_id=1, source_target_pairs={{0,256},{8,264},{16,272},{24,280},{32,288},{40,296},{48,304},{56,3... | collective-permute-start | bytes 884744 | tf_op jit(solution)/shard_map/ppermute | solution.py:26
  76.3 59.0 %all-to-all-start.1 = ((bf16[32,32,1024]{2,1,0:T(8,128)(2,1)}), bf16[32,32,1024]{2,1,0:T(8,128)(2,1)}, u32[]{:S(2)}, u32[]{:S(2)}) async-start(bf16[32,32,1024]{2,1,0:T(8,128)(2,1)} %get-tuple-element.50), calls=%async_computation.1 | async-start | bytes 4194304 | tf_op jit(solution)/shard_map/all_to_all | solution.py:323
  84.2 8.1 %copy-start.10 = (bf16[3,48,1024]{2,1,0:T(8,128)(2,1)}, bf16[3,48,1024]{2,1,0:T(8,128)(2,1)S(1)}, u32[]{:S(2)}) copy-start(bf16[3,48,1024]{2,1,0:T(8,128)(2,1)S(1)} %collective-permute-done.6.refs_3_) | copy-start | bytes 884740
  87.1 5.2 %copy-start.11 = (bf16[3,48,1024]{2,1,0:T(8,128)(2,1)}, bf16[3,48,1024]{2,1,0:T(8,128)(2,1)S(1)}, u32[]{:S(2)}) copy-start(bf16[3,48,1024]{2,1,0:T(8,128)(2,1)S(1)} %collective-permute-done.5.refs_2_) | copy-start | bytes 884740
  91.1 1.2 copy-start.7
  92.3 4.7 %collective-permute-start.7 = (bf16[4,3,48,1024]{3,2,1,0:T(8,128)(2,1)S(1)}, bf16[4,3,48,1024]{3,2,1,0:T(8,128)(2,1)S(1)}, u32[]{:S(2)}, u32[]{:S(2)}) collective-permute-start(bf16[4,3,48,1024]{3,2,1,0:T(8,128)(2,1)S(1)} %pad_maximum_fusion), channel_id=1, source_target_pairs={{0,1},{1,0},{2,3},{3,2},{4,5},{5,4},{6,7},{7,6},{8,9},{9,8},{10,11... | collective-permute-start | bytes 3538952 | tf_op jit(solution)/shard_map/ppermute | solution.py:212
  97.1 1.0 copy-start.19
  101.3 34.0 %copy-start.13 = (bf16[1,3,48,1024]{3,2,1,0:T(8,128)(2,1)S(1)}, bf16[1,3,48,1024]{3,2,1,0:T(8,128)(2,1)}, u32[]{:S(2)}) copy-start(bf16[1,3,48,1024]{3,2,1,0:T(8,128)(2,1)} %convert_element_type.35) | copy-start | bytes 884740
  135.2 22.5 %collective-permute-start.8 = (bf16[1,3,48,1024]{3,2,1,0:T(8,128)(2,1)S(1)}, bf16[1,3,48,1024]{3,2,1,0:T(8,128)(2,1)S(1)}, u32[]{:S(2)}, u32[]{:S(2)}) collective-permute-start(bf16[1,3,48,1024]{3,2,1,0:T(8,128)(2,1)S(1)} %copy-done.13), channel_id=1, source_target_pairs={{0,256},{8,264},{16,272},{24,280},{32,288},{40,296},{48,304},{56,3... | collective-permute-start | bytes 884744 | tf_op jit(solution)/shard_map/ppermute | solution.py:26
  149.5 58.1 %all-to-all-start.2 = ((bf16[32,32,1024]{2,1,0:T(8,128)(2,1)}), bf16[32,32,1024]{2,1,0:T(8,128)(2,1)S(1)}, u32[]{:S(2)}, u32[]{:S(2)}) async-start(bf16[32,32,1024]{2,1,0:T(8,128)(2,1)} %get-tuple-element.63), calls=%async_computation.2 | async-start | bytes 4194304 | tf_op jit(solution)/shard_map/all_to_all | solution.py:323
  157.7 7.0 %copy-start.8 = (bf16[1,3,48,1024]{3,2,1,0:T(8,128)(2,1)}, bf16[1,3,48,1024]{3,2,1,0:T(8,128)(2,1)S(1)}, u32[]{:S(2)}) copy-start(bf16[1,3,48,1024]{3,2,1,0:T(8,128)(2,1)S(1)} %collective-permute-done.8) | copy-start | bytes 884740
  164.7 4.9 %collective-permute-start.9 = (bf16[3,192,1024]{2,1,0:T(8,128)(2,1)}, bf16[3,192,1024]{2,1,0:T(8,128)(2,1)S(1)}, u32[]{:S(2)}, u32[]{:S(2)}) collective-permute-start(bf16[3,192,1024]{2,1,0:T(8,128)(2,1)} %get-tuple-element.69), channel_id=1, source_target_pairs={{0,1},{1,0},{2,3},{3,2},{4,5},{5,4},{6,7},{7,6},{8,9},{9,8},{10,11... | collective-permute-start | bytes 3538952 | tf_op jit(solution)/shard_map/ppermute | solution.py:212
  169.7 1.0 copy-start.18
  173.5 40.6 %collective-permute-start.10 = (bf16[3,48,1024]{2,1,0:T(8,128)(2,1)}, bf16[3,48,1024]{2,1,0:T(8,128)(2,1)S(1)}, u32[]{:S(2)}, u32[]{:S(2)}) collective-permute-start(bf16[3,48,1024]{2,1,0:T(8,128)(2,1)} %get-tuple-element.75), channel_id=1, source_target_pairs={{0,2},{1,3},{2,0},{3,1},{4,6},{5,7},{6,4},{7,5},{8,10},{9,11},{10,... | collective-permute-start | bytes 884744 | tf_op jit(solution)/shard_map/ppermute | solution.py:212
  176.2 37.8 %collective-permute-start.11 = (bf16[3,48,1024]{2,1,0:T(8,128)(2,1)}, bf16[3,48,1024]{2,1,0:T(8,128)(2,1)}, u32[]{:S(2)}, u32[]{:S(2)}) collective-permute-start(bf16[3,48,1024]{2,1,0:T(8,128)(2,1)} %get-tuple-element.76), channel_id=1, source_target_pairs={{0,4},{1,5},{2,6},{3,7},{4,0},{5,1},{6,2},{7,3},{8,12},{9,13},{10,... | collective-permute-start | bytes 884744 | tf_op jit(solution)/shard_map/ppermute | solution.py:212
  181.9 32.1 %collective-permute-start.12 = (bf16[3,48,1024]{2,1,0:T(8,128)(2,1)}, bf16[3,48,1024]{2,1,0:T(8,128)(2,1)}, u32[]{:S(2)}, u32[]{:S(2)}) collective-permute-start(bf16[3,48,1024]{2,1,0:T(8,128)(2,1)} %get-tuple-element.77), channel_id=1, source_target_pairs={{0,6},{1,7},{2,4},{3,5},{4,2},{5,3},{6,0},{7,1},{8,14},{9,15},{10,... | collective-permute-start | bytes 884744 | tf_op jit(solution)/shard_map/ppermute | solution.py:212
  207.7 6.1 %copy-start.6 = (bf16[3,512,128]{2,1,0:T(8,128)(2,1)S(1)}, bf16[3,512,128]{2,1,0:T(8,128)(2,1)}, u32[]{:S(2)}) copy-start(bf16[3,512,128]{2,1,0:T(8,128)(2,1)} %get-tuple-element.74) | copy-start | bytes 1179652
  207.7 55.2 %all-to-all-start.3 = ((bf16[32,32,1024]{2,1,0:T(8,128)(2,1)}), bf16[32,32,1024]{2,1,0:T(8,128)(2,1)}, u32[]{:S(2)}, u32[]{:S(2)}) async-start(bf16[32,32,1024]{2,1,0:T(8,128)(2,1)} %get-tuple-element.71), calls=%async_computation.3 | async-start | bytes 4194304 | tf_op jit(solution)/shard_map/all_to_all | solution.py:323
  214.0 0.7 copy-start.9
  214.8 11.2 %copy-start.1 = (bf16[1,3,48,1024]{3,2,1,0:T(8,128)(2,1)S(1)}, bf16[1,3,48,1024]{3,2,1,0:T(8,128)(2,1)}, u32[]{:S(2)}) copy-start(bf16[1,3,48,1024]{3,2,1,0:T(8,128)(2,1)} %copy-done) | copy-start | bytes 884740
  215.3 10.6 %copy-start.3 = (f32[1,3,48,1024]{3,2,1,0:T(8,128)S(1)}, f32[1,3,48,1024]{3,2,1,0:T(8,128)}, u32[]{:S(2)}) copy-start(f32[1,3,48,1024]{3,2,1,0:T(8,128)} %param.16) | copy-start | bytes 1769476
  215.4 19.8 %collective-permute-start.13 = (bf16[256,1024]{1,0:T(8,128)(2,1)S(1)}, bf16[256,1024]{1,0:T(8,128)(2,1)S(1)}, u32[]{:S(2)}, u32[]{:S(2)}) collective-permute-start(bf16[256,1024]{1,0:T(8,128)(2,1)S(1)} %share.1), channel_id=1, source_target_pairs={{0,32},{8,40},{16,48},{24,56},{32,0},{40,8},{48,16},{56,24},{64,96... | collective-permute-start | bytes 1572872 | tf_op jit(solution)/shard_map/ppermute | solution.py:26
